TPU v7x, 32 devices: a whole 2x2x4 slice. The times are simulated.
32 devices in a mesh: grp: 2 (over x), loc: 16 (over z, y, core).
Axes of the slice: x: 2, y: 2, z: 4, core: 2. Of those that a mesh axis runs over, the one named last changes fastest.
Arguments:
- latents: bfloat16 [16384, 2048], P(('grp', 'loc')), parts along dimension 0, may hold values from -6 to 6
- obs_inst: int32 [16384, 1], P(('grp', 'loc')), parts along dimension 0, may hold values from 0 to 15; in each aligned block of 512 rows (0 to 511, 512 to 1023, ...) at most 64 rows name the same one
- owner_slot: int32 [16], replicated, may hold values from 0 to 15, each once
- head_weights: bfloat16 [16, 2048, 512], P('loc'), may hold values from -0.125 to 0.125
- error_weight: float32 [16, 512], P('loc'), may hold values from 0.25 to 4
- block_pattern: int32 [16, 16, 4], P('loc'), may hold values 0 or 1
- targets: bfloat16 [16384, 512], P(('grp', 'loc')), parts along dimension 0, may hold values from -6 to 6
Outputs:
- latent_grad: bfloat16 [16384, 2048], P(('grp', 'loc')), parts along dimension 0
- head_grad: float32 [32, 2048, 512], P(('grp', 'loc')), parts along dimension 0
There are 2 independent parts, one for each index of `grp`. A program takes and returns all parts, laid end to end along the dimension named above; an argument that names none is the same for every part. Nothing has to cross between parts.
Inputs may be any that keep to these rules, and one draw needn't show every extreme that they name: `obs_inst`: in each aligned block of 512 rows (the rows of one device) no instrument is named by more than 64 rows; some instrument is named by exactly 64 rows in some blocks. `owner_slot`: each row number appears once.
All inputs are finite; a program needn't handle non-finite values. No bound on the sum of `block_pattern` on one device may be relied on, other than what follows from the above.
Results may differ from a plain program's by a relative error of at most 0.0048.
Values may be sent and summed in bfloat16 or wider, within the bound.
No kernel may reach another device: no remote copies, remote signals or barrier semaphores. Data moves between devices by JAX's collectives and lax.ppermute only.
A program may use at most 64 MiB of HBM per device.

v0:
```python
import math

import jax
import jax.numpy as jnp
from jax import lax
from jax.sharding import PartitionSpec as P

BLK = 128


def forward_heads(arrived, effective):
    return jnp.einsum("sicd,idh->sich", arrived, effective, preferred_element_type=jnp.float32)


def per_device(latents, obs_inst, owner_slot, head_weights, error_weight, block_pattern, targets):
    members = lax.axis_size("loc")
    local_heads, width, channels = head_weights.shape
    instruments = local_heads * members
    rows_dev = latents.shape[0]
    capacity = 2 * rows_dev // instruments
    numbers = jnp.arange(instruments, dtype=jnp.int32)
    inst_hit = obs_inst == numbers[None, :]
    slot_of = jnp.sum(jnp.where(inst_hit, owner_slot[None, :], 0), 1)
    slot_hit = (slot_of[:, None] == numbers[None, :]).astype(jnp.int32)
    rank_in = jnp.sum((jnp.cumsum(slot_hit, 0) - 1) * slot_hit, 1)
    placed = slot_of * capacity + rank_in
    send_rows = jnp.zeros((instruments * capacity, width), latents.dtype).at[placed].set(latents)
    send_targets = (
        jnp.zeros((instruments * capacity, channels), targets.dtype).at[placed].set(targets)
    )
    block_mask = jnp.repeat(jnp.repeat(block_pattern, BLK, 1), BLK, 2)
    effective = head_weights * block_mask.astype(head_weights.dtype)
    layout = (members, local_heads, capacity, width)
    got_rows = lax.all_to_all(send_rows, "loc", split_axis=0, concat_axis=0, tiled=True)
    arrived = got_rows.reshape(layout)
    predicted = forward_heads(arrived, effective)
    returned_pred = lax.all_to_all(
        predicted.reshape(-1, channels), "loc", split_axis=0, concat_axis=0, tiled=True
    )
    local_misfit = returned_pred - send_targets.astype(jnp.float32)
    misfit = lax.all_to_all(local_misfit, "loc", split_axis=0, concat_axis=0, tiled=True).reshape(
        members, local_heads, capacity, channels
    )
    residual = (error_weight[None, :, None, :] * misfit).astype(jnp.bfloat16)
    raw_grad = jnp.einsum(
        "sicd,sich->idh", arrived, residual, preferred_element_type=jnp.float32
    ) * block_mask.astype(jnp.float32)
    squares = lax.psum(jnp.sum(raw_grad * raw_grad), "loc")
    factor = jnp.minimum(1.0, math.sqrt(instruments * width * channels) / jnp.sqrt(squares + 1e-06))
    head_grad = raw_grad * factor
    row_grad = jnp.einsum(
        "sich,idh->sicd", residual, effective, preferred_element_type=jnp.float32
    ).astype(jnp.bfloat16)
    returned = lax.all_to_all(
        row_grad.reshape(-1, width), "loc", split_axis=0, concat_axis=0, tiled=True
    )
    latent_grad = returned[placed]
    return (latent_grad, head_grad)


def solution(mesh):
    in_specs = (
        P(("grp", "loc"), None),
        P(("grp", "loc"), None),
        P(),
        P("loc", None, None),
        P("loc", None),
        P("loc", None, None),
        P(("grp", "loc"), None),
    )
    out_specs = (P(("grp", "loc"), None), P(("grp", "loc"), None, None))
    return jax.shard_map(
        per_device, mesh=mesh, in_specs=in_specs, out_specs=out_specs, check_vma=False
    )
```

profile of v0, /device:TPU:1, one launch (start us, length us, event | category | flops | bytes accessed | tf_op | source)
XLA Modules:
  0.0 349.8 jit_solution(17132440116027835459)
XLA Ops:
  0.6 0.8 select_reduce_fusion
  1.4 1.1 reduce-window.6
  2.6 0.2 slice_reduce_fusion
  2.8 0.1 fusion.13
  3.0 7.3 %scatter_custom_fusion = bf16[1024,2048]{1,0:T(8,128)(2,1)} fusion(s32[512]{0:T(512)S(1)} %bitcast.66, bf16[512,2048]{1,0:T(8,128)(2,1)} %param.7, bf16[]{:T(256)} %constant.9.clone.1), kind=kCustom, calls=%fused_computation.12 | custom fusion | bytes 4194816 | tf_op jit(solution)/shard_map/scatter | solution.py:27
  10.3 7.5 %all-to-all-start = ((bf16[16,64,2048]{2,1,0:T(8,128)(2,1)}), bf16[16,64,2048]{2,1,0:T(8,128)(2,1)}, u32[]{:S(2)}, u32[]{:S(2)}) async-start(bf16[16,64,2048]{2,1,0:T(8,128)(2,1)} %bitcast.60), calls=%async_computation | async-start | bytes 8388608 | tf_op jit(solution)/shard_map/all_to_all | solution.py:34
  17.7 0.0 copy-done.1
  17.8 0.1 copy.11
  17.9 0.1 broadcast_in_dim.36
  17.9 5.8 %broadcast_in_dim.37 = bf16[2048,4,128]{2,1,0:T(4,128)(2,1)S(1)} broadcast(bf16[2048,4]{1,0:T(8,128)(2,1)S(1)} %bitcast.64), dimensions={0,1} | broadcast | bytes 2113536 | tf_op jit(solution)/shard_map/broadcast_in_dim | solution.py:31
  23.7 2.2 convert_element_type.66
  25.9 69.9 %all-to-all-done = bf16[16,64,2048]{2,1,0:T(8,128)(2,1)} async-done(((bf16[16,64,2048]{2,1,0:T(8,128)(2,1)}), bf16[16,64,2048]{2,1,0:T(8,128)(2,1)}, u32[]{:S(2)}, u32[]{:S(2)}) %all-to-all-start) | async-done | bytes 4194336 | tf_op jit(solution)/shard_map/all_to_all | solution.py:34
  95.8 7.1 %fusion.5 = f32[16,64,512]{2,1,0:T(8,128)} fusion(bf16[16,64,2048]{2,1,0:T(8,128)(2,1)} %all-to-all-done, bf16[1,2048,512]{2,1,0:T(8,128)(2,1)} %param.10, bf16[1,2048,512]{2,1,0:T(8,128)(2,1)} %convert_element_type.66), kind=kOutput, calls=%fused_computation.14 | convolution fusion | flops 2151677952 | bytes 10485760 | tf_op jit(solution)/shard_map/sicd,idh->sich/dot_general | solution.py:12
  103.0 19.3 %all-to-all-start.1 = ((f32[16,64,512]{2,1,0:T(8,128)}), f32[16,64,512]{2,1,0:T(8,128)S(1)}, u32[]{:S(2)}, u32[]{:S(2)}) async-start(f32[16,64,512]{2,1,0:T(8,128)} %fusion.5), calls=%async_computation.1 | async-start | bytes 4194304 | tf_op jit(solution)/shard_map/all_to_all | solution.py:37
  122.2 3.2 scatter_custom_fusion.1
  125.5 38.2 %all-to-all-done.1 = f32[16,64,512]{2,1,0:T(8,128)S(1)} async-done(((f32[16,64,512]{2,1,0:T(8,128)}), f32[16,64,512]{2,1,0:T(8,128)S(1)}, u32[]{:S(2)}, u32[]{:S(2)}) %all-to-all-start.1) | async-done | bytes 2097184 | tf_op jit(solution)/shard_map/all_to_all | solution.py:37
  163.7 0.3 bitcast_subtract_fusion
  164.0 0.0 copy-start
  164.0 0.0 copy-start.2
  164.1 58.6 %all_to_all.42 = f32[16,64,512]{2,1,0:T(8,128)S(1)} all-to-all(f32[16,64,512]{2,1,0:T(8,128)S(1)} %bitcast.61), channel_id=1, replica_groups=mesh['grp'=2,'loc'=16] {'loc'}, dimensions={0} | all-to-all | bytes 4194304 | tf_op jit(solution)/shard_map/all_to_all | solution.py:41
  222.7 0.0 copy-done.3
  222.7 0.0 copy-done
  222.7 4.4 %convert_bitcast_fusion = bf16[16,64,2048]{2,1,0:T(8,128)(2,1)} fusion(bf16[1,2048,512]{2,1,0:T(8,128)(2,1)S(1)} %copy-done.2, bf16[1,2048,512]{2,1,0:T(8,128)(2,1)S(1)} %copy-done, f32[16,64,512]{2,1,0:T(8,128)S(1)} %all_to_all.42, f32[512]{0:T(512)S(1)} %bitcast.71), kind=kOutput, calls=%fused_computation.6 | convolution fusion | flops 2154823680 | bytes 10487808 | tf_op jit(solution)/shard_map/sich,idh->sicd/dot_general | solution.py:51
  227.1 4.8 %all-to-all-start.3 = ((bf16[16,64,2048]{2,1,0:T(8,128)(2,1)}), bf16[16,64,2048]{2,1,0:T(8,128)(2,1)}, u32[]{:S(2)}, u32[]{:S(2)}) async-start(bf16[16,64,2048]{2,1,0:T(8,128)(2,1)} %convert_bitcast_fusion), calls=%async_computation.3 | async-start | bytes 8388608 | tf_op jit(solution)/shard_map/all_to_all | solution.py:54
  231.8 0.1 copy.13
  231.9 0.1 broadcast_in_dim.42
  232.0 4.7 %broadcast_in_dim.43 = f32[2048,4,128]{2,1,0:T(4,128)S(1)} broadcast(f32[2048,4]{1,0:T(8,128)S(1)} %bitcast.63), dimensions={0,1} | broadcast | bytes 4227072 | tf_op jit(solution)/shard_map/broadcast_in_dim | solution.py:31
  236.7 7.2 %multiply_reduce_fusion = (f32[]{:T(128)}, f32[2048,512]{1,0:T(8,128)}) fusion(f32[256,8,4,128]{3,2,1,0:T(4,128)S(1)} %bitcast.62, bf16[16,64,2048]{2,1,0:T(8,128)(2,1)} %all-to-all-done, f32[16,64,512]{2,1,0:T(8,128)S(1)} %all_to_all.42, f32[512]{0:T(512)S(1)} %bitcast.72), kind=kOutput, calls=%fused_computation.5 | convolution fusion | flops 2151677952 | bytes 14682116 | tf_op jit(solution)/shard_map/sicd,sich->idh/dot_general | solution.py:45
  243.9 92.6 %psum.7 = f32[]{:T(128)} all-reduce(f32[]{:T(128)} %get-tuple-element.4), channel_id=1, replica_groups=mesh['grp'=2,'loc'=16] {'loc'}, use_global_device_ids=true, to_apply=%region_7.8 | all-reduce | flops 1 | bytes 8 | tf_op jit(solution)/shard_map/psum | solution.py:48
  337.2 4.7 %multiply_bitcast_fusion = f32[1,2048,512]{2,1,0:T(8,128)} fusion(f32[2048,512]{1,0:T(8,128)} %get-tuple-element.5, f32[]{:T(128)S(6)} %min_shard_map.3), kind=kLoop, calls=%fused_computation.4 | loop fusion | flops 1048576 | bytes 8388612 | tf_op jit(solution)/shard_map/mul | solution.py:50
  341.9 0.0 all-to-all-done.3
  341.9 8.0 %gather_fusion = bf16[512,2048]{1,0:T(8,128)(2,1)} fusion(bf16[1024,2048]{1,0:T(8,128)(2,1)} %bitcast.19, s32[1024]{0:T(1024)S(1)} %pad_clamp_fusion), kind=kCustom, calls=%fused_computation | custom fusion | bytes 4196352 | tf_op jit(solution)/shard_map/gather | solution.py:57
  (10 shorter events, 0.1 us)
Async XLA Ops:
  10.3 7.5 %copy-start.1 = (s32[1,16,4]{1,2,0:T(4,128)S(1)}, s32[1,16,4]{1,2,0:T(4,128)}, u32[]{:S(2)}) copy-start(s32[1,16,4]{1,2,0:T(4,128)} %param.12) | copy-start | bytes 772
  10.3 85.6 %all-to-all-start = ((bf16[16,64,2048]{2,1,0:T(8,128)(2,1)}), bf16[16,64,2048]{2,1,0:T(8,128)(2,1)}, u32[]{:S(2)}, u32[]{:S(2)}) async-start(bf16[16,64,2048]{2,1,0:T(8,128)(2,1)} %bitcast.60), calls=%async_computation | async-start | bytes 8388608 | tf_op jit(solution)/shard_map/all_to_all | solution.py:34
  103.0 60.8 %all-to-all-start.1 = ((f32[16,64,512]{2,1,0:T(8,128)}), f32[16,64,512]{2,1,0:T(8,128)S(1)}, u32[]{:S(2)}, u32[]{:S(2)}) async-start(f32[16,64,512]{2,1,0:T(8,128)} %fusion.5), calls=%async_computation.1 | async-start | bytes 4194304 | tf_op jit(solution)/shard_map/all_to_all | solution.py:37
  163.7 58.9 %copy-start.3 = (f32[1,512]{1,0:T(1,128)S(1)}, f32[1,512]{1,0:T(1,128)}, u32[]{:S(2)}) copy-start(f32[1,512]{1,0:T(1,128)} %param.11) | copy-start | bytes 6148
  164.0 58.6 %copy-start = (bf16[1,2048,512]{2,1,0:T(8,128)(2,1)S(1)}, bf16[1,2048,512]{2,1,0:T(8,128)(2,1)}, u32[]{:S(2)}) copy-start(bf16[1,2048,512]{2,1,0:T(8,128)(2,1)} %convert_element_type.66) | copy-start | bytes 6291460
  164.0 58.6 %copy-start.2 = (bf16[1,2048,512]{2,1,0:T(8,128)(2,1)S(1)}, bf16[1,2048,512]{2,1,0:T(8,128)(2,1)}, u32[]{:S(2)}) copy-start(bf16[1,2048,512]{2,1,0:T(8,128)(2,1)} %param.10) | copy-start | bytes 6291460
  227.1 114.8 %all-to-all-start.3 = ((bf16[16,64,2048]{2,1,0:T(8,128)(2,1)}), bf16[16,64,2048]{2,1,0:T(8,128)(2,1)}, u32[]{:S(2)}, u32[]{:S(2)}) async-start(bf16[16,64,2048]{2,1,0:T(8,128)(2,1)} %convert_bitcast_fusion), calls=%async_computation.3 | async-start | bytes 8388608 | tf_op jit(solution)/shard_map/all_to_all | solution.py:54
where the time goes:
time: 356 us; the launch traced here: 350 us
  blocking collectives  151 us (42%)
  waiting for transfers between devices  108 us (30%)
  local copies, waits for them, and re-layouts  31.7 us (9%)
  starting transfers between devices  31.5 us (9%)
  matrix products  18.7 us (5%)
  other arithmetic  7.11 us (2%)
    psum x1, blocking collectives, per_device(): squares = lax.psum(jnp.sum(raw_grad * raw_grad), 'loc')  92.6 us
    all_to_all x1, waiting for transfers between devices, per_device(): lax.all_to_all(send_rows, 'loc', split_axis=0, concat_axis=0, tiled=True)  69.9 us
    all_to_all x1, blocking collectives, per_device(): lax.all_to_all(local_misfit, 'loc', split_axis=0, concat_axis=0, tiled=True)  58.6 us
    all_to_all x1, waiting for transfers between devices, per_device(): lax.all_to_all(predicted.reshape(-1, channels), 'loc', split_axis=0, conc...  38.2 us
    all_to_all x1, starting transfers between devices, per_device(): lax.all_to_all(predicted.reshape(-1, channels), 'loc', split_axis=0, conc...  19.3 us
    broadcast_in_dim x4, local copies, waits for them, and re-layouts, per_device(): block_mask = jnp.repeat(jnp.repeat(block_pattern, BLK, 1), BLK, 2)  10.6 us
    gather x1, local copies, waits for them, and re-layouts, per_device(): latent_grad = returned[placed]  7.95 us
    all_to_all x1, starting transfers between devices, per_device(): lax.all_to_all(send_rows, 'loc', split_axis=0, concat_axis=0, tiled=True)  7.48 us
  transfers between devices with their start and end apart: 3, of which 2 were waited for; matrix products, arithmetic and copies ran while one was open for 8% of the time, Pallas kernels for 0%

commit v1 on v0

v1 whole, which is shorter than its diff:
```python
import math

import jax
import jax.numpy as jnp
from jax import lax
from jax.sharding import PartitionSpec as P

BLK = 128


def per_device(latents, obs_inst, owner_slot, head_weights, error_weight, block_pattern, targets):
    members = lax.axis_size("loc")
    local_heads, width, channels = head_weights.shape
    instruments = local_heads * members
    rows_dev = latents.shape[0]
    capacity = 2 * rows_dev // instruments
    numbers = jnp.arange(instruments, dtype=jnp.int32)
    inst_hit = obs_inst == numbers[None, :]
    slot_of = jnp.sum(jnp.where(inst_hit, owner_slot[None, :], 0), 1)
    slot_hit = (slot_of[:, None] == numbers[None, :]).astype(jnp.int32)
    rank_in = jnp.sum((jnp.cumsum(slot_hit, 0) - 1) * slot_hit, 1)
    placed = slot_of * capacity + rank_in
    send_rows = jnp.zeros((instruments * capacity, width), latents.dtype).at[placed].set(latents)
    send_targets = (
        jnp.zeros((instruments * capacity, channels), targets.dtype).at[placed].set(targets)
    )
    block_mask = jnp.repeat(jnp.repeat(block_pattern, BLK, 1), BLK, 2)
    effective = head_weights * block_mask.astype(head_weights.dtype)
    got = lax.all_to_all(
        jnp.concatenate([send_rows, send_targets], 1), "loc", split_axis=0, concat_axis=0, tiled=True
    )
    arrived = got[:, :width]
    predicted = jnp.dot(arrived, effective[0], preferred_element_type=jnp.float32)
    misfit = predicted - got[:, width:].astype(jnp.float32)
    residual = (error_weight * misfit).astype(jnp.bfloat16)
    row_grad = lax.dot_general(
        residual, effective[0], (((1,), (1,)), ((), ())), preferred_element_type=jnp.float32
    ).astype(jnp.bfloat16)
    returned = lax.all_to_all(row_grad, "loc", split_axis=0, concat_axis=0, tiled=True)
    raw_grad = lax.dot_general(
        arrived, residual, (((0,), (0,)), ((), ())), preferred_element_type=jnp.float32
    ) * block_mask[0].astype(jnp.float32)
    squares = jnp.broadcast_to(jnp.sum(raw_grad * raw_grad), (8, 128))
    step = 1
    while step < members:
        squares = squares + lax.ppermute(squares, "loc", [(i, i ^ step) for i in range(members)])
        step *= 2
    squares = squares[0, 0]
    factor = jnp.minimum(1.0, math.sqrt(instruments * width * channels) / jnp.sqrt(squares + 1e-06))
    head_grad = (raw_grad * factor)[None]
    latent_grad = returned[placed]
    return (latent_grad, head_grad)


def solution(mesh):
    in_specs = (
        P(("grp", "loc"), None),
        P(("grp", "loc"), None),
        P(),
        P("loc", None, None),
        P("loc", None),
        P("loc", None, None),
        P(("grp", "loc"), None),
    )
    out_specs = (P(("grp", "loc"), None), P(("grp", "loc"), None, None))
    return jax.shard_map(
        per_device, mesh=mesh, in_specs=in_specs, out_specs=out_specs, check_vma=False
    )
```

time: 356 us -> 263 us (0.74); the launches traced: 350 us -> 261 us
  blocking collectives: 151 us -> 0 us
  waiting for transfers between devices: 108 us -> 163 us
  starting transfers between devices: 31.5 us -> 36.9 us
  other arithmetic: 7.11 us -> 10.9 us
    psum x1 -> x0, blocking collectives: 92.6 us -> none  [per_device(): squares = lax.psum(jnp.sum(raw_grad * raw_grad), 'loc')]
    ppermute x0 -> x4, waiting for transfers between devices: none -> 74.7 us  [per_device(): lax.ppermute(squares, 'loc', [(i, i ^ step) for i in range(members)])]
    all_to_all x1 -> x0, blocking collectives: 58.6 us -> none  [per_device(): lax.all_to_all(local_misfit, 'loc', split_axis=0, concat_axis=0, tiled=True)]
    all_to_all x3 -> x2, waiting for transfers between devices: 108 us -> 88.1 us  [the longest x1 88.1 us: per_device(): lax.all_to_all(jnp.concatenate([send_rows, send_targets], 1), 'loc', spli...]
    ppermute x0 -> x4, starting transfers between devices: none -> 5.91 us  [per_device(): lax.ppermute(squares, 'loc', [(i, i ^ step) for i in range(members)])]
    concatenate x0 -> x1, other arithmetic: none -> 4.96 us  [per_device(): jnp.concatenate([send_rows, send_targets], 1)]
    mul x1 -> x0, other arithmetic: 4.7 us -> none  [per_device(): head_grad = raw_grad * factor]
    all_to_all x3 -> x2, starting transfers between devices: 31.5 us -> 31 us  [the longest x1 23.5 us: per_device(): lax.all_to_all(row_grad, 'loc', split_axis=0, concat_axis=0, tiled=True)]
  transfers between devices with their start and end apart: 3 -> 6, of which waited for: 2 -> 5; matrix products, arithmetic and copies ran while one was open for 8% -> 9% of each run, Pallas kernels for 0% -> 0%
where the time goes in v1:
time: 263 us; the launch traced here: 261 us
  waiting for transfers between devices  163 us (62%)
  starting transfers between devices  36.9 us (14%)
  local copies, waits for them, and re-layouts  32.9 us (13%)
  matrix products  16.4 us (6%)
  other arithmetic  10.9 us (4%)
    all_to_all x1, waiting for transfers between devices, per_device(): lax.all_to_all(jnp.concatenate([send_rows, send_targets], 1), 'loc', spli...  88.1 us
    ppermute x4, waiting for transfers between devices, per_device(): lax.ppermute(squares, 'loc', [(i, i ^ step) for i in range(members)])  74.7 us
    all_to_all x1, starting transfers between devices, per_device(): lax.all_to_all(row_grad, 'loc', split_axis=0, concat_axis=0, tiled=True)  23.5 us
    broadcast_in_dim x4, local copies, waits for them, and re-layouts, per_device(): block_mask = jnp.repeat(jnp.repeat(block_pattern, BLK, 1), BLK, 2)  10.6 us
    gather x1, local copies, waits for them, and re-layouts, per_device(): latent_grad = returned[placed]  7.95 us
    all_to_all x1, starting transfers between devices, per_device(): lax.all_to_all(jnp.concatenate([send_rows, send_targets], 1), 'loc', spli...  7.48 us
    scatter x1, local copies, waits for them, and re-layouts, per_device(): jnp.zeros((instruments * capacity, width), latents.dtype).at[placed]  7.3 us
    dot_general x1, matrix products, per_device(): jnp.dot(arrived, effective[0], preferred_element_type=jnp.float32)  6.15 us
  transfers between devices with their start and end apart: 6, of which 5 were waited for; matrix products, arithmetic and copies ran while one was open for 9% of the time, Pallas kernels for 0%

profile of v1, /device:TPU:1, one launch (start us, length us, event | category | flops | bytes accessed | tf_op | source)
XLA Modules:
  0.0 261.2 jit_solution(14181008365554875414)
XLA Ops:
  0.6 0.8 select_reduce_fusion
  1.4 1.1 reduce-window.6
  2.6 0.2 slice_reduce_fusion
  2.8 0.1 fusion.19
  3.0 3.2 %scatter_custom_fusion.1 = bf16[1024,512]{1,0:T(8,128)(2,1)S(1)} fusion(s32[512]{0:T(512)S(1)} %bitcast.51, bf16[512,512]{1,0:T(8,128)(2,1)} %param.13, bf16[]{:T(256)} %constant.9.clone.1), kind=kCustom, calls=%fused_computation.19 | custom fusion | bytes 1049088 | tf_op jit(solution)/shard_map/scatter | solution.py:25
  6.2 7.3 %scatter_custom_fusion = bf16[1024,2048]{1,0:T(8,128)(2,1)} fusion(s32[512]{0:T(512)S(1)} %bitcast.52, bf16[512,2048]{1,0:T(8,128)(2,1)} %param.7, bf16[]{:T(256)} %constant.9.clone.1), kind=kCustom, calls=%fused_computation.15 | custom fusion | bytes 4194816 | tf_op jit(solution)/shard_map/scatter | solution.py:23
  13.5 5.0 %pad_maximum_fusion = bf16[1024,2560]{1,0:T(8,128)(2,1)} fusion(bf16[1024,512]{1,0:T(8,128)(2,1)S(1)} %scatter_custom_fusion.1, bf16[1024,2048]{1,0:T(8,128)(2,1)} %scatter_custom_fusion), kind=kLoop, calls=%fused_computation.3 | loop fusion | flops 10485760 | bytes 10485760 | tf_op jit(solution)/shard_map/concatenate | solution.py:30
  18.4 7.5 %all-to-all-start = ((bf16[16,64,2560]{2,1,0:T(8,128)(2,1)}), bf16[16,64,2560]{2,1,0:T(8,128)(2,1)}, u32[]{:S(2)}, u32[]{:S(2)}) async-start(bf16[16,64,2560]{2,1,0:T(8,128)(2,1)} %bitcast.45), calls=%async_computation | async-start | bytes 10485760 | tf_op jit(solution)/shard_map/all_to_all | solution.py:29
  26.0 0.1 copy.12
  26.1 5.8 %broadcast_in_dim.46 = bf16[2048,4,128]{2,1,0:T(4,128)(2,1)S(1)} broadcast(bf16[2048,4]{1,0:T(8,128)(2,1)S(1)} %bitcast.49), dimensions={0,1} | broadcast | bytes 2113536 | tf_op jit(solution)/shard_map/broadcast_in_dim | solution.py:27
  31.9 2.2 convert_element_type.54
  34.1 88.1 %all-to-all-done = bf16[16,64,2560]{2,1,0:T(8,128)(2,1)} async-done(((bf16[16,64,2560]{2,1,0:T(8,128)(2,1)}), bf16[16,64,2560]{2,1,0:T(8,128)(2,1)}, u32[]{:S(2)}, u32[]{:S(2)}) %all-to-all-start) | async-done | bytes 5242912 | tf_op jit(solution)/shard_map/all_to_all | solution.py:29
  122.3 6.1 %multiply_convert_fusion = bf16[1024,512]{1,0:T(8,128)(2,1)S(1)} fusion(bf16[1024,2560]{1,0:T(8,128)(2,1)} %bitcast.7, f32[512]{0:T(512)S(1)} %bitcast.56, bf16[1,2048,512]{2,1,0:T(8,128)(2,1)} %param.10, bf16[1,2048,512]{2,1,0:T(8,128)(2,1)} %convert_element_type.54), kind=kOutput, calls=%fused_computation.14 | convolution fusion | flops 2150629376 | bytes 10487808 | tf_op jit(solution)/shard_map/dot_general | solution.py:33
  128.4 4.5 %convolution_convert_fusion = bf16[1024,2048]{1,0:T(8,128)(2,1)} fusion(bf16[1024,512]{1,0:T(8,128)(2,1)S(1)} %multiply_convert_fusion, bf16[1,2048,512]{2,1,0:T(8,128)(2,1)S(1)} %copy-done.2, bf16[1,2048,512]{2,1,0:T(8,128)(2,1)S(1)} %copy-done), kind=kOutput, calls=%fused_computation.7 | convolution fusion | flops 2150629376 | bytes 9437184 | tf_op jit(solution)/shard_map/dot_general | solution.py:36
  132.9 23.5 %all-to-all-start.1 = ((bf16[16,64,2048]{2,1,0:T(8,128)(2,1)}), bf16[16,64,2048]{2,1,0:T(8,128)(2,1)}, u32[]{:S(2)}, u32[]{:S(2)}) async-start(bf16[16,64,2048]{2,1,0:T(8,128)(2,1)} %bitcast.48), calls=%async_computation.1 | async-start | bytes 8388608 | tf_op jit(solution)/shard_map/all_to_all | solution.py:39
  156.4 0.1 copy.13
  156.6 4.7 %broadcast_in_dim.48 = f32[2048,4,128]{2,1,0:T(4,128)S(1)} broadcast(f32[2048,4]{1,0:T(8,128)S(1)} %bitcast.47), dimensions={0,1} | broadcast | bytes 4227072 | tf_op jit(solution)/shard_map/broadcast_in_dim | solution.py:27
  161.2 5.8 %multiply_reduce_fusion = (f32[]{:T(128)}, f32[2048,512]{1,0:T(8,128)S(1)}) fusion(f32[256,8,4,128]{3,2,1,0:T(4,128)S(1)} %bitcast.46, bf16[1024,512]{1,0:T(8,128)(2,1)S(1)} %multiply_convert_fusion, bf16[1024,2560]{1,0:T(8,128)(2,1)} %bitcast.7), kind=kOutput, calls=%fused_computation.6 | convolution fusion | flops 2150629376 | bytes 13631492 | tf_op jit(solution)/shard_map/dot_general | solution.py:40
  167.0 0.6 broadcast_in_dim.49
  167.7 0.2 collective-permute-start
  167.9 1.0 collective-permute-done
  168.9 0.6 broadcast_add_fusion
  169.5 1.5 collective-permute-start.1
  171.0 5.8 %collective-permute-done.1 = f32[8,128]{1,0:T(8,128)S(1)} collective-permute-done((f32[8,128]{1,0:T(8,128)S(1)}, f32[8,128]{1,0:T(8,128)S(1)}, u32[]{:S(2)}, u32[]{:S(2)}) %collective-permute-start.1) | collective-permute-done | bytes 4128 | tf_op jit(solution)/shard_map/ppermute | solution.py:46
  176.9 0.6 fusion.23
  177.5 0.2 collective-permute-start.2
  177.7 46.9 %collective-permute-done.2 = f32[8,128]{1,0:T(8,128)S(1)} collective-permute-done((f32[8,128]{1,0:T(8,128)S(1)}, f32[8,128]{1,0:T(8,128)S(1)}, u32[]{:S(2)}, u32[]{:S(2)}) %collective-permute-start.2) | collective-permute-done | bytes 4128 | tf_op jit(solution)/shard_map/ppermute | solution.py:46
  224.6 4.0 %collective-permute-start.3 = (f32[8,128]{1,0:T(8,128)S(1)}, f32[8,128]{1,0:T(8,128)S(1)}, u32[]{:S(2)}, u32[]{:S(2)}) collective-permute-start(f32[8,128]{1,0:T(8,128)S(1)} %add.49), channel_id=1, source_target_pairs={{0,8},{1,9},{2,10},{3,11},{4,12},{5,13},{6,14},{7,15},{8,0},{9,1},... | collective-permute-start | bytes 12296 | tf_op jit(solution)/shard_map/ppermute | solution.py:46
  228.6 20.9 %collective-permute-done.3 = f32[8,128]{1,0:T(8,128)S(1)} collective-permute-done((f32[8,128]{1,0:T(8,128)S(1)}, f32[8,128]{1,0:T(8,128)S(1)}, u32[]{:S(2)}, u32[]{:S(2)}) %collective-permute-start.3) | collective-permute-done | bytes 4128 | tf_op jit(solution)/shard_map/ppermute | solution.py:46
  249.6 0.5 slice.19
  250.8 2.5 multiply_bitcast_fusion
  253.3 8.0 %gather_fusion = bf16[512,2048]{1,0:T(8,128)(2,1)} fusion(bf16[1024,2048]{1,0:T(8,128)(2,1)} %bitcast.12, s32[1024]{0:T(1024)S(1)} %pad_clamp_fusion), kind=kCustom, calls=%fused_computation | custom fusion | bytes 4196352 | tf_op jit(solution)/shard_map/gather | solution.py:51
  (20 shorter events, 0.2 us)
Async XLA Ops:
  18.4 7.5 %copy-start.1 = (s32[1,16,4]{1,2,0:T(4,128)S(1)}, s32[1,16,4]{1,2,0:T(4,128)}, u32[]{:S(2)}) copy-start(s32[1,16,4]{1,2,0:T(4,128)} %param.12) | copy-start | bytes 772
  18.4 103.8 %all-to-all-start = ((bf16[16,64,2560]{2,1,0:T(8,128)(2,1)}), bf16[16,64,2560]{2,1,0:T(8,128)(2,1)}, u32[]{:S(2)}, u32[]{:S(2)}) async-start(bf16[16,64,2560]{2,1,0:T(8,128)(2,1)} %bitcast.45), calls=%async_computation | async-start | bytes 10485760 | tf_op jit(solution)/shard_map/all_to_all | solution.py:29
  25.9 96.3 %copy-start.3 = (f32[1,512]{1,0:T(1,128)S(1)}, f32[1,512]{1,0:T(1,128)}, u32[]{:S(2)}) copy-start(f32[1,512]{1,0:T(1,128)} %param.11) | copy-start | bytes 6148
  122.3 6.2 %copy-start = (bf16[1,2048,512]{2,1,0:T(8,128)(2,1)S(1)}, bf16[1,2048,512]{2,1,0:T(8,128)(2,1)}, u32[]{:S(2)}) copy-start(bf16[1,2048,512]{2,1,0:T(8,128)(2,1)} %convert_element_type.54) | copy-start | bytes 6291460
  122.3 6.2 %copy-start.2 = (bf16[1,2048,512]{2,1,0:T(8,128)(2,1)S(1)}, bf16[1,2048,512]{2,1,0:T(8,128)(2,1)}, u32[]{:S(2)}) copy-start(bf16[1,2048,512]{2,1,0:T(8,128)(2,1)} %param.10) | copy-start | bytes 6291460
  132.9 120.4 %all-to-all-start.1 = ((bf16[16,64,2048]{2,1,0:T(8,128)(2,1)}), bf16[16,64,2048]{2,1,0:T(8,128)(2,1)}, u32[]{:S(2)}, u32[]{:S(2)}) async-start(bf16[16,64,2048]{2,1,0:T(8,128)(2,1)} %bitcast.48), calls=%async_computation.1 | async-start | bytes 8388608 | tf_op jit(solution)/shard_map/all_to_all | solution.py:39
  167.7 1.2 collective-permute-start
  169.5 7.3 %collective-permute-start.1 = (f32[8,128]{1,0:T(8,128)S(1)}, f32[8,128]{1,0:T(8,128)S(1)}, u32[]{:S(2)}, u32[]{:S(2)}) collective-permute-start(f32[8,128]{1,0:T(8,128)S(1)} %broadcast_add_fusion), channel_id=1, source_target_pairs={{0,2},{1,3},{2,0},{3,1},{4,6},{5,7},{6,4},{7,5},{8,10},{9,11},{10,... | collective-permute-start | bytes 12296 | tf_op jit(solution)/shard_map/ppermute | solution.py:46
  177.5 47.1 %collective-permute-start.2 = (f32[8,128]{1,0:T(8,128)S(1)}, f32[8,128]{1,0:T(8,128)S(1)}, u32[]{:S(2)}, u32[]{:S(2)}) collective-permute-start(f32[8,128]{1,0:T(8,128)S(1)} %fusion.23), channel_id=1, source_target_pairs={{0,4},{1,5},{2,6},{3,7},{4,0},{5,1},{6,2},{7,3},{8,12},{9,13},{10,... | collective-permute-start | bytes 12296 | tf_op jit(solution)/shard_map/ppermute | solution.py:46
  224.6 24.9 %collective-permute-start.3 = (f32[8,128]{1,0:T(8,128)S(1)}, f32[8,128]{1,0:T(8,128)S(1)}, u32[]{:S(2)}, u32[]{:S(2)}) collective-permute-start(f32[8,128]{1,0:T(8,128)S(1)} %add.49), channel_id=1, source_target_pairs={{0,8},{1,9},{2,10},{3,11},{4,12},{5,13},{6,14},{7,15},{8,0},{9,1},... | collective-permute-start | bytes 12296 | tf_op jit(solution)/shard_map/ppermute | solution.py:46

commit v2 on v1

v2 whole, which is shorter than its diff:
```python
import functools
import math

import jax
import jax.numpy as jnp
from jax import lax
from jax.experimental import pallas as pl
from jax.experimental.pallas import tpu as pltpu
from jax.sharding import PartitionSpec as P

BLK = 128
F32 = jnp.float32
BF16 = jnp.bfloat16
VMEM = pl.BlockSpec(memory_space=pltpu.VMEM)
SMEM = pl.BlockSpec(memory_space=pltpu.SMEM)
PARAMS = pltpu.CompilerParams(vmem_limit_bytes=48 * 1024 * 1024)


def dot(a, b, ca=1, cb=0):
    return lax.dot_general(a, b, (((ca,), (cb,)), ((), ())), preferred_element_type=F32)


def cost(flops, nbytes):
    return pl.CostEstimate(flops=int(flops), bytes_accessed=int(nbytes), transcendentals=0)


def places(inst, owner_ref, heads):
    rows = inst.shape[1]
    slot = jnp.zeros_like(inst)
    for k in range(heads):
        slot = jnp.where(inst == k, owner_ref[k], slot)
    hit = lax.broadcasted_iota(jnp.int32, (heads, rows), 0) == slot
    upto = lax.broadcasted_iota(jnp.int32, (rows, rows), 0) <= lax.broadcasted_iota(
        jnp.int32, (rows, rows), 1
    )
    count = dot(hit.astype(BF16), upto.astype(BF16))
    rank = jnp.sum(jnp.where(hit, count, 0.0), 0, keepdims=True).astype(jnp.int32) - 1
    return slot, rank


def one_hot_rows(pos, start, size):
    number = lax.broadcasted_iota(jnp.int32, (size, pos.shape[1]), 0) + start
    return (number == pos).astype(F32).astype(BF16)


def one_hot_back(pos, size):
    column = jnp.transpose(jnp.broadcast_to(pos.astype(F32), (128, pos.shape[1])))[:, :1]
    number = lax.broadcasted_iota(jnp.int32, (pos.shape[1], size), 1)
    return (number == column.astype(jnp.int32)).astype(F32).astype(BF16)


def prep_kernel(heads, capacity, inst_ref, owner_ref, x_ref, t_ref, out_ref, place_ref):
    size, width = out_ref.shape[0], x_ref.shape[1]
    step = pl.program_id(0)

    @pl.when(step == 0)
    def _():
        slot, rank = places(inst_ref[...], owner_ref, heads)
        place_ref[...] = jnp.broadcast_to(slot * capacity + rank, place_ref.shape)

    pick = one_hot_rows(place_ref[0:1, :], step * size, size)
    out_ref[:, :width] = dot(pick, x_ref[...]).astype(BF16)
    out_ref[:, width:] = dot(pick, t_ref[...]).astype(BF16)


def back_kernel(heads, capacity, inst_ref, owner_ref, back_ref):
    slot, rank = places(inst_ref[...], owner_ref, heads)
    back_ref[...] = one_hot_back(slot * capacity + rank, back_ref.shape[1])


def effective_kernel(w_ref, mask_ref, out_ref):
    for block in range(mask_ref.shape[0]):
        here = slice(block * BLK, (block + 1) * BLK)
        out_ref[here, :] = (w_ref[here, :].astype(F32) * mask_ref[block : block + 1, :]).astype(BF16)


def head_kernel(width, x_ref, eff_ref, weight_ref, grad_ref, res_ref):
    predicted = dot(x_ref[:, :width], eff_ref[...])
    residual = (weight_ref[...] * (predicted - x_ref[:, width:].astype(F32))).astype(BF16)
    res_ref[...] = residual
    grad_ref[...] = dot(residual, eff_ref[...], 1, 1).astype(BF16)


def raw_kernel(x_ref, res_ref, mask_ref, raw_ref, square_ref):
    step = pl.program_id(0)
    size, channels = raw_ref.shape
    raw = dot(x_ref[...], res_ref[...], 0, 0)

    @pl.when(step == 0)
    def _():
        square_ref[...] = jnp.zeros_like(square_ref)

    for block in range(size // BLK):
        here = slice(block * BLK, (block + 1) * BLK)
        part = raw[here, :] * mask_ref[pl.ds(step * (size // BLK) + block, 1), :]
        raw_ref[here, :] = part
        total = jnp.sum((part * part).reshape(BLK // 8, 8, channels), 0)
        for lane in range(channels // 128):
            square_ref[...] += total[:, lane * 128 : (lane + 1) * 128]


def scale_kernel(limit, raw_ref, square_ref, out_ref):
    squares = jnp.sum(square_ref[...], keepdims=True)
    factor = jnp.minimum(1.0, limit / jnp.sqrt(squares + 1e-06))
    out_ref[...] = (raw_ref[...] * factor)[None]


def place_back_kernel(back_ref, got_ref, out_ref):
    out_ref[...] = dot(back_ref[...], got_ref[...]).astype(BF16)


def per_device(latents, obs_inst, owner_slot, head_weights, error_weight, block_pattern, targets):
    members = lax.axis_size("loc")
    local_heads, width, channels = head_weights.shape
    heads = local_heads * members
    rows = latents.shape[0]
    capacity = 2 * rows // heads
    padded = heads * capacity
    wide = width + channels
    inst = obs_inst.reshape(1, rows)
    mask = jnp.repeat(block_pattern[0], BLK, 1).astype(F32)

    def whole(shape):
        return pl.BlockSpec(shape, lambda i: (0, 0))

    cut = 4
    send = pl.pallas_call(
        functools.partial(prep_kernel, heads, capacity),
        grid=(cut,),
        in_specs=[whole((1, rows)), SMEM, whole((rows, width)), whole((rows, channels))],
        out_specs=pl.BlockSpec((padded // cut, wide), lambda i: (i, 0)),
        out_shape=jax.ShapeDtypeStruct((padded, wide), BF16),
        scratch_shapes=[pltpu.VMEM((8, rows), jnp.int32)],
        compiler_params=PARAMS,
        cost_estimate=cost(2 * padded * rows * wide, 2 * (padded + rows) * wide),
        name="prep",
    )(inst, owner_slot, latents, targets)
    got = lax.all_to_all(send, "loc", split_axis=0, concat_axis=0, tiled=True)

    back = pl.pallas_call(
        functools.partial(back_kernel, heads, capacity),
        in_specs=[VMEM, SMEM],
        out_specs=VMEM,
        out_shape=jax.ShapeDtypeStruct((rows, padded), BF16),
        compiler_params=PARAMS,
        cost_estimate=cost(2 * rows * rows * 128, 2 * rows * padded),
        name="back_places",
    )(inst, owner_slot)
    effective = pl.pallas_call(
        effective_kernel,
        in_specs=[VMEM, VMEM],
        out_specs=VMEM,
        out_shape=jax.ShapeDtypeStruct((width, channels), BF16),
        compiler_params=PARAMS,
        cost_estimate=cost(width * channels, 4 * width * channels),
        name="effective",
    )(head_weights[0], mask)

    size = padded // cut
    row_grad, residual = pl.pallas_call(
        functools.partial(head_kernel, width),
        grid=(cut,),
        in_specs=[
            pl.BlockSpec((size, wide), lambda i: (i, 0)),
            whole((width, channels)),
            whole((1, channels)),
        ],
        out_specs=[
            pl.BlockSpec((size, width), lambda i: (i, 0)),
            pl.BlockSpec((size, channels), lambda i: (i, 0)),
        ],
        out_shape=[
            jax.ShapeDtypeStruct((padded, width), BF16),
            jax.ShapeDtypeStruct((padded, channels), BF16),
        ],
        compiler_params=PARAMS,
        cost_estimate=cost(4 * padded * width * channels, 2 * padded * (2 * wide + width)),
        name="heads",
    )(got, effective, error_weight)
    returned = lax.all_to_all(row_grad, "loc", split_axis=0, concat_axis=0, tiled=True)

    tall = 256
    raw_grad, squares = pl.pallas_call(
        raw_kernel,
        grid=(width // tall,),
        in_specs=[
            pl.BlockSpec((padded, tall), lambda i: (0, i)),
            whole((padded, channels)),
            whole(mask.shape),
        ],
        out_specs=[pl.BlockSpec((tall, channels), lambda i: (i, 0)), whole((8, 128))],
        out_shape=[
            jax.ShapeDtypeStruct((width, channels), F32),
            jax.ShapeDtypeStruct((8, 128), F32),
        ],
        compiler_params=PARAMS,
        cost_estimate=cost(2 * padded * width * channels, 4 * width * channels),
        name="raw_grad",
    )(got, residual, mask)
    step = members // 2
    while step:
        squares = squares + lax.ppermute(squares, "loc", [(i, i ^ step) for i in range(members)])
        step //= 2
    head_grad = pl.pallas_call(
        functools.partial(scale_kernel, math.sqrt(heads * width * channels)),
        grid=(cut,),
        in_specs=[
            pl.BlockSpec((width // cut, channels), lambda i: (i, 0)),
            whole((8, 128)),
        ],
        out_specs=pl.BlockSpec((1, width // cut, channels), lambda i: (0, i, 0)),
        out_shape=jax.ShapeDtypeStruct((1, width, channels), F32),
        compiler_params=PARAMS,
        cost_estimate=cost(width * channels, 8 * width * channels),
        name="scale",
    )(raw_grad, squares)
    latent_grad = pl.pallas_call(
        place_back_kernel,
        grid=(cut,),
        in_specs=[whole((rows, padded)), pl.BlockSpec((padded, width // cut), lambda i: (0, i))],
        out_specs=pl.BlockSpec((rows, width // cut), lambda i: (0, i)),
        out_shape=jax.ShapeDtypeStruct((rows, width), BF16),
        compiler_params=PARAMS,
        cost_estimate=cost(2 * rows * padded * width, 4 * padded * width),
        name="place_back",
    )(back, returned)
    return (latent_grad, head_grad)


def solution(mesh):
    in_specs = (
        P(("grp", "loc"), None),
        P(("grp", "loc"), None),
        P(),
        P("loc", None, None),
        P("loc", None),
        P("loc", None, None),
        P(("grp", "loc"), None),
    )
    out_specs = (P(("grp", "loc"), None), P(("grp", "loc"), None, None))
    return jax.shard_map(
        per_device, mesh=mesh, in_specs=in_specs, out_specs=out_specs, check_vma=False
    )
```

time: 263 us -> 259 us (0.985)
  Pallas kernels: 0 us -> 30.5 us
  local copies, waits for them, and re-layouts: 32.9 us -> 7.06 us
  waiting for transfers between devices: 163 us -> 182 us
  matrix products: 16.4 us -> 0 us
  other arithmetic: 10.9 us -> 0.02 us
    pallas_call x0 -> x7, Pallas kernels: none -> 30.5 us  [the longest x1 8.16 us: per_device(): pl.pallas_call(functools.partial(head_kernel, width), grid=(cut,), in_spe...]
    dot_general x3 -> x0, matrix products: 16.4 us -> none  [the longest x1 6.15 us: per_device(): jnp.dot(arrived, effective[0], preferred_element_type=jnp.float32)]
    ppermute x4, waiting for transfers between devices: 74.7 us -> 87.5 us  [per_device(): lax.ppermute(squares, 'loc', [(i, i ^ step) for i in range(members)])]
    broadcast_in_dim x5 -> x1, local copies, waits for them, and re-layouts: 11.2 us -> 0.08 us  [per_device(): mask = jnp.repeat(block_pattern[0], BLK, 1).astype(F32)]
    scatter x2 -> x0, local copies, waits for them, and re-layouts: 10.5 us -> none  [the longest x1 7.3 us: per_device(): jnp.zeros((instruments * capacity, width), latents.dtype).at[placed]]
    gather x1 -> x0, local copies, waits for them, and re-layouts: 7.95 us -> none  [per_device(): latent_grad = returned[placed]]
    unnamed x8 -> x23, local copies, waits for them, and re-layouts: 0.02 us -> 6.9 us
    all_to_all x1, waiting for transfers between devices: 88.1 us -> 94.5 us  [per_device(): got = lax.all_to_all(send, 'loc', split_axis=0, concat_axis=0, tiled=True)]
  transfers between devices with their start and end apart: 6 -> 6, of which waited for: 5 -> 4; matrix products, arithmetic and copies ran while one was open for 9% -> 0% of each run, Pallas kernels for 0% -> 4%
where the time goes in v2:
time: 259 us; the launch traced here: 258 us
  waiting for transfers between devices  182 us (70%)
  starting transfers between devices  38 us (15%)
  Pallas kernels  30.5 us (12%)
  local copies, waits for them, and re-layouts  7.06 us (3%)
    all_to_all x1, waiting for transfers between devices, per_device(): got = lax.all_to_all(send, 'loc', split_axis=0, concat_axis=0, tiled=True)  94.5 us
    ppermute x4, waiting for transfers between devices, per_device(): lax.ppermute(squares, 'loc', [(i, i ^ step) for i in range(members)])  87.5 us
    all_to_all x1, starting transfers between devices, per_device(): lax.all_to_all(row_grad, 'loc', split_axis=0, concat_axis=0, tiled=True)  23.5 us
    pallas_call x1, Pallas kernels, per_device(): pl.pallas_call(functools.partial(head_kernel, width), grid=(cut,), in_spe...  8.16 us
    all_to_all x1, starting transfers between devices, per_device(): got = lax.all_to_all(send, 'loc', split_axis=0, concat_axis=0, tiled=True)  7.48 us
    pallas_call x1, Pallas kernels, per_device(): pl.pallas_call(raw_kernel, grid=(width // tall,), in_specs=[pl.BlockSpec(...  7.03 us
    ppermute x4, starting transfers between devices, per_device(): lax.ppermute(squares, 'loc', [(i, i ^ step) for i in range(members)])  7 us
    unnamed x23, local copies, waits for them, and re-layouts  6.9 us
  transfers between devices with their start and end apart: 6, of which 4 were waited for; matrix products, arithmetic and copies ran while one was open for 0% of the time, Pallas kernels for 4%

profile of v2, /device:TPU:1, one launch (start us, length us, event | category | flops | bytes accessed | tf_op | source)
XLA Modules:
  0.0 258.2 jit_solution(8084873768699897753)
XLA Ops:
  0.6 0.0 copy-start.3
  0.6 0.7 copy-done.3
  1.3 0.7 copy-done.5
  2.0 1.6 copy-done.7
  3.6 1.0 copy-done.8
  4.6 5.5 %prep.1 = bf16[1024,2560]{1,0:T(8,128)(2,1)} custom-call(s32[1,512]{1,0:T(1,128)S(1)} %bitcast.15, s32[16]{0:T(128)S(1)} %copy-done.5, bf16[512,2048]{1,0:T(8,128)(2,1)S(1)} %copy-done.7, bf16[512,512]{1,0:T(8,128)(2,1)S(1)} %copy-done.8), custom_call_target="tpu_custom_call" | custom-call | flops 2684354560 | bytes 7864320 | tf_op jit(solution)/shard_map/prep/pallas_call | solution.py:127
  10.1 7.5 %all-to-all-start = ((bf16[16,64,2560]{2,1,0:T(8,128)(2,1)}), bf16[16,64,2560]{2,1,0:T(8,128)(2,1)}, u32[]{:S(2)}, u32[]{:S(2)}) async-start(bf16[16,64,2560]{2,1,0:T(8,128)(2,1)} %bitcast.17), calls=%async_computation | async-start | bytes 10485760 | tf_op jit(solution)/shard_map/all_to_all | solution.py:138
  17.6 0.0 copy-start.9
  17.6 0.1 copy.9
  17.7 0.1 broadcast_in_dim.3
  17.8 0.3 effective.1.eff_ref
  18.2 0.0 copy-start.1
  18.2 1.3 copy-done.1
  19.5 94.5 %all-to-all-done = bf16[16,64,2560]{2,1,0:T(8,128)(2,1)} async-done(((bf16[16,64,2560]{2,1,0:T(8,128)(2,1)}), bf16[16,64,2560]{2,1,0:T(8,128)(2,1)}, u32[]{:S(2)}, u32[]{:S(2)}) %all-to-all-start) | async-done | bytes 5242912 | tf_op jit(solution)/shard_map/all_to_all | solution.py:138
  113.9 0.0 copy-done.9
  114.0 1.6 copy-done.2
  115.5 8.2 %heads.1 = (bf16[1024,2048]{1,0:T(8,128)(2,1)}, bf16[1024,512]{1,0:T(8,128)(2,1)S(1)}) custom-call(bf16[1024,2560]{1,0:T(8,128)(2,1)} %bitcast.2.x_ref, bf16[2048,512]{1,0:T(8,128)(2,1)S(1)} %copy-done.2, f32[1,512]{1,0:T(1,128)S(1)} %copy-done.9), custom_call_target="tpu_custom_call" | custom-call | flops 4294967296 | bytes 14680064 | tf_op jit(solution)/shard_map/heads/pallas_call | solution.py:160
  123.7 23.5 %all-to-all-start.1 = ((bf16[16,64,2048]{2,1,0:T(8,128)(2,1)}), bf16[16,64,2048]{2,1,0:T(8,128)(2,1)}, u32[]{:S(2)}, u32[]{:S(2)}) async-start(bf16[16,64,2048]{2,1,0:T(8,128)(2,1)} %bitcast.18), calls=%async_computation.1 | async-start | bytes 8388608 | tf_op jit(solution)/shard_map/all_to_all | solution.py:180
  147.2 0.0 copy-start.6
  147.2 7.0 %raw_grad.1 = (f32[2048,512]{1,0:T(8,128)S(1)}, f32[8,128]{1,0:T(8,128)S(1)}) custom-call(bf16[1024,2560]{1,0:T(8,128)(2,1)} %bitcast.2.x_ref, bf16[1024,512]{1,0:T(8,128)(2,1)S(1)} %get-tuple-element.7.res_ref, f32[16,512]{1,0:T(8,128)S(1)} %bitcast.14), custom_call_target="tpu_custom_call" | custom-call | flops 2147483648 | bytes 4194304 | tf_op jit(solution)/shard_map/raw_grad/pallas_call | solution.py:183
  154.3 2.3 collective-permute-start
  156.6 83.8 %collective-permute-done = f32[8,128]{1,0:T(8,128)S(1)} collective-permute-done((f32[8,128]{1,0:T(8,128)S(1)}, f32[8,128]{1,0:T(8,128)S(1)}, u32[]{:S(2)}, u32[]{:S(2)}) %collective-permute-start) | collective-permute-done | bytes 4128 | tf_op jit(solution)/shard_map/ppermute | solution.py:202
  240.4 0.0 collective-permute-start.1
  240.4 2.5 collective-permute-done.1
  242.8 1.2 collective-permute-start.2
  244.0 1.3 collective-permute-done.2
  245.3 3.5 %collective-permute-start.3 = (f32[8,128]{1,0:T(8,128)S(1)}, f32[8,128]{1,0:T(8,128)S(1)}, u32[]{:S(2)}, u32[]{:S(2)}) collective-permute-start(f32[8,128]{1,0:T(8,128)S(1)} %add.14), channel_id=1, source_target_pairs={{0,1},{1,0},{2,3},{3,2},{4,5},{5,4},{6,7},{7,6},{8,9},{9,8},{10,11... | collective-permute-start | bytes 12296 | tf_op jit(solution)/shard_map/ppermute | solution.py:202
  248.8 1.1 back_places.1.back_ref
  249.8 0.0 collective-permute-done.3
  249.9 2.7 %scale.1 = f32[1,2048,512]{2,1,0:T(8,128)} custom-call(f32[2048,512]{1,0:T(8,128)S(1)} %get-tuple-element.8.raw_ref, f32[8,128]{1,0:T(8,128)S(1)} %add.15.square_ref), custom_call_target="tpu_custom_call" | custom-call | flops 1048576 | bytes 8388608 | tf_op jit(solution)/shard_map/scale/pallas_call | solution.py:204
  252.6 0.0 all-to-all-done.1
  252.6 5.7 %place_back.1 = bf16[512,2048]{1,0:T(8,128)(2,1)} custom-call(bf16[512,1024]{1,0:T(8,128)(2,1)S(1)} %back_places.1.back_ref, bf16[1024,2048]{1,0:T(8,128)(2,1)} %bitcast.6.got_ref), custom_call_target="tpu_custom_call" | custom-call | flops 2147483648 | bytes 8388608 | tf_op jit(solution)/shard_map/place_back/pallas_call | solution.py:217
  (17 shorter events, 0.0 us)
Async XLA Ops:
  0.6 0.7 copy-start.3
  1.3 0.7 copy-start.5
  2.0 1.6 copy-start.7
  3.6 1.0 copy-start.8
  10.1 7.5 %copy-start.10 = (s32[1,16,4]{1,2,0:T(4,128)S(1)}, s32[1,16,4]{1,2,0:T(4,128)}, u32[]{:S(2)}) copy-start(s32[1,16,4]{1,2,0:T(4,128)} %param.12) | copy-start | bytes 772
  10.1 7.7 %copy-start = (bf16[1,2048,512]{2,1,0:T(8,128)(2,1)S(1)}, bf16[1,2048,512]{2,1,0:T(8,128)(2,1)}, u32[]{:S(2)}) copy-start(bf16[1,2048,512]{2,1,0:T(8,128)(2,1)} %param.10) | copy-start | bytes 6291460
  10.1 103.8 %all-to-all-start = ((bf16[16,64,2560]{2,1,0:T(8,128)(2,1)}), bf16[16,64,2560]{2,1,0:T(8,128)(2,1)}, u32[]{:S(2)}, u32[]{:S(2)}) async-start(bf16[16,64,2560]{2,1,0:T(8,128)(2,1)} %bitcast.17), calls=%async_computation | async-start | bytes 10485760 | tf_op jit(solution)/shard_map/all_to_all | solution.py:138
  17.6 96.3 %copy-start.9 = (f32[1,512]{1,0:T(1,128)S(1)}, f32[1,512]{1,0:T(1,128)}, u32[]{:S(2)}) copy-start(f32[1,512]{1,0:T(1,128)} %weight_ref.1) | copy-start | bytes 6148
  18.2 1.3 copy-start.1
  114.0 1.6 copy-start.2
  123.7 128.9 %all-to-all-start.1 = ((bf16[16,64,2048]{2,1,0:T(8,128)(2,1)}), bf16[16,64,2048]{2,1,0:T(8,128)(2,1)}, u32[]{:S(2)}, u32[]{:S(2)}) async-start(bf16[16,64,2048]{2,1,0:T(8,128)(2,1)} %bitcast.18), calls=%async_computation.1 | async-start | bytes 8388608 | tf_op jit(solution)/shard_map/all_to_all | solution.py:180
  147.2 101.6 %copy-start.4 = (s32[512,1]{0,1:T(1,128)S(1)}, s32[512,1]{0,1:T(1,128)}, u32[]{:S(2)}) copy-start(s32[512,1]{0,1:T(1,128)} %param.8) | copy-start | bytes 6148
  147.2 101.6 %copy-start.6 = (s32[16]{0:T(128)S(1)}, s32[16]{0:T(128)}, u32[]{:S(2)}) copy-start(s32[16]{0:T(128)} %owner_ref.3) | copy-start | bytes 196
  154.3 86.1 %collective-permute-start = (f32[8,128]{1,0:T(8,128)S(1)}, f32[8,128]{1,0:T(8,128)S(1)}, u32[]{:S(2)}, u32[]{:S(2)}) collective-permute-start(f32[8,128]{1,0:T(8,128)S(1)} %get-tuple-element.9), channel_id=1, source_target_pairs={{0,8},{1,9},{2,10},{3,11},{4,12},{5,13},{6,14},{7,15},{8,0},{9,1},... | collective-permute-start | bytes 12296 | tf_op jit(solution)/shard_map/ppermute | solution.py:202
  240.4 2.5 collective-permute-start.1
  242.8 2.5 collective-permute-start.2
  245.3 4.6 %collective-permute-start.3 = (f32[8,128]{1,0:T(8,128)S(1)}, f32[8,128]{1,0:T(8,128)S(1)}, u32[]{:S(2)}, u32[]{:S(2)}) collective-permute-start(f32[8,128]{1,0:T(8,128)S(1)} %add.14), channel_id=1, source_target_pairs={{0,1},{1,0},{2,3},{3,2},{4,5},{5,4},{6,7},{7,6},{8,9},{9,8},{10,11... | collective-permute-start | bytes 12296 | tf_op jit(solution)/shard_map/ppermute | solution.py:202

commit v3 on v2

--- a/solution.py
+++ b/solution.py
@@ -13,7 +13,7 @@
 BF16 = jnp.bfloat16
 VMEM = pl.BlockSpec(memory_space=pltpu.VMEM)
 SMEM = pl.BlockSpec(memory_space=pltpu.SMEM)
-PARAMS = pltpu.CompilerParams(vmem_limit_bytes=48 * 1024 * 1024)
+PARAMS = pltpu.CompilerParams(vmem_limit_bytes=60 * 1024 * 1024)
 
 
 def dot(a, b, ca=1, cb=0):
@@ -156,6 +156,7 @@
         name="effective",
     )(head_weights[0], mask)
 
+    got, back, effective = lax.optimization_barrier((got, back, effective))
     size = padded // cut
     row_grad, residual = pl.pallas_call(
         functools.partial(head_kernel, width),
@@ -197,10 +198,21 @@
         cost_estimate=cost(2 * padded * width * channels, 4 * width * channels),
         name="raw_grad",
     )(got, residual, mask)
-    step = members // 2
-    while step:
+    step = 1
+    while step < members:
         squares = squares + lax.ppermute(squares, "loc", [(i, i ^ step) for i in range(members)])
-        step //= 2
+        step *= 2
+    latent_grad = pl.pallas_call(
+        place_back_kernel,
+        grid=(cut,),
+        in_specs=[whole((rows, padded)), pl.BlockSpec((padded, width // cut), lambda i: (0, i))],
+        out_specs=pl.BlockSpec((rows, width // cut), lambda i: (0, i)),
+        out_shape=jax.ShapeDtypeStruct((rows, width), BF16),
+        compiler_params=PARAMS,
+        cost_estimate=cost(2 * rows * padded * width, 4 * padded * width),
+        name="place_back",
+    )(back, returned)
+    latent_grad, squares = lax.optimization_barrier((latent_grad, squares))
     head_grad = pl.pallas_call(
         functools.partial(scale_kernel, math.sqrt(heads * width * channels)),
         grid=(cut,),
@@ -214,16 +226,6 @@
         cost_estimate=cost(width * channels, 8 * width * channels),
         name="scale",
     )(raw_grad, squares)
-    latent_grad = pl.pallas_call(
-        place_back_kernel,
-        grid=(cut,),
-        in_specs=[whole((rows, padded)), pl.BlockSpec((padded, width // cut), lambda i: (0, i))],
-        out_specs=pl.BlockSpec((rows, width // cut), lambda i: (0, i)),
-        out_shape=jax.ShapeDtypeStruct((rows, width), BF16),
-        compiler_params=PARAMS,
-        cost_estimate=cost(2 * rows * padded * width, 4 * padded * width),
-        name="place_back",
-    )(back, returned)
     return (latent_grad, head_grad)
 
 

time: 259 us -> 250 us (0.965)
  waiting for transfers between devices: 182 us -> 168 us
  Pallas kernels: 30.5 us -> 40.7 us
  local copies, waits for them, and re-layouts: 7.06 us -> 0.79 us
    ppermute x4, waiting for transfers between devices: 87.5 us -> 78 us  [per_device(): lax.ppermute(squares, 'loc', [(i, i ^ step) for i in range(members)])]
    unnamed x23 -> x3, local copies, waits for them, and re-layouts: 6.9 us -> 0.63 us
    all_to_all x1, waiting for transfers between devices: 94.5 us -> 90 us  [per_device(): got = lax.all_to_all(send, 'loc', split_axis=0, concat_axis=0, tiled=True)]
    pallas_call x1, Pallas kernels: 0.34 us -> 3.25 us  [per_device(): pl.pallas_call(effective_kernel, in_specs=[VMEM, VMEM], out_specs=VMEM, o...]
  transfers between devices with their start and end apart: 6 -> 6, of which waited for: 4 -> 5; matrix products, arithmetic and copies ran while one was open for 0% -> 1% of each run, Pallas kernels for 4% -> 6%
where the time goes in v3:
time: 250 us; the launch traced here: 248 us
  waiting for transfers between devices  168 us (67%)
  Pallas kernels  40.7 us (16%)
  starting transfers between devices  36.7 us (15%)
    all_to_all x1, waiting for transfers between devices, per_device(): got = lax.all_to_all(send, 'loc', split_axis=0, concat_axis=0, tiled=True)  90 us
    ppermute x4, waiting for transfers between devices, per_device(): lax.ppermute(squares, 'loc', [(i, i ^ step) for i in range(members)])  78 us
    all_to_all x1, starting transfers between devices, per_device(): lax.all_to_all(row_grad, 'loc', split_axis=0, concat_axis=0, tiled=True)  23.5 us
    pallas_call x1, Pallas kernels, per_device(): pl.pallas_call(functools.partial(head_kernel, width), grid=(cut,), in_spe...  8.79 us
    pallas_call x1, Pallas kernels, per_device(): pl.pallas_call(raw_kernel, grid=(width // tall,), in_specs=[pl.BlockSpec(...  8.76 us
    all_to_all x1, starting transfers between devices, per_device(): got = lax.all_to_all(send, 'loc', split_axis=0, concat_axis=0, tiled=True)  7.48 us
    pallas_call x1, Pallas kernels, per_device(): pl.pallas_call(functools.partial(prep_kernel, heads, capacity), grid=(cut...  6.66 us
    pallas_call x1, Pallas kernels, per_device(): pl.pallas_call(place_back_kernel, grid=(cut,), in_specs=[whole((rows, pad...  5.99 us
  transfers between devices with their start and end apart: 6, of which 5 were waited for; matrix products, arithmetic and copies ran while one was open for 1% of the time, Pallas kernels for 6%

profile of v3, /device:TPU:1, one launch (start us, length us, event | category | flops | bytes accessed | tf_op | source)
XLA Modules:
  0.0 248.1 jit_solution(17039316799940506940)
XLA Ops:
  0.6 6.7 %prep.1 = bf16[1024,2560]{1,0:T(8,128)(2,1)} custom-call(s32[1,512]{1,0:T(1,128)} %bitcast.18, s32[16]{0:T(128)} %owner_ref.3, bf16[512,2048]{1,0:T(8,128)(2,1)} %x_ref.1, bf16[512,512]{1,0:T(8,128)(2,1)} %t_ref.1), custom_call_target="tpu_custom_call" | custom-call | flops 2684354560 | bytes 7864320 | tf_op jit(solution)/shard_map/prep/pallas_call | solution.py:127
  7.3 0.0 copy-start
  7.3 7.5 %all-to-all-start = ((bf16[16,64,2560]{2,1,0:T(8,128)(2,1)}), bf16[16,64,2560]{2,1,0:T(8,128)(2,1)}, u32[]{:S(2)}, u32[]{:S(2)}) async-start(bf16[16,64,2560]{2,1,0:T(8,128)(2,1)} %bitcast.12), calls=%async_computation | async-start | bytes 10485760 | tf_op jit(solution)/shard_map/all_to_all | solution.py:138
  14.8 0.0 copy-done
  14.8 0.1 copy.9
  14.9 0.1 broadcast_in_dim.3
  15.0 0.6 copy.12
  15.6 3.3 %effective.1.eff_ref = bf16[2048,512]{1,0:T(8,128)(2,1)} custom-call(bf16[2048,512]{1,0:T(8,128)(2,1)} %bitcast.14, f32[16,512]{1,0:T(8,128)} %bitcast.15), custom_call_target="tpu_custom_call" | custom-call | flops 1048576 | bytes 4194304 | tf_op jit(solution)/shard_map/effective/pallas_call | solution.py:149
  18.8 2.3 back_places.1.back_ref
  21.1 90.0 %all-to-all-done = bf16[16,64,2560]{2,1,0:T(8,128)(2,1)} async-done(((bf16[16,64,2560]{2,1,0:T(8,128)(2,1)}), bf16[16,64,2560]{2,1,0:T(8,128)(2,1)}, u32[]{:S(2)}, u32[]{:S(2)}) %all-to-all-start) | async-done | bytes 5242912 | tf_op jit(solution)/shard_map/all_to_all | solution.py:138
  111.1 8.8 %heads.1 = (bf16[1024,2048]{1,0:T(8,128)(2,1)}, bf16[1024,512]{1,0:T(8,128)(2,1)}) custom-call(bf16[1024,2560]{1,0:T(8,128)(2,1)} %bitcast.2.x_ref, bf16[2048,512]{1,0:T(8,128)(2,1)} %effective.1.eff_ref, f32[1,512]{1,0:T(1,128)} %weight_ref.1), custom_call_target="tpu_custom_call" | custom-call | flops 4294967296 | bytes 14680064 | tf_op jit(solution)/shard_map/heads/pallas_call | solution.py:161
  119.9 23.5 %all-to-all-start.1 = ((bf16[16,64,2048]{2,1,0:T(8,128)(2,1)}), bf16[16,64,2048]{2,1,0:T(8,128)(2,1)}, u32[]{:S(2)}, u32[]{:S(2)}) async-start(bf16[16,64,2048]{2,1,0:T(8,128)(2,1)} %bitcast.13), calls=%async_computation.1 | async-start | bytes 8388608 | tf_op jit(solution)/shard_map/all_to_all | solution.py:181
  143.4 8.8 %raw_grad.1 = (f32[2048,512]{1,0:T(8,128)}, f32[8,128]{1,0:T(8,128)}) custom-call(bf16[1024,2560]{1,0:T(8,128)(2,1)} %bitcast.2.x_ref, bf16[1024,512]{1,0:T(8,128)(2,1)} %get-tuple-element.15.res_ref, f32[16,512]{1,0:T(8,128)} %bitcast.16), custom_call_target="tpu_custom_call" | custom-call | flops 2147483648 | bytes 4194304 | tf_op jit(solution)/shard_map/raw_grad/pallas_call | solution.py:184
  152.2 0.2 collective-permute-start
  152.3 1.2 collective-permute-done
  153.6 0.7 add.12
  154.2 1.4 collective-permute-start.1
  155.7 8.2 %collective-permute-done.1 = f32[8,128]{1,0:T(8,128)S(1)} collective-permute-done((f32[8,128]{1,0:T(8,128)S(1)}, f32[8,128]{1,0:T(8,128)S(1)}, u32[]{:S(2)}, u32[]{:S(2)}) %collective-permute-start.1) | collective-permute-done | bytes 4128 | tf_op jit(solution)/shard_map/ppermute | solution.py:203
  163.9 0.1 collective-permute-start.2
  164.0 47.6 %collective-permute-done.2 = f32[8,128]{1,0:T(8,128)S(1)} collective-permute-done((f32[8,128]{1,0:T(8,128)S(1)}, f32[8,128]{1,0:T(8,128)S(1)}, u32[]{:S(2)}, u32[]{:S(2)}) %collective-permute-start.2) | collective-permute-done | bytes 4128 | tf_op jit(solution)/shard_map/ppermute | solution.py:203
  211.6 4.0 %collective-permute-start.3 = (f32[8,128]{1,0:T(8,128)S(1)}, f32[8,128]{1,0:T(8,128)S(1)}, u32[]{:S(2)}, u32[]{:S(2)}) collective-permute-start(f32[8,128]{1,0:T(8,128)S(1)} %add.14), channel_id=1, source_target_pairs={{0,8},{1,9},{2,10},{3,11},{4,12},{5,13},{6,14},{7,15},{8,0},{9,1},... | collective-permute-start | bytes 12296 | tf_op jit(solution)/shard_map/ppermute | solution.py:203
  215.7 20.9 %collective-permute-done.3 = f32[8,128]{1,0:T(8,128)S(1)} collective-permute-done((f32[8,128]{1,0:T(8,128)S(1)}, f32[8,128]{1,0:T(8,128)S(1)}, u32[]{:S(2)}, u32[]{:S(2)}) %collective-permute-start.3) | collective-permute-done | bytes 4128 | tf_op jit(solution)/shard_map/ppermute | solution.py:203
  236.6 0.6 add.15.square_ref
  237.2 0.0 all-to-all-done.1
  237.2 6.0 %place_back.1 = bf16[512,2048]{1,0:T(8,128)(2,1)} custom-call(bf16[512,1024]{1,0:T(8,128)(2,1)} %back_places.1.back_ref, bf16[1024,2048]{1,0:T(8,128)(2,1)} %bitcast.6.got_ref), custom_call_target="tpu_custom_call" | custom-call | flops 2147483648 | bytes 8388608 | tf_op jit(solution)/shard_map/place_back/pallas_call | solution.py:205
  243.2 5.0 %scale.1 = f32[1,2048,512]{2,1,0:T(8,128)} custom-call(f32[2048,512]{1,0:T(8,128)} %get-tuple-element.18.raw_ref, f32[8,128]{1,0:T(8,128)} %add.15.square_ref), custom_call_target="tpu_custom_call" | custom-call | flops 1048576 | bytes 8388608 | tf_op jit(solution)/shard_map/scale/pallas_call | solution.py:216
  (3 shorter events, 0.0 us)
Async XLA Ops:
  7.3 7.5 %copy-start = (s32[1,16,4]{1,2,0:T(4,128)S(1)}, s32[1,16,4]{1,2,0:T(4,128)}, u32[]{:S(2)}) copy-start(s32[1,16,4]{1,2,0:T(4,128)} %param.12) | copy-start | bytes 772
  7.3 103.8 %all-to-all-start = ((bf16[16,64,2560]{2,1,0:T(8,128)(2,1)}), bf16[16,64,2560]{2,1,0:T(8,128)(2,1)}, u32[]{:S(2)}, u32[]{:S(2)}) async-start(bf16[16,64,2560]{2,1,0:T(8,128)(2,1)} %bitcast.12), calls=%async_computation | async-start | bytes 10485760 | tf_op jit(solution)/shard_map/all_to_all | solution.py:138
  119.9 117.3 %all-to-all-start.1 = ((bf16[16,64,2048]{2,1,0:T(8,128)(2,1)}), bf16[16,64,2048]{2,1,0:T(8,128)(2,1)}, u32[]{:S(2)}, u32[]{:S(2)}) async-start(bf16[16,64,2048]{2,1,0:T(8,128)(2,1)} %bitcast.13), calls=%async_computation.1 | async-start | bytes 8388608 | tf_op jit(solution)/shard_map/all_to_all | solution.py:181
  152.2 1.4 collective-permute-start
  154.2 9.6 %collective-permute-start.1 = (f32[8,128]{1,0:T(8,128)S(1)}, f32[8,128]{1,0:T(8,128)S(1)}, u32[]{:S(2)}, u32[]{:S(2)}) collective-permute-start(f32[8,128]{1,0:T(8,128)S(1)} %add.12), channel_id=1, source_target_pairs={{0,2},{1,3},{2,0},{3,1},{4,6},{5,7},{6,4},{7,5},{8,10},{9,11},{10,... | collective-permute-start | bytes 12296 | tf_op jit(solution)/shard_map/ppermute | solution.py:203
  163.9 47.8 %collective-permute-start.2 = (f32[8,128]{1,0:T(8,128)S(1)}, f32[8,128]{1,0:T(8,128)S(1)}, u32[]{:S(2)}, u32[]{:S(2)}) collective-permute-start(f32[8,128]{1,0:T(8,128)S(1)} %add.13), channel_id=1, source_target_pairs={{0,4},{1,5},{2,6},{3,7},{4,0},{5,1},{6,2},{7,3},{8,12},{9,13},{10,... | collective-permute-start | bytes 12296 | tf_op jit(solution)/shard_map/ppermute | solution.py:203
  211.6 24.9 %collective-permute-start.3 = (f32[8,128]{1,0:T(8,128)S(1)}, f32[8,128]{1,0:T(8,128)S(1)}, u32[]{:S(2)}, u32[]{:S(2)}) collective-permute-start(f32[8,128]{1,0:T(8,128)S(1)} %add.14), channel_id=1, source_target_pairs={{0,8},{1,9},{2,10},{3,11},{4,12},{5,13},{6,14},{7,15},{8,0},{9,1},... | collective-permute-start | bytes 12296 | tf_op jit(solution)/shard_map/ppermute | solution.py:203

commit v4 on v1

v4 whole, which is shorter than its diff:
```python
import functools
import math

import jax
import jax.numpy as jnp
from jax import lax
from jax.experimental import pallas as pl
from jax.experimental.pallas import tpu as pltpu
from jax.sharding import PartitionSpec as P


BLK = 128
CHUNKS = 2
F32 = jnp.float32
BF16 = jnp.bfloat16
VMEM = pl.BlockSpec(memory_space=pltpu.VMEM)
SMEM = pl.BlockSpec(memory_space=pltpu.SMEM)
STREAM = pltpu.CompilerParams(vmem_limit_bytes=60 * 1024 * 1024)
SMALL = pltpu.CompilerParams(vmem_limit_bytes=32 * 1024 * 1024)


def dot(a, b, ca=1, cb=0):
    return lax.dot_general(a, b, (((ca,), (cb,)), ((), ())), preferred_element_type=F32)


def cost(flops, nbytes):
    return pl.CostEstimate(flops=int(flops), bytes_accessed=int(nbytes), transcendentals=0)


def whole(shape):
    return pl.BlockSpec(shape, lambda i: (0,) * len(shape))


def places(inst, owner_ref, heads):
    rows = inst.shape[1]
    slot = jnp.zeros_like(inst)
    for k in range(heads):
        slot = jnp.where(inst == k, owner_ref[k], slot)
    hit = lax.broadcasted_iota(jnp.int32, (heads, rows), 0) == slot
    upto = lax.broadcasted_iota(jnp.int32, (rows, rows), 0) <= lax.broadcasted_iota(
        jnp.int32, (rows, rows), 1
    )
    count = dot(hit.astype(BF16), upto.astype(BF16))
    rank = jnp.sum(jnp.where(hit, count, 0.0), 0, keepdims=True).astype(jnp.int32) - 1
    return slot, rank


def half_places(inst, owner_ref, heads, capacity):
    slot, rank = places(inst, owner_ref, heads)
    half = heads // 2
    mine = (slot >= half) == (lax.axis_index("loc") >= half)
    place = jnp.where(slot >= half, slot - half, slot) * capacity + rank
    return jnp.where(mine, place, -1), jnp.where(mine, -1, place)


def one_hot_back(pos, size):
    column = jnp.transpose(jnp.broadcast_to(pos.astype(F32), (128, pos.shape[1])))[:, :1]
    number = lax.broadcasted_iota(jnp.int32, (pos.shape[1], size), 1)
    return (number == column.astype(jnp.int32)).astype(F32).astype(BF16)


def prep_kernel(heads, capacity, which, inst_ref, owner_ref, x_ref, t_ref, out_ref, place_ref):
    size, width = out_ref.shape[0], x_ref.shape[1]
    step = pl.program_id(0)

    @pl.when(step == 0)
    def _():
        place = half_places(inst_ref[...], owner_ref, heads, capacity)[which]
        place_ref[...] = jnp.broadcast_to(place, place_ref.shape)

    number = lax.broadcasted_iota(jnp.int32, (size, inst_ref.shape[1]), 0) + step * size
    pick = (number == place_ref[0:1, :]).astype(F32).astype(BF16)
    out_ref[:, :width] = dot(pick, x_ref[...]).astype(BF16)
    out_ref[:, width:] = dot(pick, t_ref[...]).astype(BF16)


def back_kernel(heads, capacity, inst_ref, owner_ref, near_ref, far_ref):
    near, far = half_places(inst_ref[...], owner_ref, heads, capacity)
    near_ref[...] = one_hot_back(near, near_ref.shape[1])
    far_ref[...] = one_hot_back(far, far_ref.shape[1])


def masked(block, pattern_ref, row, column):
    return (block.astype(F32) * pattern_ref[0, row, column].astype(F32)).astype(BF16)


def piece_kernel(w_ref, pattern_ref, *out_refs):
    rows, channels = out_refs[0].shape
    for chunk, out_ref in enumerate(out_refs):
        first = (lax.axis_index("grp") * len(out_refs) + chunk) * (rows // BLK)
        for i in range(rows // BLK):
            here = pl.ds(pl.multiple_of((first + i) * BLK, BLK), BLK)
            for j in range(channels // BLK):
                cols = slice(j * BLK, (j + 1) * BLK)
                out_ref[i * BLK : (i + 1) * BLK, cols] = masked(
                    w_ref[0, here, cols], pattern_ref, first + i, j
                )


def effective_kernel(w_ref, pattern_ref, out_ref):
    width, channels = out_ref.shape
    for i in range(width // BLK):
        for j in range(channels // BLK):
            rows, cols = slice(i * BLK, (i + 1) * BLK), slice(j * BLK, (j + 1) * BLK)
            out_ref[rows, cols] = masked(w_ref[0, rows, cols], pattern_ref, i, j)


def head_kernel(width, x_ref, eff_ref, weight_ref, grad_ref, res_ref):
    predicted = dot(x_ref[:, :width], eff_ref[...])
    residual = (weight_ref[...] * (predicted - x_ref[:, width:].astype(F32))).astype(BF16)
    res_ref[...] = residual
    grad_ref[...] = dot(residual, eff_ref[...], 1, 1).astype(BF16)


def far_head_kernel(width, count, x_ref, weight_ref, *refs):
    eff_refs, (grad_ref, res_ref) = refs[:count], refs[count:]
    deep = eff_refs[0].shape[0]
    group = lax.axis_index("grp")

    def columns(number):
        first = (group ^ (number // CHUNKS)) * CHUNKS + number % CHUNKS
        return pl.ds(pl.multiple_of(first * deep, deep), deep)

    predicted = dot(x_ref[:, columns(0)], eff_refs[0][...])
    for number in range(1, count):
        predicted += dot(x_ref[:, columns(number)], eff_refs[number][...])
    residual = (weight_ref[...] * (predicted - x_ref[:, width:].astype(F32))).astype(BF16)
    res_ref[...] = residual
    for number in range(count):
        grad_ref[:, columns(number)] = dot(residual, eff_refs[number][...], 1, 1).astype(BF16)


def far_raw_kernel(x_ref, res_ref, out_ref):
    out_ref[...] = dot(x_ref[...], res_ref[...], 0, 0).astype(BF16)


def raw_kernel(first, x_ref, res_ref, far_ref, pattern_ref, raw_ref, square_ref):
    step = pl.program_id(0)
    size, channels = raw_ref.shape
    raw = dot(x_ref[...], res_ref[...], 0, 0) + far_ref[...].astype(F32)

    @pl.when(step == 0)
    def _():
        square_ref[...] = jnp.zeros_like(square_ref)

    for i in range(size // BLK):
        for j in range(channels // BLK):
            rows, cols = slice(i * BLK, (i + 1) * BLK), slice(j * BLK, (j + 1) * BLK)
            used = pattern_ref[0, first + step * (size // BLK) + i, j].astype(F32)
            part = raw[rows, cols] * used
            raw_ref[rows, cols] = part
            square_ref[...] += jnp.sum((part * part).reshape(BLK // 8, 8, BLK), 0)


def scale_kernel(limit, parts, *refs):
    raw_refs, square_ref, out_ref = refs[:parts], refs[parts], refs[parts + 1]
    squares = jnp.sum(square_ref[...], keepdims=True)
    factor = jnp.minimum(1.0, limit / jnp.sqrt(squares + 1e-06))
    step = pl.program_id(0)
    per = pl.num_programs(0) // parts
    for part in range(parts):

        @pl.when(step // per == part)
        def _():
            out_ref[...] = (raw_refs[part][...] * factor)[None]


def place_back_kernel(near_ref, far_ref, near_got_ref, far_got_ref, out_ref):
    out = dot(near_ref[...], near_got_ref[...]) + dot(far_ref[...], far_got_ref[...])
    out_ref[...] = out.astype(BF16)


def per_device(latents, obs_inst, owner_slot, head_weights, error_weight, block_pattern, targets):
    members, groups = lax.axis_size("loc"), lax.axis_size("grp")
    local_heads, width, channels = head_weights.shape
    heads = local_heads * members
    rows = latents.shape[0]
    capacity = 2 * rows // heads
    half = members // 2
    placed = half * capacity
    wide = width + channels
    inst = obs_inst.reshape(1, rows)
    halves = [list(range(half)), list(range(half, members))]

    def partner(x):
        return lax.ppermute(x, "loc", [(i, i ^ half) for i in range(members)])

    def in_half(x):
        return lax.all_to_all(
            x, "loc", split_axis=0, concat_axis=0, tiled=True, axis_index_groups=halves
        )

    deep = width // (groups * CHUNKS)
    pieces = pl.pallas_call(
        piece_kernel,
        in_specs=[VMEM, SMEM],
        out_specs=[VMEM] * CHUNKS,
        out_shape=[jax.ShapeDtypeStruct((deep, channels), BF16)] * CHUNKS,
        compiler_params=STREAM,
        cost_estimate=cost(CHUNKS * deep * channels, 4 * CHUNKS * deep * channels),
        name="piece",
    )(head_weights, block_pattern)
    inst, pieces = lax.optimization_barrier((inst, pieces))
    far_weight = partner(error_weight)
    swapped = [[partner(piece)] for piece in pieces]
    step = 1
    while step < groups:
        swap = [(i, i ^ step) for i in range(groups)]
        swapped = [held + [lax.ppermute(x, "grp", swap) for x in held] for held in swapped]
        step *= 2
    far_eff = [swapped[chunk][number] for number in range(groups) for chunk in range(CHUNKS)]

    cut = 4

    def prep(which, name):
        return pl.pallas_call(
            functools.partial(prep_kernel, heads, capacity, which),
            grid=(cut,),
            in_specs=[whole((1, rows)), SMEM, whole((rows, width)), whole((rows, channels))],
            out_specs=pl.BlockSpec((placed // cut, wide), lambda i: (i, 0)),
            out_shape=jax.ShapeDtypeStruct((placed, wide), BF16),
            scratch_shapes=[pltpu.VMEM((8, rows), jnp.int32)],
            compiler_params=STREAM,
            cost_estimate=cost(2 * placed * rows * wide, 2 * (placed + rows) * wide),
            name=name,
        )(inst, owner_slot, latents, targets)

    far_x = in_half(prep(1, "prep_far"))
    near_send = prep(0, "prep_near")
    near_send, far_x = lax.optimization_barrier((near_send, far_x))
    near_x = in_half(near_send)

    near_back, far_back = pl.pallas_call(
        functools.partial(back_kernel, heads, capacity),
        in_specs=[VMEM, SMEM],
        out_specs=[VMEM, VMEM],
        out_shape=[jax.ShapeDtypeStruct((rows, placed), BF16)] * 2,
        compiler_params=STREAM,
        cost_estimate=cost(2 * rows * rows * 128, 4 * rows * placed),
        name="back_places",
    )(inst, owner_slot)
    effective = pl.pallas_call(
        effective_kernel,
        in_specs=[VMEM, SMEM],
        out_specs=VMEM,
        out_shape=jax.ShapeDtypeStruct((width, channels), BF16),
        compiler_params=STREAM,
        cost_estimate=cost(width * channels, 4 * width * channels),
        name="effective",
    )(head_weights, block_pattern)

    size = placed // cut
    head_out = [
        pl.BlockSpec((size, width), lambda i: (i, 0)),
        pl.BlockSpec((size, channels), lambda i: (i, 0)),
    ]
    head_shape = [
        jax.ShapeDtypeStruct((placed, width), BF16),
        jax.ShapeDtypeStruct((placed, channels), BF16),
    ]
    head_cost = cost(4 * placed * width * channels, 2 * placed * (2 * wide + width))
    row_spec = pl.BlockSpec((size, wide), lambda i: (i, 0))
    far_grad, far_res = pl.pallas_call(
        functools.partial(far_head_kernel, width, len(far_eff)),
        grid=(cut,),
        in_specs=[row_spec, whole((1, channels))] + [whole((deep, channels))] * len(far_eff),
        out_specs=head_out,
        out_shape=head_shape,
        compiler_params=STREAM,
        cost_estimate=head_cost,
        name="far_head",
    )(far_x, far_weight, *far_eff)

    tall = 256
    steps = width // (CHUNKS * tall)
    far_raw = []
    for chunk in range(CHUNKS):
        part = pl.pallas_call(
            far_raw_kernel,
            grid=(steps,),
            in_specs=[
                pl.BlockSpec((placed, tall), lambda i, chunk=chunk: (0, chunk * steps + i)),
                whole((placed, channels)),
            ],
            out_specs=pl.BlockSpec((tall, channels), lambda i: (i, 0)),
            out_shape=jax.ShapeDtypeStruct((width // CHUNKS, channels), BF16),
            compiler_params=STREAM,
            cost_estimate=cost(2 * placed * width * channels // CHUNKS, 2 * width * channels),
            name="far_raw",
        )(far_x, far_res)
        far_raw.append(partner(part))

    near_x, effective, near_back, far_back = lax.optimization_barrier(
        (near_x, effective, near_back, far_back)
    )
    near_grad, near_res = pl.pallas_call(
        functools.partial(head_kernel, width),
        grid=(cut,),
        in_specs=[row_spec, whole((width, channels)), whole((1, channels))],
        out_specs=head_out,
        out_shape=head_shape,
        compiler_params=STREAM,
        cost_estimate=head_cost,
        name="near_head",
    )(near_x, effective, error_weight)

    far_got = in_half(far_grad)
    near_grad, far_got = lax.optimization_barrier((near_grad, far_got))
    near_got = in_half(near_grad)
    latent_grad = pl.pallas_call(
        place_back_kernel,
        grid=(cut,),
        in_specs=[whole((rows, placed))] * 2
        + [pl.BlockSpec((placed, width // cut), lambda i: (0, i))] * 2,
        out_specs=pl.BlockSpec((rows, width // cut), lambda i: (0, i)),
        out_shape=jax.ShapeDtypeStruct((rows, width), BF16),
        compiler_params=STREAM,
        cost_estimate=cost(4 * rows * placed * width, 8 * placed * width),
        name="place_back",
    )(near_back, far_back, near_got, far_got)

    raw_grad, squares = [], 0.0
    for chunk in range(CHUNKS):
        part, square = pl.pallas_call(
            functools.partial(raw_kernel, chunk * steps * (tall // BLK)),
            grid=(steps,),
            in_specs=[
                pl.BlockSpec((placed, tall), lambda i, chunk=chunk: (0, chunk * steps + i)),
                whole((placed, channels)),
                pl.BlockSpec((tall, channels), lambda i: (i, 0)),
                SMEM,
            ],
            out_specs=[pl.BlockSpec((tall, channels), lambda i: (i, 0)), whole((8, 128))],
            out_shape=[
                jax.ShapeDtypeStruct((width // CHUNKS, channels), F32),
                jax.ShapeDtypeStruct((8, 128), F32),
            ],
            compiler_params=SMALL,
            cost_estimate=cost(2 * placed * width * channels // CHUNKS, 4 * width * channels),
            name="raw",
        )(near_x, near_res, far_raw[chunk], block_pattern)
        raw_grad.append(part)
        squares = squares + square
    step = 1
    while step < members:
        squares = squares + lax.ppermute(squares, "loc", [(i, i ^ step) for i in range(members)])
        step *= 2

    def raw_spec(part):
        low = part * (cut // CHUNKS)
        return pl.BlockSpec(
            (width // cut, channels), lambda i: (jnp.clip(i - low, 0, cut // CHUNKS - 1), 0)
        )

    head_grad = pl.pallas_call(
        functools.partial(scale_kernel, math.sqrt(heads * width * channels), CHUNKS),
        grid=(cut,),
        in_specs=[raw_spec(part) for part in range(CHUNKS)] + [whole((8, 128))],
        out_specs=pl.BlockSpec((1, width // cut, channels), lambda i: (0, i, 0)),
        out_shape=jax.ShapeDtypeStruct((1, width, channels), F32),
        compiler_params=SMALL,
        cost_estimate=cost(width * channels, 8 * width * channels),
        name="scale",
    )(*raw_grad, squares)
    return (latent_grad, head_grad)


def solution(mesh):
    in_specs = (
        P(("grp", "loc"), None),
        P(("grp", "loc"), None),
        P(),
        P("loc", None, None),
        P("loc", None),
        P("loc", None, None),
        P(("grp", "loc"), None),
    )
    out_specs = (P(("grp", "loc"), None), P(("grp", "loc"), None, None))
    return jax.shard_map(
        per_device, mesh=mesh, in_specs=in_specs, out_specs=out_specs, check_vma=False
    )
```

time: 263 us -> 287 us (1.091); the launches traced: 261 us -> 282 us
  Pallas kernels: 0 us -> 56.5 us
  local copies, waits for them, and re-layouts: 32.9 us -> 5.97 us
  waiting for transfers between devices: 163 us -> 183 us
  matrix products: 16.4 us -> 0 us
  other arithmetic: 10.9 us -> 0.02 us
    ppermute x0 -> x7, waiting for transfers between devices: none -> 139 us  [the longest x5 132 us: partner(): return lax.ppermute(x, 'loc', [(i, i ^ half) for i in range(members)])]
    ppermute x4, waiting for transfers between devices: 74.7 us -> 7.04 us  [per_device(): lax.ppermute(squares, 'loc', [(i, i ^ step) for i in range(members)])]
    pallas_call x0 -> x13, Pallas kernels: none -> 56.5 us  [the longest x2 10.4 us: prep(): pl.pallas_call(functools.partial(prep_kernel, heads, capacity, which), gr...]
    all_to_all x2 -> x4, waiting for transfers between devices: 88.1 us -> 37 us  [in_half(): lax.all_to_all(x, 'loc', split_axis=0, concat_axis=0, tiled=True, axis_in...]
    dot_general x3 -> x0, matrix products: 16.4 us -> none  [the longest x1 6.15 us: per_device(): jnp.dot(arrived, effective[0], preferred_element_type=jnp.float32)]
    broadcast_in_dim x5 -> x0, local copies, waits for them, and re-layouts: 11.2 us -> none  [the longest x4 10.6 us: per_device(): block_mask = jnp.repeat(jnp.repeat(block_pattern, BLK, 1), BLK, 2)]
    scatter x2 -> x0, local copies, waits for them, and re-layouts: 10.5 us -> none  [the longest x1 7.3 us: per_device(): jnp.zeros((instruments * capacity, width), latents.dtype).at[placed]]
    ppermute x0 -> x7, starting transfers between devices: none -> 10.2 us  [the longest x5 7.76 us: partner(): return lax.ppermute(x, 'loc', [(i, i ^ half) for i in range(members)])]
  transfers between devices with their start and end apart: 6 -> 15, of which waited for: 5 -> 12; matrix products, arithmetic and copies ran while one was open for 9% -> 0% of each run, Pallas kernels for 0% -> 15%
where the time goes in v4:
time: 287 us; the launch traced here: 282 us
  waiting for transfers between devices  183 us (64%)
  Pallas kernels  56.5 us (20%)
  starting transfers between devices  36 us (13%)
  local copies, waits for them, and re-layouts  5.97 us (2%)
    ppermute x5, waiting for transfers between devices, partner(): return lax.ppermute(x, 'loc', [(i, i ^ half) for i in range(members)])  132 us
    all_to_all x4, waiting for transfers between devices, in_half(): lax.all_to_all(x, 'loc', split_axis=0, concat_axis=0, tiled=True, axis_in...  37 us
    all_to_all x4, starting transfers between devices, in_half(): lax.all_to_all(x, 'loc', split_axis=0, concat_axis=0, tiled=True, axis_in...  22.7 us
    pallas_call x2, Pallas kernels, prep(): pl.pallas_call(functools.partial(prep_kernel, heads, capacity, which), gr...  10.4 us
    pallas_call x2, Pallas kernels, per_device(): pl.pallas_call(far_raw_kernel, grid=(steps,), in_specs=[pl.BlockSpec((pla...  8.47 us
    ppermute x5, starting transfers between devices, partner(): return lax.ppermute(x, 'loc', [(i, i ^ half) for i in range(members)])  7.76 us
    pallas_call x1, Pallas kernels, per_device(): pl.pallas_call(functools.partial(head_kernel, width), grid=(cut,), in_spe...  7.49 us
    pallas_call x1, Pallas kernels, per_device(): pl.pallas_call(functools.partial(far_head_kernel, width, len(far_eff)), g...  7.37 us
  transfers between devices with their start and end apart: 15, of which 12 were waited for; matrix products, arithmetic and copies ran while one was open for 0% of the time, Pallas kernels for 15%

profile of v4, /device:TPU:1, one launch (start us, length us, event | category | flops | bytes accessed | tf_op | source)
XLA Modules:
  0.0 282.0 jit_solution(7117439489480746942)
XLA Ops:
  2.0 2.7 piece.1
  4.7 5.2 %prep_far.1 = bf16[512,2560]{1,0:T(8,128)(2,1)} custom-call(s32[1,512]{1,0:T(1,128)} %bitcast.19, s32[16]{0:T(128)} %owner_ref.5, bf16[512,2048]{1,0:T(8,128)(2,1)} %x_ref.3, bf16[512,512]{1,0:T(8,128)(2,1)} %t_ref.3), custom_call_target="tpu_custom_call" | custom-call | flops 1342177280 | bytes 5242880 | tf_op jit(solution)/shard_map/prep_far/pallas_call | solution.py:216
  9.9 5.3 %all-to-all-start = ((bf16[8,64,2560]{2,1,0:T(8,128)(2,1)}), bf16[8,64,2560]{2,1,0:T(8,128)(2,1)S(1)}, u32[]{:S(2)}, u32[]{:S(2)}) async-start(bf16[8,64,2560]{2,1,0:T(8,128)(2,1)} %bitcast.16), calls=%async_computation | async-start | bytes 5242880 | tf_op jit(solution)/shard_map/all_to_all | solution.py:189
  15.2 5.2 %prep_near.1 = bf16[512,2560]{1,0:T(8,128)(2,1)} custom-call(s32[1,512]{1,0:T(1,128)} %bitcast.20, s32[16]{0:T(128)} %owner_ref.5, bf16[512,2048]{1,0:T(8,128)(2,1)} %x_ref.3, bf16[512,512]{1,0:T(8,128)(2,1)} %t_ref.3), custom_call_target="tpu_custom_call" | custom-call | flops 1342177280 | bytes 5242880 | tf_op jit(solution)/shard_map/prep_near/pallas_call | solution.py:216
  20.3 25.3 %all-to-all-done = bf16[8,64,2560]{2,1,0:T(8,128)(2,1)S(1)} async-done(((bf16[8,64,2560]{2,1,0:T(8,128)(2,1)}), bf16[8,64,2560]{2,1,0:T(8,128)(2,1)S(1)}, u32[]{:S(2)}, u32[]{:S(2)}) %all-to-all-start) | async-done | bytes 2621472 | tf_op jit(solution)/shard_map/all_to_all | solution.py:189
  45.6 1.5 copy-done.4
  47.1 4.4 %all-to-all-start.1 = ((bf16[8,64,2560]{2,1,0:T(8,128)(2,1)}), bf16[8,64,2560]{2,1,0:T(8,128)(2,1)S(1)}, u32[]{:S(2)}, u32[]{:S(2)}) async-start(bf16[8,64,2560]{2,1,0:T(8,128)(2,1)} %bitcast.15), calls=%async_computation.1 | async-start | bytes 5242880 | tf_op jit(solution)/shard_map/all_to_all | solution.py:189
  51.5 2.3 collective-permute-start.1
  53.9 37.5 %collective-permute-done.1.refs_0_ = bf16[512,512]{1,0:T(8,128)(2,1)S(1)} collective-permute-done((bf16[512,512]{1,0:T(8,128)(2,1)}, bf16[512,512]{1,0:T(8,128)(2,1)S(1)}, u32[]{:S(2)}, u32[]{:S(2)}) %collective-permute-start.1) | collective-permute-done | bytes 524320 | tf_op jit(solution)/shard_map/ppermute | solution.py:186
  92.7 9.9 %collective-permute-done.2.refs_1_ = bf16[512,512]{1,0:T(8,128)(2,1)S(1)} collective-permute-done((bf16[512,512]{1,0:T(8,128)(2,1)S(1)}, bf16[512,512]{1,0:T(8,128)(2,1)S(1)}, u32[]{:S(2)}, u32[]{:S(2)}) %collective-permute-start.2) | collective-permute-done | bytes 524320 | tf_op jit(solution)/shard_map/ppermute | solution.py:186
  103.8 3.1 %collective-permute-start = (f32[1,512]{1,0:T(1,128)S(1)}, f32[1,512]{1,0:T(1,128)S(1)}, u32[]{:S(2)}, u32[]{:S(2)}) collective-permute-start(f32[1,512]{1,0:T(1,128)S(1)} %copy-done.10), channel_id=1, source_target_pairs={{0,8},{1,9},{2,10},{3,11},{4,12},{5,13},{6,14},{7,15},{8,0},{9,1},... | collective-permute-start | bytes 6152 | tf_op jit(solution)/shard_map/ppermute | solution.py:186
  108.7 7.0 %collective-permute-done.4.refs_3_ = bf16[512,512]{1,0:T(8,128)(2,1)S(1)} collective-permute-done((bf16[512,512]{1,0:T(8,128)(2,1)S(1)}, bf16[512,512]{1,0:T(8,128)(2,1)S(1)}, u32[]{:S(2)}, u32[]{:S(2)}) %collective-permute-start.4) | collective-permute-done | bytes 524320 | tf_op jit(solution)/shard_map/ppermute | solution.py:209
  116.5 7.4 %far_head.1 = (bf16[512,2048]{1,0:T(8,128)(2,1)}, bf16[512,512]{1,0:T(8,128)(2,1)}) custom-call(bf16[512,2560]{1,0:T(8,128)(2,1)} %bitcast.12, f32[1,512]{1,0:T(1,128)} %copy-done.11, bf16[512,512]{1,0:T(8,128)(2,1)} %copy-done.5, bf16[512,512]{1,0:T(8,128)(2,1)} %copy-done.7, bf16[512,512]{1,0:T(8,128)(2,1)} %copy-done.8, bf16[512,512]{1,0:T(8,128)(2,1)} %copy-done.9), custom_call_target="tpu_custom_call" | custom-call | flops 2147483648 | bytes 7340032 | tf_op jit(solution)/shard_map/far_head/pallas_call | solution.py:263
  123.9 1.5 copy-done
  125.4 7.9 %all-to-all-start.2 = ((bf16[8,64,2048]{2,1,0:T(8,128)(2,1)}), bf16[8,64,2048]{2,1,0:T(8,128)(2,1)}, u32[]{:S(2)}, u32[]{:S(2)}) async-start(bf16[8,64,2048]{2,1,0:T(8,128)(2,1)} %bitcast.18), calls=%async_computation.2 | async-start | bytes 4194304 | tf_op jit(solution)/shard_map/all_to_all | solution.py:189
  133.3 3.3 %effective.1.eff_ref = bf16[2048,512]{1,0:T(8,128)(2,1)} custom-call(bf16[1,2048,512]{2,1,0:T(8,128)(2,1)} %w_ref.3, s32[1,16,4]{2,1,0:T(8,128)} %copy.9.pattern_ref), custom_call_target="tpu_custom_call" | custom-call | flops 1048576 | bytes 4194304 | tf_op jit(solution)/shard_map/effective/pallas_call | solution.py:242
  136.6 2.4 back_places.1
  139.0 7.5 %near_head.1 = (bf16[512,2048]{1,0:T(8,128)(2,1)}, bf16[512,512]{1,0:T(8,128)(2,1)}) custom-call(bf16[512,2560]{1,0:T(8,128)(2,1)} %bitcast.9, bf16[2048,512]{1,0:T(8,128)(2,1)} %effective.1.eff_ref, f32[1,512]{1,0:T(1,128)} %weight_ref.1), custom_call_target="tpu_custom_call" | custom-call | flops 2147483648 | bytes 7340032 | tf_op jit(solution)/shard_map/near_head/pallas_call | solution.py:296
  146.5 11.7 %all-to-all-done.2 = bf16[8,64,2048]{2,1,0:T(8,128)(2,1)} async-done(((bf16[8,64,2048]{2,1,0:T(8,128)(2,1)}), bf16[8,64,2048]{2,1,0:T(8,128)(2,1)}, u32[]{:S(2)}, u32[]{:S(2)}) %all-to-all-start.2) | async-done | bytes 2097184 | tf_op jit(solution)/shard_map/all_to_all | solution.py:189
  158.2 5.1 %all-to-all-start.3 = ((bf16[8,64,2048]{2,1,0:T(8,128)(2,1)}), bf16[8,64,2048]{2,1,0:T(8,128)(2,1)}, u32[]{:S(2)}, u32[]{:S(2)}) async-start(bf16[8,64,2048]{2,1,0:T(8,128)(2,1)} %bitcast.17), calls=%async_computation.3 | async-start | bytes 4194304 | tf_op jit(solution)/shard_map/all_to_all | solution.py:189
  163.3 4.2 %far_raw.3 = bf16[1024,512]{1,0:T(8,128)(2,1)} custom-call(bf16[512,2560]{1,0:T(8,128)(2,1)} %bitcast.13, bf16[512,512]{1,0:T(8,128)(2,1)} %get-tuple-element.43.res_ref), custom_call_target="tpu_custom_call" | custom-call | flops 536870912 | bytes 2097152 | tf_op jit(solution)/shard_map/far_raw/pallas_call | solution.py:278
  168.2 4.3 %far_raw.2 = bf16[1024,512]{1,0:T(8,128)(2,1)} custom-call(bf16[512,2560]{1,0:T(8,128)(2,1)} %bitcast.14, bf16[512,512]{1,0:T(8,128)(2,1)} %get-tuple-element.43.res_ref), custom_call_target="tpu_custom_call" | custom-call | flops 536870912 | bytes 2097152 | tf_op jit(solution)/shard_map/far_raw/pallas_call | solution.py:278
  172.5 1.5 collective-permute-start.5
  174.0 64.3 %collective-permute-done.6.far_ref = bf16[1024,512]{1,0:T(8,128)(2,1)} collective-permute-done((bf16[1024,512]{1,0:T(8,128)(2,1)}, bf16[1024,512]{1,0:T(8,128)(2,1)}, u32[]{:S(2)}, u32[]{:S(2)}) %collective-permute-start.6) | collective-permute-done | bytes 1048608 | tf_op jit(solution)/shard_map/ppermute | solution.py:186
  238.3 3.3 %raw.3 = (f32[1024,512]{1,0:T(8,128)S(1)}, f32[8,128]{1,0:T(8,128)S(1)}) custom-call(bf16[512,2560]{1,0:T(8,128)(2,1)S(1)} %bitcast.10, bf16[512,512]{1,0:T(8,128)(2,1)S(1)} %copy-done.2, bf16[1024,512]{1,0:T(8,128)(2,1)} %collective-permute-done.6.far_ref, s32[1,16,4]{2,1,0:T(8,128)S(1)} %copy-done.3), custom_call_target="tpu_custom_call" | custom-call | flops 536870912 | bytes 4194304 | tf_op jit(solution)/shard_map/raw/pallas_call | solution.py:324
  241.6 19.1 %collective-permute-done.5.far_ref = bf16[1024,512]{1,0:T(8,128)(2,1)S(1)} collective-permute-done((bf16[1024,512]{1,0:T(8,128)(2,1)}, bf16[1024,512]{1,0:T(8,128)(2,1)S(1)}, u32[]{:S(2)}, u32[]{:S(2)}) %collective-permute-start.5) | collective-permute-done | bytes 1048608 | tf_op jit(solution)/shard_map/ppermute | solution.py:186
  260.7 2.4 raw.2
  265.0 1.4 collective-permute-start.8
  267.5 2.5 collective-permute-done.9
  270.6 2.7 collective-permute-done.10
  273.3 2.7 scale.1
  276.0 6.0 %place_back.1 = bf16[512,2048]{1,0:T(8,128)(2,1)} custom-call(bf16[512,512]{1,0:T(8,128)(2,1)} %get-tuple-element.31.near_ref, bf16[512,512]{1,0:T(8,128)(2,1)} %get-tuple-element.32.far_ref, bf16[512,2048]{1,0:T(8,128)(2,1)} %bitcast.8.near_got_ref, bf16[512,2048]{1,0:T(8,128)(2,1)} %bitcast.6.far_got_ref), custom_call_target="tpu_custom_call" | custom-call | flops 2147483648 | bytes 8388608 | tf_op jit(solution)/shard_map/place_back/pallas_call | solution.py:310
  (41 shorter events, 10.9 us)
Async XLA Ops:
  9.9 35.8 %all-to-all-start = ((bf16[8,64,2560]{2,1,0:T(8,128)(2,1)}), bf16[8,64,2560]{2,1,0:T(8,128)(2,1)S(1)}, u32[]{:S(2)}, u32[]{:S(2)}) async-start(bf16[8,64,2560]{2,1,0:T(8,128)(2,1)} %bitcast.16), calls=%async_computation | async-start | bytes 5242880 | tf_op jit(solution)/shard_map/all_to_all | solution.py:189
  45.6 1.5 copy-start.4
  45.6 8.2 %copy-start.6 = (bf16[512,512]{1,0:T(8,128)(2,1)S(1)}, bf16[512,512]{1,0:T(8,128)(2,1)}, u32[]{:S(2)}) copy-start(bf16[512,512]{1,0:T(8,128)(2,1)} %get-tuple-element.38) | copy-start | bytes 1572868
  45.6 58.2 %copy-start.10 = (f32[1,512]{1,0:T(1,128)S(1)}, f32[1,512]{1,0:T(1,128)}, u32[]{:S(2)}) copy-start(f32[1,512]{1,0:T(1,128)} %weight_ref.1) | copy-start | bytes 6148
  47.1 76.7 %all-to-all-start.1 = ((bf16[8,64,2560]{2,1,0:T(8,128)(2,1)}), bf16[8,64,2560]{2,1,0:T(8,128)(2,1)S(1)}, u32[]{:S(2)}, u32[]{:S(2)}) async-start(bf16[8,64,2560]{2,1,0:T(8,128)(2,1)} %bitcast.15), calls=%async_computation.1 | async-start | bytes 5242880 | tf_op jit(solution)/shard_map/all_to_all | solution.py:189
  51.5 40.0 %collective-permute-start.1 = (bf16[512,512]{1,0:T(8,128)(2,1)}, bf16[512,512]{1,0:T(8,128)(2,1)S(1)}, u32[]{:S(2)}, u32[]{:S(2)}) collective-permute-start(bf16[512,512]{1,0:T(8,128)(2,1)} %get-tuple-element.37), channel_id=1, source_target_pairs={{0,8},{1,9},{2,10},{3,11},{4,12},{5,13},{6,14},{7,15},{8,0},{9,1},... | collective-permute-start | bytes 1572872 | tf_op jit(solution)/shard_map/ppermute | solution.py:186
  53.8 48.8 %collective-permute-start.2 = (bf16[512,512]{1,0:T(8,128)(2,1)S(1)}, bf16[512,512]{1,0:T(8,128)(2,1)S(1)}, u32[]{:S(2)}, u32[]{:S(2)}) collective-permute-start(bf16[512,512]{1,0:T(8,128)(2,1)S(1)} %copy-done.6), channel_id=1, source_target_pairs={{0,8},{1,9},{2,10},{3,11},{4,12},{5,13},{6,14},{7,15},{8,0},{9,1},... | collective-permute-start | bytes 1572872 | tf_op jit(solution)/shard_map/ppermute | solution.py:186
  91.5 24.2 %copy-start.5 = (bf16[512,512]{1,0:T(8,128)(2,1)}, bf16[512,512]{1,0:T(8,128)(2,1)S(1)}, u32[]{:S(2)}) copy-start(bf16[512,512]{1,0:T(8,128)(2,1)S(1)} %collective-permute-done.1.refs_0_) | copy-start | bytes 1572868
  91.5 16.4 %collective-permute-start.3 = (bf16[512,512]{1,0:T(8,128)(2,1)S(1)}, bf16[512,512]{1,0:T(8,128)(2,1)S(1)}, u32[]{:S(2)}, u32[]{:S(2)}) collective-permute-start(bf16[512,512]{1,0:T(8,128)(2,1)S(1)} %collective-permute-done.1.refs_0_), channel_id=1, source_target_pairs={{0,16},{16,0},{1,17},{17,1},{2,18},{18,2},{3,19},{19,3},{4,20},{20... | collective-permute-start | bytes 1572872 | tf_op jit(solution)/shard_map/ppermute | solution.py:209
  102.6 5.3 %copy-start.7 = (bf16[512,512]{1,0:T(8,128)(2,1)}, bf16[512,512]{1,0:T(8,128)(2,1)S(1)}, u32[]{:S(2)}) copy-start(bf16[512,512]{1,0:T(8,128)(2,1)S(1)} %collective-permute-done.2.refs_1_) | copy-start | bytes 1572868
  102.6 13.1 %collective-permute-start.4 = (bf16[512,512]{1,0:T(8,128)(2,1)S(1)}, bf16[512,512]{1,0:T(8,128)(2,1)S(1)}, u32[]{:S(2)}, u32[]{:S(2)}) collective-permute-start(bf16[512,512]{1,0:T(8,128)(2,1)S(1)} %collective-permute-done.2.refs_1_), channel_id=1, source_target_pairs={{0,16},{16,0},{1,17},{17,1},{2,18},{18,2},{3,19},{19,3},{4,20},{20... | collective-permute-start | bytes 1572872 | tf_op jit(solution)/shard_map/ppermute | solution.py:209
  103.8 4.1 %collective-permute-start = (f32[1,512]{1,0:T(1,128)S(1)}, f32[1,512]{1,0:T(1,128)S(1)}, u32[]{:S(2)}, u32[]{:S(2)}) collective-permute-start(f32[1,512]{1,0:T(1,128)S(1)} %copy-done.10), channel_id=1, source_target_pairs={{0,8},{1,9},{2,10},{3,11},{4,12},{5,13},{6,14},{7,15},{8,0},{9,1},... | collective-permute-start | bytes 6152 | tf_op jit(solution)/shard_map/ppermute | solution.py:186
  107.9 7.8 %copy-start.11 = (f32[1,512]{1,0:T(1,128)}, f32[1,512]{1,0:T(1,128)S(1)}, u32[]{:S(2)}) copy-start(f32[1,512]{1,0:T(1,128)S(1)} %collective-permute-done.weight_ref) | copy-start | bytes 6148
  107.9 0.8 copy-start.8
  115.7 0.8 copy-start.9
  123.9 1.5 copy-start
  125.4 32.8 %all-to-all-start.2 = ((bf16[8,64,2048]{2,1,0:T(8,128)(2,1)}), bf16[8,64,2048]{2,1,0:T(8,128)(2,1)}, u32[]{:S(2)}, u32[]{:S(2)}) async-start(bf16[8,64,2048]{2,1,0:T(8,128)(2,1)} %bitcast.18), calls=%async_computation.2 | async-start | bytes 4194304 | tf_op jit(solution)/shard_map/all_to_all | solution.py:189
  158.2 117.8 %all-to-all-start.3 = ((bf16[8,64,2048]{2,1,0:T(8,128)(2,1)}), bf16[8,64,2048]{2,1,0:T(8,128)(2,1)}, u32[]{:S(2)}, u32[]{:S(2)}) async-start(bf16[8,64,2048]{2,1,0:T(8,128)(2,1)} %bitcast.17), calls=%async_computation.3 | async-start | bytes 4194304 | tf_op jit(solution)/shard_map/all_to_all | solution.py:189
  167.4 70.9 %copy-start.1 = (bf16[8,64,2560]{2,1,0:T(8,128)(2,1)S(1)}, bf16[8,64,2560]{2,1,0:T(8,128)(2,1)}, u32[]{:S(2)}) copy-start(bf16[8,64,2560]{2,1,0:T(8,128)(2,1)} %copy-done) | copy-start | bytes 7864324
  167.4 70.9 %copy-start.2 = (bf16[512,512]{1,0:T(8,128)(2,1)S(1)}, bf16[512,512]{1,0:T(8,128)(2,1)}, u32[]{:S(2)}) copy-start(bf16[512,512]{1,0:T(8,128)(2,1)} %get-tuple-element.42.res_ref) | copy-start | bytes 1572868
  167.4 70.9 %copy-start.3 = (s32[1,16,4]{2,1,0:T(8,128)S(1)}, s32[1,16,4]{2,1,0:T(8,128)}, u32[]{:S(2)}) copy-start(s32[1,16,4]{2,1,0:T(8,128)} %copy.9.pattern_ref) | copy-start | bytes 772
  167.5 70.9 %collective-permute-start.6 = (bf16[1024,512]{1,0:T(8,128)(2,1)}, bf16[1024,512]{1,0:T(8,128)(2,1)}, u32[]{:S(2)}, u32[]{:S(2)}) collective-permute-start(bf16[1024,512]{1,0:T(8,128)(2,1)} %far_raw.3), channel_id=1, source_target_pairs={{0,8},{1,9},{2,10},{3,11},{4,12},{5,13},{6,14},{7,15},{8,0},{9,1},... | collective-permute-start | bytes 3145736 | tf_op jit(solution)/shard_map/ppermute | solution.py:186
  172.5 88.2 %collective-permute-start.5 = (bf16[1024,512]{1,0:T(8,128)(2,1)}, bf16[1024,512]{1,0:T(8,128)(2,1)S(1)}, u32[]{:S(2)}, u32[]{:S(2)}) collective-permute-start(bf16[1024,512]{1,0:T(8,128)(2,1)} %far_raw.2), channel_id=1, source_target_pairs={{0,8},{1,9},{2,10},{3,11},{4,12},{5,13},{6,14},{7,15},{8,0},{9,1},... | collective-permute-start | bytes 3145736 | tf_op jit(solution)/shard_map/ppermute | solution.py:186
  263.2 1.8 collective-permute-start.7
  265.0 2.5 collective-permute-start.8
  267.5 2.5 collective-permute-start.9
  269.9 3.4 %collective-permute-start.10 = (f32[8,128]{1,0:T(8,128)S(1)}, f32[8,128]{1,0:T(8,128)S(1)}, u32[]{:S(2)}, u32[]{:S(2)}) collective-permute-start(f32[8,128]{1,0:T(8,128)S(1)} %add.18), channel_id=1, source_target_pairs={{0,8},{1,9},{2,10},{3,11},{4,12},{5,13},{6,14},{7,15},{8,0},{9,1},... | collective-permute-start | bytes 12296 | tf_op jit(solution)/shard_map/ppermute | solution.py:346

commit v5 on v4

--- a/solution.py
+++ b/solution.py
@@ -227,7 +227,8 @@
 
     far_x = in_half(prep(1, "prep_far"))
     near_send = prep(0, "prep_near")
-    near_send, far_x = lax.optimization_barrier((near_send, far_x))
+    crossed = [held[0] for held in swapped]
+    near_send, far_x, crossed = lax.optimization_barrier((near_send, far_x, crossed))
     near_x = in_half(near_send)
 
     near_back, far_back = pl.pallas_call(
@@ -288,7 +289,10 @@
             cost_estimate=cost(2 * placed * width * channels // CHUNKS, 2 * width * channels),
             name="far_raw",
         )(far_x, far_res)
-        far_raw.append(partner(part))
+        far_raw.append(part)
+    sent = far_raw
+    far_raw = [partner(part) for part in sent]
+    far_grad, sent = lax.optimization_barrier((far_grad, sent))
 
     near_x, effective, near_back, far_back = lax.optimization_barrier(
         (near_x, effective, near_back, far_back)
@@ -341,6 +345,7 @@
         )(near_x, near_res, far_raw[chunk], block_pattern)
         raw_grad.append(part)
         squares = squares + square
+    latent_grad, squares = lax.optimization_barrier((latent_grad, squares))
     step = 1
     while step < members:
         squares = squares + lax.ppermute(squares, "loc", [(i, i ^ step) for i in range(members)])

time: 287 us -> 280 us (0.976)
  waiting for transfers between devices: 183 us -> 176 us
  local copies, waits for them, and re-layouts: 5.97 us -> 9.41 us
    ppermute x5, waiting for transfers between devices: 132 us -> 158 us  [partner(): return lax.ppermute(x, 'loc', [(i, i ^ half) for i in range(members)])]
    all_to_all x4, waiting for transfers between devices: 37 us -> 13.4 us  [in_half(): lax.all_to_all(x, 'loc', split_axis=0, concat_axis=0, tiled=True, axis_in...]
    ppermute x2, waiting for transfers between devices: 6.96 us -> 0.01 us  [per_device(): lax.ppermute(x, 'grp', swap)]
    unnamed x25 -> x27, local copies, waits for them, and re-layouts: 5.97 us -> 9.41 us
  transfers between devices with their start and end apart: 15 -> 15, of which waited for: 12 -> 11; matrix products, arithmetic and copies ran while one was open for 0% -> 0% of each run, Pallas kernels for 15% -> 14%
where the time goes in v5:
time: 280 us; the launch traced here: 275 us
  waiting for transfers between devices  176 us (63%)
  Pallas kernels  55.6 us (20%)
  starting transfers between devices  33.5 us (12%)
  local copies, waits for them, and re-layouts  9.41 us (3%)
    ppermute x5, waiting for transfers between devices, partner(): return lax.ppermute(x, 'loc', [(i, i ^ half) for i in range(members)])  158 us
    all_to_all x4, starting transfers between devices, in_half(): lax.all_to_all(x, 'loc', split_axis=0, concat_axis=0, tiled=True, axis_in...  21.7 us
    all_to_all x4, waiting for transfers between devices, in_half(): lax.all_to_all(x, 'loc', split_axis=0, concat_axis=0, tiled=True, axis_in...  13.4 us
    pallas_call x2, Pallas kernels, prep(): pl.pallas_call(functools.partial(prep_kernel, heads, capacity, which), gr...  10.3 us
    unnamed x27, local copies, waits for them, and re-layouts  9.41 us
    pallas_call x2, Pallas kernels, per_device(): pl.pallas_call(far_raw_kernel, grid=(steps,), in_specs=[pl.BlockSpec((pla...  8.34 us
    pallas_call x1, Pallas kernels, per_device(): pl.pallas_call(functools.partial(head_kernel, width), grid=(cut,), in_spe...  7.46 us
    pallas_call x1, Pallas kernels, per_device(): pl.pallas_call(functools.partial(far_head_kernel, width, len(far_eff)), g...  7.37 us
  transfers between devices with their start and end apart: 15, of which 11 were waited for; matrix products, arithmetic and copies ran while one was open for 0% of the time, Pallas kernels for 14%

profile of v5, /device:TPU:1, one launch (start us, length us, event | category | flops | bytes accessed | tf_op | source)
XLA Modules:
  0.0 275.3 jit_solution(2549681334703692218)
XLA Ops:
  2.0 2.7 piece.1
  4.7 5.2 %prep_far.1 = bf16[512,2560]{1,0:T(8,128)(2,1)} custom-call(s32[1,512]{1,0:T(1,128)} %bitcast.19, s32[16]{0:T(128)} %owner_ref.5, bf16[512,2048]{1,0:T(8,128)(2,1)} %x_ref.3, bf16[512,512]{1,0:T(8,128)(2,1)} %t_ref.3), custom_call_target="tpu_custom_call" | custom-call | flops 1342177280 | bytes 5242880 | tf_op jit(solution)/shard_map/prep_far/pallas_call | solution.py:216
  9.9 5.3 %all-to-all-start = ((bf16[8,64,2560]{2,1,0:T(8,128)(2,1)}), bf16[8,64,2560]{2,1,0:T(8,128)(2,1)S(1)}, u32[]{:S(2)}, u32[]{:S(2)}) async-start(bf16[8,64,2560]{2,1,0:T(8,128)(2,1)} %bitcast.16), calls=%async_computation | async-start | bytes 5242880 | tf_op jit(solution)/shard_map/all_to_all | solution.py:189
  15.2 2.3 collective-permute-start
  17.5 5.2 %prep_near.1 = bf16[512,2560]{1,0:T(8,128)(2,1)} custom-call(s32[1,512]{1,0:T(1,128)} %bitcast.20, s32[16]{0:T(128)} %owner_ref.5, bf16[512,2048]{1,0:T(8,128)(2,1)} %x_ref.3, bf16[512,512]{1,0:T(8,128)(2,1)} %t_ref.3), custom_call_target="tpu_custom_call" | custom-call | flops 1342177280 | bytes 5242880 | tf_op jit(solution)/shard_map/prep_near/pallas_call | solution.py:216
  22.7 32.5 %collective-permute-done.refs_0_ = bf16[512,512]{1,0:T(8,128)(2,1)S(1)} collective-permute-done((bf16[512,512]{1,0:T(8,128)(2,1)}, bf16[512,512]{1,0:T(8,128)(2,1)S(1)}, u32[]{:S(2)}, u32[]{:S(2)}) %collective-permute-start) | collective-permute-done | bytes 524320 | tf_op jit(solution)/shard_map/ppermute | solution.py:186
  55.2 11.2 %collective-permute-done.1.refs_1_ = bf16[512,512]{1,0:T(8,128)(2,1)} collective-permute-done((bf16[512,512]{1,0:T(8,128)(2,1)}, bf16[512,512]{1,0:T(8,128)(2,1)}, u32[]{:S(2)}, u32[]{:S(2)}) %collective-permute-start.1) | collective-permute-done | bytes 524320 | tf_op jit(solution)/shard_map/ppermute | solution.py:186
  66.4 1.7 all-to-all-done
  68.1 1.5 copy-done.8
  69.6 5.7 %all-to-all-start.1 = ((bf16[8,64,2560]{2,1,0:T(8,128)(2,1)}), bf16[8,64,2560]{2,1,0:T(8,128)(2,1)S(1)}, u32[]{:S(2)}, u32[]{:S(2)}) async-start(bf16[8,64,2560]{2,1,0:T(8,128)(2,1)} %bitcast.15), calls=%async_computation.1 | async-start | bytes 5242880 | tf_op jit(solution)/shard_map/all_to_all | solution.py:189
  77.0 27.1 %collective-permute-done.2.weight_ref = f32[1,512]{1,0:T(1,128)S(1)} collective-permute-done((f32[1,512]{1,0:T(1,128)S(1)}, f32[1,512]{1,0:T(1,128)S(1)}, u32[]{:S(2)}, u32[]{:S(2)}) %collective-permute-start.2) | collective-permute-done | bytes 2080 | tf_op jit(solution)/shard_map/ppermute | solution.py:186
  104.9 7.4 %far_head.1 = (bf16[512,2048]{1,0:T(8,128)(2,1)}, bf16[512,512]{1,0:T(8,128)(2,1)}) custom-call(bf16[512,2560]{1,0:T(8,128)(2,1)} %bitcast.12, f32[1,512]{1,0:T(1,128)} %copy-done.12, bf16[512,512]{1,0:T(8,128)(2,1)} %copy-done.9, bf16[512,512]{1,0:T(8,128)(2,1)} %collective-permute-done.1.refs_1_, bf16[512,512]{1,0:T(8,128)(2,1)} %copy-done.10, ...), custom_call_target="tpu_custom_call" | custom-call | flops 2147483648 | bytes 7340032 | tf_op jit(solution)/shard_map/far_head/pallas_call | solution.py:264
  112.3 4.2 %far_raw.3 = bf16[1024,512]{1,0:T(8,128)(2,1)} custom-call(bf16[512,2560]{1,0:T(8,128)(2,1)} %bitcast.13, bf16[512,512]{1,0:T(8,128)(2,1)} %get-tuple-element.43.res_ref), custom_call_target="tpu_custom_call" | custom-call | flops 536870912 | bytes 2097152 | tf_op jit(solution)/shard_map/far_raw/pallas_call | solution.py:279
  116.5 4.1 %far_raw.2 = bf16[1024,512]{1,0:T(8,128)(2,1)} custom-call(bf16[512,2560]{1,0:T(8,128)(2,1)} %bitcast.14, bf16[512,512]{1,0:T(8,128)(2,1)} %get-tuple-element.43.res_ref), custom_call_target="tpu_custom_call" | custom-call | flops 536870912 | bytes 2097152 | tf_op jit(solution)/shard_map/far_raw/pallas_call | solution.py:279
  120.6 1.5 copy-done
  122.1 5.2 %all-to-all-start.2 = ((bf16[8,64,2048]{2,1,0:T(8,128)(2,1)}), bf16[8,64,2048]{2,1,0:T(8,128)(2,1)}, u32[]{:S(2)}, u32[]{:S(2)}) async-start(bf16[8,64,2048]{2,1,0:T(8,128)(2,1)} %bitcast.18), calls=%async_computation.2 | async-start | bytes 4194304 | tf_op jit(solution)/shard_map/all_to_all | solution.py:189
  127.3 3.3 %effective.1.eff_ref = bf16[2048,512]{1,0:T(8,128)(2,1)} custom-call(bf16[1,2048,512]{2,1,0:T(8,128)(2,1)} %w_ref.3, s32[1,16,4]{2,1,0:T(8,128)} %copy.9.pattern_ref), custom_call_target="tpu_custom_call" | custom-call | flops 1048576 | bytes 4194304 | tf_op jit(solution)/shard_map/effective/pallas_call | solution.py:243
  130.7 2.4 back_places.1
  133.0 7.5 %near_head.1 = (bf16[512,2048]{1,0:T(8,128)(2,1)}, bf16[512,512]{1,0:T(8,128)(2,1)}) custom-call(bf16[512,2560]{1,0:T(8,128)(2,1)} %bitcast.9, bf16[2048,512]{1,0:T(8,128)(2,1)} %effective.1.eff_ref, f32[1,512]{1,0:T(1,128)} %weight_ref.1), custom_call_target="tpu_custom_call" | custom-call | flops 2147483648 | bytes 7340032 | tf_op jit(solution)/shard_map/near_head/pallas_call | solution.py:300
  140.5 11.7 %all-to-all-done.2 = bf16[8,64,2048]{2,1,0:T(8,128)(2,1)} async-done(((bf16[8,64,2048]{2,1,0:T(8,128)(2,1)}), bf16[8,64,2048]{2,1,0:T(8,128)(2,1)}, u32[]{:S(2)}, u32[]{:S(2)}) %all-to-all-start.2) | async-done | bytes 2097184 | tf_op jit(solution)/shard_map/all_to_all | solution.py:189
  152.2 5.4 %all-to-all-start.3 = ((bf16[8,64,2048]{2,1,0:T(8,128)(2,1)}), bf16[8,64,2048]{2,1,0:T(8,128)(2,1)}, u32[]{:S(2)}, u32[]{:S(2)}) async-start(bf16[8,64,2048]{2,1,0:T(8,128)(2,1)} %bitcast.17), calls=%async_computation.3 | async-start | bytes 4194304 | tf_op jit(solution)/shard_map/all_to_all | solution.py:189
  157.6 2.6 collective-permute-start.6
  160.3 43.0 %collective-permute-done.6.far_ref = bf16[1024,512]{1,0:T(8,128)(2,1)S(1)} collective-permute-done((bf16[1024,512]{1,0:T(8,128)(2,1)}, bf16[1024,512]{1,0:T(8,128)(2,1)S(1)}, u32[]{:S(2)}, u32[]{:S(2)}) %collective-permute-start.6) | collective-permute-done | bytes 1048608 | tf_op jit(solution)/shard_map/ppermute | solution.py:186
  203.3 2.4 raw.3
  207.1 44.3 %collective-permute-done.5.far_ref = bf16[1024,512]{1,0:T(8,128)(2,1)S(1)} collective-permute-done((bf16[1024,512]{1,0:T(8,128)(2,1)}, bf16[1024,512]{1,0:T(8,128)(2,1)S(1)}, u32[]{:S(2)}, u32[]{:S(2)}) %collective-permute-start.5) | collective-permute-done | bytes 1048608 | tf_op jit(solution)/shard_map/ppermute | solution.py:186
  251.4 2.4 raw.2
  255.1 6.1 %place_back.1 = bf16[512,2048]{1,0:T(8,128)(2,1)} custom-call(bf16[512,512]{1,0:T(8,128)(2,1)} %get-tuple-element.36.near_ref, bf16[512,512]{1,0:T(8,128)(2,1)} %get-tuple-element.37.far_ref, bf16[512,2048]{1,0:T(8,128)(2,1)} %bitcast.8.near_got_ref, bf16[512,2048]{1,0:T(8,128)(2,1)} %bitcast.6.far_got_ref), custom_call_target="tpu_custom_call" | custom-call | flops 2147483648 | bytes 8388608 | tf_op jit(solution)/shard_map/place_back/pallas_call | solution.py:314
  262.8 1.4 collective-permute-start.8
  266.0 1.7 collective-permute-done.9
  267.7 2.3 collective-permute-start.10
  271.1 1.6 copy-done.5
  272.7 2.7 scale.1
  (43 shorter events, 11.0 us)
Async XLA Ops:
  9.9 58.2 %all-to-all-start = ((bf16[8,64,2560]{2,1,0:T(8,128)(2,1)}), bf16[8,64,2560]{2,1,0:T(8,128)(2,1)S(1)}, u32[]{:S(2)}, u32[]{:S(2)}) async-start(bf16[8,64,2560]{2,1,0:T(8,128)(2,1)} %bitcast.16), calls=%async_computation | async-start | bytes 5242880 | tf_op jit(solution)/shard_map/all_to_all | solution.py:189
  15.2 40.0 %collective-permute-start = (bf16[512,512]{1,0:T(8,128)(2,1)}, bf16[512,512]{1,0:T(8,128)(2,1)S(1)}, u32[]{:S(2)}, u32[]{:S(2)}) collective-permute-start(bf16[512,512]{1,0:T(8,128)(2,1)} %get-tuple-element.31), channel_id=1, source_target_pairs={{0,8},{1,9},{2,10},{3,11},{4,12},{5,13},{6,14},{7,15},{8,0},{9,1},... | collective-permute-start | bytes 1572872 | tf_op jit(solution)/shard_map/ppermute | solution.py:186
  17.5 48.9 %collective-permute-start.1 = (bf16[512,512]{1,0:T(8,128)(2,1)}, bf16[512,512]{1,0:T(8,128)(2,1)}, u32[]{:S(2)}, u32[]{:S(2)}) collective-permute-start(bf16[512,512]{1,0:T(8,128)(2,1)} %get-tuple-element.32), channel_id=1, source_target_pairs={{0,8},{1,9},{2,10},{3,11},{4,12},{5,13},{6,14},{7,15},{8,0},{9,1},... | collective-permute-start | bytes 1572872 | tf_op jit(solution)/shard_map/ppermute | solution.py:186
  55.2 48.9 %copy-start.9 = (bf16[512,512]{1,0:T(8,128)(2,1)}, bf16[512,512]{1,0:T(8,128)(2,1)S(1)}, u32[]{:S(2)}) copy-start(bf16[512,512]{1,0:T(8,128)(2,1)S(1)} %collective-permute-done.refs_0_) | copy-start | bytes 1572868
  68.1 1.5 copy-start.8
  68.1 8.7 %copy-start.11 = (f32[1,512]{1,0:T(1,128)S(1)}, f32[1,512]{1,0:T(1,128)}, u32[]{:S(2)}) copy-start(f32[1,512]{1,0:T(1,128)} %weight_ref.1) | copy-start | bytes 6148
  69.6 51.0 %all-to-all-start.1 = ((bf16[8,64,2560]{2,1,0:T(8,128)(2,1)}), bf16[8,64,2560]{2,1,0:T(8,128)(2,1)S(1)}, u32[]{:S(2)}, u32[]{:S(2)}) async-start(bf16[8,64,2560]{2,1,0:T(8,128)(2,1)} %bitcast.15), calls=%async_computation.1 | async-start | bytes 5242880 | tf_op jit(solution)/shard_map/all_to_all | solution.py:189
  75.3 28.8 %collective-permute-start.3 = (bf16[512,512]{1,0:T(8,128)(2,1)S(1)}, bf16[512,512]{1,0:T(8,128)(2,1)S(1)}, u32[]{:S(2)}, u32[]{:S(2)}) collective-permute-start(bf16[512,512]{1,0:T(8,128)(2,1)S(1)} %collective-permute-done.refs_0_), channel_id=1, source_target_pairs={{0,16},{16,0},{1,17},{17,1},{2,18},{18,2},{3,19},{19,3},{4,20},{20... | collective-permute-start | bytes 1572872 | tf_op jit(solution)/shard_map/ppermute | solution.py:209
  76.6 27.6 %collective-permute-start.4 = (bf16[512,512]{1,0:T(8,128)(2,1)}, bf16[512,512]{1,0:T(8,128)(2,1)}, u32[]{:S(2)}, u32[]{:S(2)}) collective-permute-start(bf16[512,512]{1,0:T(8,128)(2,1)} %collective-permute-done.1.refs_1_), channel_id=1, source_target_pairs={{0,16},{16,0},{1,17},{17,1},{2,18},{18,2},{3,19},{19,3},{4,20},{20... | collective-permute-start | bytes 1572872 | tf_op jit(solution)/shard_map/ppermute | solution.py:209
  76.8 27.3 %collective-permute-start.2 = (f32[1,512]{1,0:T(1,128)S(1)}, f32[1,512]{1,0:T(1,128)S(1)}, u32[]{:S(2)}, u32[]{:S(2)}) collective-permute-start(f32[1,512]{1,0:T(1,128)S(1)} %copy-done.11), channel_id=1, source_target_pairs={{0,8},{1,9},{2,10},{3,11},{4,12},{5,13},{6,14},{7,15},{8,0},{9,1},... | collective-permute-start | bytes 6152 | tf_op jit(solution)/shard_map/ppermute | solution.py:186
  104.1 0.6 copy-start.12
  104.1 0.8 copy-start.10
  120.6 1.5 copy-start
  122.1 30.1 %all-to-all-start.2 = ((bf16[8,64,2048]{2,1,0:T(8,128)(2,1)}), bf16[8,64,2048]{2,1,0:T(8,128)(2,1)}, u32[]{:S(2)}, u32[]{:S(2)}) async-start(bf16[8,64,2048]{2,1,0:T(8,128)(2,1)} %bitcast.18), calls=%async_computation.2 | async-start | bytes 4194304 | tf_op jit(solution)/shard_map/all_to_all | solution.py:189
  152.2 51.0 %copy-start.1 = (bf16[8,64,2560]{2,1,0:T(8,128)(2,1)S(1)}, bf16[8,64,2560]{2,1,0:T(8,128)(2,1)}, u32[]{:S(2)}) copy-start(bf16[8,64,2560]{2,1,0:T(8,128)(2,1)} %copy-done) | copy-start | bytes 7864324
  152.2 51.0 %copy-start.6 = (bf16[512,512]{1,0:T(8,128)(2,1)S(1)}, bf16[512,512]{1,0:T(8,128)(2,1)}, u32[]{:S(2)}) copy-start(bf16[512,512]{1,0:T(8,128)(2,1)} %get-tuple-element.47.res_ref) | copy-start | bytes 1572868
  152.2 51.0 %copy-start.7 = (s32[1,16,4]{2,1,0:T(8,128)S(1)}, s32[1,16,4]{2,1,0:T(8,128)}, u32[]{:S(2)}) copy-start(s32[1,16,4]{2,1,0:T(8,128)} %copy.9.pattern_ref) | copy-start | bytes 772
  152.2 102.9 %all-to-all-start.3 = ((bf16[8,64,2048]{2,1,0:T(8,128)(2,1)}), bf16[8,64,2048]{2,1,0:T(8,128)(2,1)}, u32[]{:S(2)}, u32[]{:S(2)}) async-start(bf16[8,64,2048]{2,1,0:T(8,128)(2,1)} %bitcast.17), calls=%async_computation.3 | async-start | bytes 4194304 | tf_op jit(solution)/shard_map/all_to_all | solution.py:189
  157.6 45.6 %collective-permute-start.6 = (bf16[1024,512]{1,0:T(8,128)(2,1)}, bf16[1024,512]{1,0:T(8,128)(2,1)S(1)}, u32[]{:S(2)}, u32[]{:S(2)}) collective-permute-start(bf16[1024,512]{1,0:T(8,128)(2,1)} %far_raw.3), channel_id=1, source_target_pairs={{0,8},{1,9},{2,10},{3,11},{4,12},{5,13},{6,14},{7,15},{8,0},{9,1},... | collective-permute-start | bytes 3145736 | tf_op jit(solution)/shard_map/ppermute | solution.py:186
  160.3 91.1 %collective-permute-start.5 = (bf16[1024,512]{1,0:T(8,128)(2,1)}, bf16[1024,512]{1,0:T(8,128)(2,1)S(1)}, u32[]{:S(2)}, u32[]{:S(2)}) collective-permute-start(bf16[1024,512]{1,0:T(8,128)(2,1)} %far_raw.2), channel_id=1, source_target_pairs={{0,8},{1,9},{2,10},{3,11},{4,12},{5,13},{6,14},{7,15},{8,0},{9,1},... | collective-permute-start | bytes 3145736 | tf_op jit(solution)/shard_map/ppermute | solution.py:186
  205.7 1.4 copy-start.2
  253.8 1.3 copy-start.4
  255.1 15.9 %copy-start.3 = (f32[1024,512]{1,0:T(8,128)S(1)}, f32[1024,512]{1,0:T(8,128)}, u32[]{:S(2)}) copy-start(f32[1024,512]{1,0:T(8,128)} %copy-done.2) | copy-start | bytes 6291460
  261.3 1.5 collective-permute-start.7
  262.8 2.5 collective-permute-start.8
  265.2 2.5 collective-permute-start.9
  267.7 3.4 %collective-permute-start.10 = (f32[8,128]{1,0:T(8,128)S(1)}, f32[8,128]{1,0:T(8,128)S(1)}, u32[]{:S(2)}, u32[]{:S(2)}) collective-permute-start(f32[8,128]{1,0:T(8,128)S(1)} %add.18), channel_id=1, source_target_pairs={{0,8},{1,9},{2,10},{3,11},{4,12},{5,13},{6,14},{7,15},{8,0},{9,1},... | collective-permute-start | bytes 12296 | tf_op jit(solution)/shard_map/ppermute | solution.py:351
  271.1 1.6 copy-start.5

commit v6 on v5

--- a/solution.py
+++ b/solution.py
@@ -10,13 +10,13 @@
 
 
 BLK = 128
-CHUNKS = 2
+CHUNKS = 4
 F32 = jnp.float32
 BF16 = jnp.bfloat16
 VMEM = pl.BlockSpec(memory_space=pltpu.VMEM)
 SMEM = pl.BlockSpec(memory_space=pltpu.SMEM)
 STREAM = pltpu.CompilerParams(vmem_limit_bytes=60 * 1024 * 1024)
-SMALL = pltpu.CompilerParams(vmem_limit_bytes=32 * 1024 * 1024)
+SMALL = pltpu.CompilerParams(vmem_limit_bytes=24 * 1024 * 1024)
 
 
 def dot(a, b, ca=1, cb=0):
@@ -49,8 +49,7 @@
     slot, rank = places(inst, owner_ref, heads)
     half = heads // 2
     mine = (slot >= half) == (lax.axis_index("loc") >= half)
-    place = jnp.where(slot >= half, slot - half, slot) * capacity + rank
-    return jnp.where(mine, place, -1), jnp.where(mine, -1, place)
+    return mine, jnp.where(slot >= half, slot - half, slot), rank
 
 
 def one_hot_back(pos, size):
@@ -59,13 +58,14 @@
     return (number == column.astype(jnp.int32)).astype(F32).astype(BF16)
 
 
-def prep_kernel(heads, capacity, which, inst_ref, owner_ref, x_ref, t_ref, out_ref, place_ref):
+def prep_kernel(heads, capacity, near, inst_ref, owner_ref, x_ref, t_ref, out_ref, place_ref):
     size, width = out_ref.shape[0], x_ref.shape[1]
     step = pl.program_id(0)
 
     @pl.when(step == 0)
     def _():
-        place = half_places(inst_ref[...], owner_ref, heads, capacity)[which]
+        mine, head, rank = half_places(inst_ref[...], owner_ref, heads, capacity)
+        place = jnp.where(mine == near, head * capacity + rank, -1)
         place_ref[...] = jnp.broadcast_to(place, place_ref.shape)
 
     number = lax.broadcasted_iota(jnp.int32, (size, inst_ref.shape[1]), 0) + step * size
@@ -75,9 +75,10 @@
 
 
 def back_kernel(heads, capacity, inst_ref, owner_ref, near_ref, far_ref):
-    near, far = half_places(inst_ref[...], owner_ref, heads, capacity)
-    near_ref[...] = one_hot_back(near, near_ref.shape[1])
-    far_ref[...] = one_hot_back(far, far_ref.shape[1])
+    mine, head, rank = half_places(inst_ref[...], owner_ref, heads, capacity)
+    place = head * capacity + rank
+    near_ref[...] = one_hot_back(jnp.where(mine, place, -1), near_ref.shape[1])
+    far_ref[...] = one_hot_back(jnp.where(mine, -1, place), far_ref.shape[1])
 
 
 def masked(block, pattern_ref, row, column):
@@ -105,6 +106,29 @@
             out_ref[rows, cols] = masked(w_ref[0, rows, cols], pattern_ref, i, j)
 
 
+def piece_columns(number, deep):
+    first = (lax.axis_index("grp") ^ (number // CHUNKS)) * CHUNKS + number % CHUNKS
+    return pl.ds(pl.multiple_of(first * deep, deep), deep)
+
+
+def far_res_kernel(width, x_ref, weight_ref, *refs):
+    eff_refs, res_ref = refs[:-1], refs[-1]
+    deep = eff_refs[0].shape[0]
+    predicted = dot(x_ref[:, piece_columns(0, deep)], eff_refs[0][...])
+    for number in range(1, len(eff_refs)):
+        predicted += dot(x_ref[:, piece_columns(number, deep)], eff_refs[number][...])
+    misfit = predicted - x_ref[:, width:].astype(F32)
+    res_ref[...] = (weight_ref[...] * misfit).astype(BF16)
+
+
+def far_grad_kernel(res_ref, *refs):
+    eff_refs, grad_ref = refs[:-1], refs[-1]
+    deep = eff_refs[0].shape[0]
+    for number, eff_ref in enumerate(eff_refs):
+        grad = dot(res_ref[...], eff_ref[...], 1, 1)
+        grad_ref[:, piece_columns(number, deep)] = grad.astype(BF16)
+
+
 def head_kernel(width, x_ref, eff_ref, weight_ref, grad_ref, res_ref):
     predicted = dot(x_ref[:, :width], eff_ref[...])
     residual = (weight_ref[...] * (predicted - x_ref[:, width:].astype(F32))).astype(BF16)
@@ -112,36 +136,18 @@
     grad_ref[...] = dot(residual, eff_ref[...], 1, 1).astype(BF16)
 
 
-def far_head_kernel(width, count, x_ref, weight_ref, *refs):
-    eff_refs, (grad_ref, res_ref) = refs[:count], refs[count:]
-    deep = eff_refs[0].shape[0]
-    group = lax.axis_index("grp")
-
-    def columns(number):
-        first = (group ^ (number // CHUNKS)) * CHUNKS + number % CHUNKS
-        return pl.ds(pl.multiple_of(first * deep, deep), deep)
-
-    predicted = dot(x_ref[:, columns(0)], eff_refs[0][...])
-    for number in range(1, count):
-        predicted += dot(x_ref[:, columns(number)], eff_refs[number][...])
-    residual = (weight_ref[...] * (predicted - x_ref[:, width:].astype(F32))).astype(BF16)
-    res_ref[...] = residual
-    for number in range(count):
-        grad_ref[:, columns(number)] = dot(residual, eff_refs[number][...], 1, 1).astype(BF16)
-
-
 def far_raw_kernel(x_ref, res_ref, out_ref):
     out_ref[...] = dot(x_ref[...], res_ref[...], 0, 0).astype(BF16)
 
 
-def raw_kernel(first, x_ref, res_ref, far_ref, pattern_ref, raw_ref, square_ref):
+def raw_kernel(first, x_ref, res_ref, far_ref, pattern_ref, before_ref, raw_ref, square_ref):
     step = pl.program_id(0)
     size, channels = raw_ref.shape
     raw = dot(x_ref[...], res_ref[...], 0, 0) + far_ref[...].astype(F32)
 
     @pl.when(step == 0)
     def _():
-        square_ref[...] = jnp.zeros_like(square_ref)
+        square_ref[...] = before_ref[...]
 
     for i in range(size // BLK):
         for j in range(channels // BLK):
@@ -165,8 +171,12 @@
             out_ref[...] = (raw_refs[part][...] * factor)[None]
 
 
-def place_back_kernel(near_ref, far_ref, near_got_ref, far_got_ref, out_ref):
-    out = dot(near_ref[...], near_got_ref[...]) + dot(far_ref[...], far_got_ref[...])
+def far_place_kernel(back_ref, got_ref, out_ref):
+    out_ref[...] = dot(back_ref[...], got_ref[...]).astype(BF16)
+
+
+def place_back_kernel(back_ref, got_ref, far_ref, out_ref):
+    out = dot(back_ref[...], got_ref[...]) + far_ref[...].astype(F32)
     out_ref[...] = out.astype(BF16)
 
 
@@ -185,12 +195,34 @@
     def partner(x):
         return lax.ppermute(x, "loc", [(i, i ^ half) for i in range(members)])
 
+    def hop(x, distance):
+        return lax.ppermute(x, "loc", [(i, i ^ distance) for i in range(members)])
+
     def in_half(x):
         return lax.all_to_all(
             x, "loc", split_axis=0, concat_axis=0, tiled=True, axis_index_groups=halves
         )
 
+    cut = 4
+
+    def prep(near, name):
+        return pl.pallas_call(
+            functools.partial(prep_kernel, heads, capacity, near),
+            grid=(cut,),
+            in_specs=[whole((1, rows)), SMEM, whole((rows, width)), whole((rows, channels))],
+            out_specs=pl.BlockSpec((placed // cut, wide), lambda i: (i, 0)),
+            out_shape=jax.ShapeDtypeStruct((placed, wide), BF16),
+            scratch_shapes=[pltpu.VMEM((8, rows), jnp.int32)],
+            compiler_params=STREAM,
+            cost_estimate=cost(2 * placed * rows * wide, 2 * (placed + rows) * wide),
+            name=name,
+        )(inst, owner_slot, latents, targets)
+
+    far_send = prep(False, "prep_far")
+    far_send = prep(False, "prep_far")
+    near_send = prep(True, "prep_near")
     deep = width // (groups * CHUNKS)
+    head_weights, far_send = lax.optimization_barrier((head_weights, far_send))
     pieces = pl.pallas_call(
         piece_kernel,
         in_specs=[VMEM, SMEM],
@@ -200,9 +232,10 @@
         cost_estimate=cost(CHUNKS * deep * channels, 4 * CHUNKS * deep * channels),
         name="piece",
     )(head_weights, block_pattern)
-    inst, pieces = lax.optimization_barrier((inst, pieces))
     far_weight = partner(error_weight)
-    swapped = [[partner(piece)] for piece in pieces]
+    crossed = [partner(piece) for piece in pieces]
+    crossed[0], near_send = lax.optimization_barrier((crossed[0], near_send))
+    swapped = [[piece] for piece in crossed]
     step = 1
     while step < groups:
         swap = [(i, i ^ step) for i in range(groups)]
@@ -210,25 +243,14 @@
         step *= 2
     far_eff = [swapped[chunk][number] for number in range(groups) for chunk in range(CHUNKS)]
 
-    cut = 4
-
-    def prep(which, name):
-        return pl.pallas_call(
-            functools.partial(prep_kernel, heads, capacity, which),
-            grid=(cut,),
-            in_specs=[whole((1, rows)), SMEM, whole((rows, width)), whole((rows, channels))],
-            out_specs=pl.BlockSpec((placed // cut, wide), lambda i: (i, 0)),
-            out_shape=jax.ShapeDtypeStruct((placed, wide), BF16),
-            scratch_shapes=[pltpu.VMEM((8, rows), jnp.int32)],
-            compiler_params=STREAM,
-            cost_estimate=cost(2 * placed * rows * wide, 2 * (placed + rows) * wide),
-            name=name,
-        )(inst, owner_slot, latents, targets)
-
-    far_x = in_half(prep(1, "prep_far"))
-    near_send = prep(0, "prep_near")
-    crossed = [held[0] for held in swapped]
-    near_send, far_x, crossed = lax.optimization_barrier((near_send, far_x, crossed))
+    far_x = in_half(far_send)
+    last = swapped[-1][groups // 2 :]
+    swapped[-1] = swapped[-1][: groups // 2]
+    near_send, far_x, swapped, far_weight = lax.optimization_barrier(
+        (near_send, far_x, swapped, far_weight)
+    )
+    swapped[-1] = swapped[-1] + last
+    far_eff = [swapped[chunk][number] for number in range(groups) for chunk in range(CHUNKS)]
     near_x = in_half(near_send)
 
     near_back, far_back = pl.pallas_call(
@@ -236,7 +258,7 @@
         in_specs=[VMEM, SMEM],
         out_specs=[VMEM, VMEM],
         out_shape=[jax.ShapeDtypeStruct((rows, placed), BF16)] * 2,
-        compiler_params=STREAM,
+        compiler_params=SMALL,
         cost_estimate=cost(2 * rows * rows * 128, 4 * rows * placed),
         name="back_places",
     )(inst, owner_slot)
@@ -245,31 +267,27 @@
         in_specs=[VMEM, SMEM],
         out_specs=VMEM,
         out_shape=jax.ShapeDtypeStruct((width, channels), BF16),
-        compiler_params=STREAM,
+        compiler_params=SMALL,
         cost_estimate=cost(width * channels, 4 * width * channels),
         name="effective",
     )(head_weights, block_pattern)
-
-    size = placed // cut
-    head_out = [
-        pl.BlockSpec((size, width), lambda i: (i, 0)),
-        pl.BlockSpec((size, channels), lambda i: (i, 0)),
-    ]
-    head_shape = [
-        jax.ShapeDtypeStruct((placed, width), BF16),
-        jax.ShapeDtypeStruct((placed, channels), BF16),
-    ]
-    head_cost = cost(4 * placed * width * channels, 2 * placed * (2 * wide + width))
+    far_x, effective, near_back, far_back = lax.optimization_barrier(
+        (far_x, effective, near_back, far_back)
+    )
+
+    size = placed // 2
     row_spec = pl.BlockSpec((size, wide), lambda i: (i, 0))
-    far_grad, far_res = pl.pallas_call(
-        functools.partial(far_head_kernel, width, len(far_eff)),
-        grid=(cut,),
-        in_specs=[row_spec, whole((1, channels))] + [whole((deep, channels))] * len(far_eff),
-        out_specs=head_out,
-        out_shape=head_shape,
-        compiler_params=STREAM,
-        cost_estimate=head_cost,
-        name="far_head",
+    res_spec = pl.BlockSpec((size, channels), lambda i: (i, 0))
+    far_specs = [whole((deep, channels))] * len(far_eff)
+    far_res = pl.pallas_call(
+        functools.partial(far_res_kernel, width),
+        grid=(2,),
+        in_specs=[row_spec, whole((1, channels))] + far_specs,
+        out_specs=res_spec,
+        out_shape=jax.ShapeDtypeStruct((placed, channels), BF16),
+        compiler_params=SMALL,
+        cost_estimate=cost(2 * placed * width * channels, 2 * placed * wide),
+        name="far_res",
     )(far_x, far_weight, *far_eff)
 
     tall = 256
@@ -285,47 +303,60 @@
             ],
             out_specs=pl.BlockSpec((tall, channels), lambda i: (i, 0)),
             out_shape=jax.ShapeDtypeStruct((width // CHUNKS, channels), BF16),
-            compiler_params=STREAM,
+            compiler_params=SMALL,
             cost_estimate=cost(2 * placed * width * channels // CHUNKS, 2 * width * channels),
             name="far_raw",
         )(far_x, far_res)
         far_raw.append(part)
     sent = far_raw
     far_raw = [partner(part) for part in sent]
+
+    grad_spec = pl.BlockSpec((size, width), lambda i: (i, 0))
+    far_grad = pl.pallas_call(
+        far_grad_kernel,
+        grid=(2,),
+        in_specs=[res_spec] + far_specs,
+        out_specs=grad_spec,
+        out_shape=jax.ShapeDtypeStruct((placed, width), BF16),
+        compiler_params=SMALL,
+        cost_estimate=cost(2 * placed * width * channels, 2 * placed * wide),
+        name="far_grad",
+    )(far_res, *far_eff)
     far_grad, sent = lax.optimization_barrier((far_grad, sent))
-
-    near_x, effective, near_back, far_back = lax.optimization_barrier(
-        (near_x, effective, near_back, far_back)
-    )
+    far_got = in_half(far_grad)
     near_grad, near_res = pl.pallas_call(
         functools.partial(head_kernel, width),
-        grid=(cut,),
+        grid=(2,),
         in_specs=[row_spec, whole((width, channels)), whole((1, channels))],
-        out_specs=head_out,
-        out_shape=head_shape,
-        compiler_params=STREAM,
-        cost_estimate=head_cost,
+        out_specs=[grad_spec, res_spec],
+        out_shape=[
+            jax.ShapeDtypeStruct((placed, width), BF16),
+            jax.ShapeDtypeStruct((placed, channels), BF16),
+        ],
+        compiler_params=SMALL,
+        cost_estimate=cost(1 << 40, 1 << 30),
         name="near_head",
     )(near_x, effective, error_weight)
-
-    far_got = in_half(far_grad)
     near_grad, far_got = lax.optimization_barrier((near_grad, far_got))
     near_got = in_half(near_grad)
-    latent_grad = pl.pallas_call(
-        place_back_kernel,
+
+    def column_spec(deep):
+        return pl.BlockSpec((deep, width // cut), lambda i: (0, i))
+
+    far_placed = pl.pallas_call(
+        far_place_kernel,
         grid=(cut,),
-        in_specs=[whole((rows, placed))] * 2
-        + [pl.BlockSpec((placed, width // cut), lambda i: (0, i))] * 2,
-        out_specs=pl.BlockSpec((rows, width // cut), lambda i: (0, i)),
+        in_specs=[whole((rows, placed)), column_spec(placed)],
+        out_specs=column_spec(rows),
         out_shape=jax.ShapeDtypeStruct((rows, width), BF16),
-        compiler_params=STREAM,
-        cost_estimate=cost(4 * rows * placed * width, 8 * placed * width),
-        name="place_back",
-    )(near_back, far_back, near_got, far_got)
-
-    raw_grad, squares = [], 0.0
+        compiler_params=SMALL,
+        cost_estimate=cost(2 * rows * placed * width, 4 * placed * width),
+        name="far_place",
+    )(far_back, far_got)
+    far_raw[0], far_placed = lax.optimization_barrier((far_raw[0], far_placed))
+    raw_grad, squares = [], jnp.zeros((8, 128), F32)
     for chunk in range(CHUNKS):
-        part, square = pl.pallas_call(
+        part, squares = pl.pallas_call(
             functools.partial(raw_kernel, chunk * steps * (tall // BLK)),
             grid=(steps,),
             in_specs=[
@@ -333,6 +364,7 @@
                 whole((placed, channels)),
                 pl.BlockSpec((tall, channels), lambda i: (i, 0)),
                 SMEM,
+                whole((8, 128)),
             ],
             out_specs=[pl.BlockSpec((tall, channels), lambda i: (i, 0)), whole((8, 128))],
             out_shape=[
@@ -340,17 +372,29 @@
                 jax.ShapeDtypeStruct((8, 128), F32),
             ],
             compiler_params=SMALL,
-            cost_estimate=cost(2 * placed * width * channels // CHUNKS, 4 * width * channels),
+            cost_estimate=cost(1 << 40, 1 << 30),
             name="raw",
-        )(near_x, near_res, far_raw[chunk], block_pattern)
+        )(near_x, near_res, far_raw[chunk], block_pattern, squares)
         raw_grad.append(part)
-        squares = squares + square
-    latent_grad, squares = lax.optimization_barrier((latent_grad, squares))
     step = 1
     while step < members:
-        squares = squares + lax.ppermute(squares, "loc", [(i, i ^ step) for i in range(members)])
-        step *= 2
-
+        ways = min(4, members // step)
+        squares = squares + sum(hop(squares, step * way) for way in range(1, ways))
+        if step == 1:
+            near_got, squares = lax.optimization_barrier((near_got, squares))
+        step *= ways
+
+    latent_grad = pl.pallas_call(
+        place_back_kernel,
+        grid=(cut,),
+        in_specs=[whole((rows, placed)), column_spec(placed), column_spec(rows)],
+        out_specs=column_spec(rows),
+        out_shape=jax.ShapeDtypeStruct((rows, width), BF16),
+        compiler_params=SMALL,
+        cost_estimate=cost(2 * rows * placed * width, 4 * placed * width),
+        name="place_back",
+    )(near_back, near_got, far_placed)
+    latent_grad, squares = lax.optimization_barrier((latent_grad, squares))
     def raw_spec(part):
         low = part * (cut // CHUNKS)
         return pl.BlockSpec(

time: 280 us -> 227 us (0.81)
  waiting for transfers between devices: 176 us -> 115 us
  starting transfers between devices: 33.5 us -> 47 us
  Pallas kernels: 55.6 us -> 47.6 us
  local copies, waits for them, and re-layouts: 9.41 us -> 13.9 us
    ppermute x5 -> x9, waiting for transfers between devices: 158 us -> 31.4 us  [partner(): return lax.ppermute(x, 'loc', [(i, i ^ half) for i in range(members)])]
    all_to_all x4, waiting for transfers between devices: 13.4 us -> 72.3 us  [in_half(): lax.all_to_all(x, 'loc', split_axis=0, concat_axis=0, tiled=True, axis_in...]
    ppermute x5 -> x9, starting transfers between devices: 5.2 us -> 12.5 us  [partner(): return lax.ppermute(x, 'loc', [(i, i ^ half) for i in range(members)])]
    ppermute x4 -> x6, waiting for transfers between devices: 4.64 us -> 11.5 us  [hop(): return lax.ppermute(x, 'loc', [(i, i ^ distance) for i in range(members)])]
    unnamed x27 -> x61, local copies, waits for them, and re-layouts: 9.41 us -> 13.9 us
    ppermute x2 -> x4, starting transfers between devices: 1.47 us -> 4.74 us  [per_device(): lax.ppermute(x, 'grp', swap)]
    pallas_call x4 -> x6, Pallas kernels: 25.2 us -> 21.9 us  [the longest x2 10.4 us: prep(): pl.pallas_call(functools.partial(prep_kernel, heads, capacity, near), gri...]
    pallas_call x2 -> x4, Pallas kernels: 4.89 us -> 7.75 us  [per_device(): pl.pallas_call(functools.partial(raw_kernel, chunk * steps * (tall // BLK...]
  transfers between devices with their start and end apart: 15 -> 23, of which waited for: 11 -> 9; matrix products, arithmetic and copies ran while one was open for 0% -> 0% of each run, Pallas kernels for 14% -> 18%
where the time goes in v6:
time: 227 us; the launch traced here: 225 us
  waiting for transfers between devices  115 us (51%)
  Pallas kernels  47.6 us (21%)
  starting transfers between devices  47 us (21%)
  local copies, waits for them, and re-layouts  13.9 us (6%)
    all_to_all x4, waiting for transfers between devices, in_half(): lax.all_to_all(x, 'loc', split_axis=0, concat_axis=0, tiled=True, axis_in...  72.3 us
    ppermute x9, waiting for transfers between devices, partner(): return lax.ppermute(x, 'loc', [(i, i ^ half) for i in range(members)])  31.4 us
    all_to_all x4, starting transfers between devices, in_half(): lax.all_to_all(x, 'loc', split_axis=0, concat_axis=0, tiled=True, axis_in...  24.1 us
    unnamed x61, local copies, waits for them, and re-layouts  13.9 us
    ppermute x9, starting transfers between devices, partner(): return lax.ppermute(x, 'loc', [(i, i ^ half) for i in range(members)])  12.5 us
    ppermute x6, waiting for transfers between devices, hop(): return lax.ppermute(x, 'loc', [(i, i ^ distance) for i in range(members)])  11.5 us
    pallas_call x2, Pallas kernels, prep(): pl.pallas_call(functools.partial(prep_kernel, heads, capacity, near), gri...  10.4 us
    pallas_call x4, Pallas kernels, per_device(): pl.pallas_call(functools.partial(raw_kernel, chunk * steps * (tall // BLK...  7.75 us
  transfers between devices with their start and end apart: 23, of which 9 were waited for; matrix products, arithmetic and copies ran while one was open for 0% of the time, Pallas kernels for 18%

profile of v6, /device:TPU:1, one launch (start us, length us, event | category | flops | bytes accessed | tf_op | source)
XLA Modules:
  0.0 224.9 jit_solution(4704053915213429903)
XLA Ops:
  0.6 5.2 %prep_far.1 = bf16[512,2560]{1,0:T(8,128)(2,1)} custom-call(s32[1,512]{1,0:T(1,128)} %bitcast.15, s32[16]{0:T(128)} %owner_ref.5, bf16[512,2048]{1,0:T(8,128)(2,1)} %x_ref.3, bf16[512,512]{1,0:T(8,128)(2,1)} %t_ref.3), custom_call_target="tpu_custom_call" | custom-call | flops 1342177280 | bytes 5242880 | tf_op jit(solution)/shard_map/prep_far/pallas_call | solution.py:209
  5.8 5.4 %all-to-all-start = ((bf16[8,64,2560]{2,1,0:T(8,128)(2,1)}), bf16[8,64,2560]{2,1,0:T(8,128)(2,1)S(1)}, u32[]{:S(2)}, u32[]{:S(2)}) async-start(bf16[8,64,2560]{2,1,0:T(8,128)(2,1)} %bitcast.19), calls=%async_computation | async-start | bytes 5242880 | tf_op jit(solution)/shard_map/all_to_all | solution.py:202
  12.0 2.7 %piece.1 = (bf16[256,512]{1,0:T(8,128)(2,1)}, bf16[256,512]{1,0:T(8,128)(2,1)}, bf16[256,512]{1,0:T(8,128)(2,1)}, bf16[256,512]{1,0:T(8,128)(2,1)}) custom-call(bf16[1,2048,512]{2,1,0:T(8,128)(2,1)} %w_ref.1, s32[1,16,4]{2,1,0:T(8,128)} %copy.9.pattern_ref), custom_call_target="tpu_custom_call" | custom-call | flops 524288 | bytes 2097152 | tf_op jit(solution)/shard_map/piece/pallas_call | solution.py:226
  14.6 2.3 %collective-permute-start = (bf16[256,512]{1,0:T(8,128)(2,1)}, bf16[256,512]{1,0:T(8,128)(2,1)S(1)}, u32[]{:S(2)}, u32[]{:S(2)}) collective-permute-start(bf16[256,512]{1,0:T(8,128)(2,1)} %get-tuple-element.46), channel_id=1, source_target_pairs={{0,8},{1,9},{2,10},{3,11},{4,12},{5,13},{6,14},{7,15},{8,0},{9,1},... | collective-permute-start | bytes 786440 | tf_op jit(solution)/shard_map/ppermute | solution.py:196
  17.0 2.3 %collective-permute-start.4 = (bf16[256,512]{1,0:T(8,128)(2,1)}, bf16[256,512]{1,0:T(8,128)(2,1)S(1)}, u32[]{:S(2)}, u32[]{:S(2)}) collective-permute-start(bf16[256,512]{1,0:T(8,128)(2,1)} %get-tuple-element.51), channel_id=1, source_target_pairs={{0,8},{1,9},{2,10},{3,11},{4,12},{5,13},{6,14},{7,15},{8,0},{9,1},... | collective-permute-start | bytes 786440 | tf_op jit(solution)/shard_map/ppermute | solution.py:196
  19.4 5.2 %prep_near.1 = bf16[512,2560]{1,0:T(8,128)(2,1)} custom-call(s32[1,512]{1,0:T(1,128)} %bitcast.16, s32[16]{0:T(128)} %owner_ref.5, bf16[512,2048]{1,0:T(8,128)(2,1)} %x_ref.3, bf16[512,512]{1,0:T(8,128)(2,1)} %t_ref.3), custom_call_target="tpu_custom_call" | custom-call | flops 1342177280 | bytes 5242880 | tf_op jit(solution)/shard_map/prep_near/pallas_call | solution.py:209
  24.5 21.2 %collective-permute-done.refs_0_ = bf16[256,512]{1,0:T(8,128)(2,1)S(1)} collective-permute-done((bf16[256,512]{1,0:T(8,128)(2,1)}, bf16[256,512]{1,0:T(8,128)(2,1)S(1)}, u32[]{:S(2)}, u32[]{:S(2)}) %collective-permute-start) | collective-permute-done | bytes 262176 | tf_op jit(solution)/shard_map/ppermute | solution.py:196
  46.9 4.4 %collective-permute-done.2.refs_1_ = bf16[256,512]{1,0:T(8,128)(2,1)S(1)} collective-permute-done((bf16[256,512]{1,0:T(8,128)(2,1)}, bf16[256,512]{1,0:T(8,128)(2,1)S(1)}, u32[]{:S(2)}, u32[]{:S(2)}) %collective-permute-start.2) | collective-permute-done | bytes 262176 | tf_op jit(solution)/shard_map/ppermute | solution.py:196
  52.5 4.4 %collective-permute-done.4.refs_2_ = bf16[256,512]{1,0:T(8,128)(2,1)S(1)} collective-permute-done((bf16[256,512]{1,0:T(8,128)(2,1)}, bf16[256,512]{1,0:T(8,128)(2,1)S(1)}, u32[]{:S(2)}, u32[]{:S(2)}) %collective-permute-start.4) | collective-permute-done | bytes 262176 | tf_op jit(solution)/shard_map/ppermute | solution.py:196
  58.2 3.0 %collective-permute-start.7 = (f32[1,512]{1,0:T(1,128)S(1)}, f32[1,512]{1,0:T(1,128)S(1)}, u32[]{:S(2)}, u32[]{:S(2)}) collective-permute-start(f32[1,512]{1,0:T(1,128)S(1)} %copy-done.25), channel_id=1, source_target_pairs={{0,8},{1,9},{2,10},{3,11},{4,12},{5,13},{6,14},{7,15},{8,0},{9,1},... | collective-permute-start | bytes 6152 | tf_op jit(solution)/shard_map/ppermute | solution.py:196
  64.8 8.3 %all-to-all-start.1 = ((bf16[8,64,2560]{2,1,0:T(8,128)(2,1)}), bf16[8,64,2560]{2,1,0:T(8,128)(2,1)}, u32[]{:S(2)}, u32[]{:S(2)}) async-start(bf16[8,64,2560]{2,1,0:T(8,128)(2,1)} %bitcast.18), calls=%async_computation.1 | async-start | bytes 5242880 | tf_op jit(solution)/shard_map/all_to_all | solution.py:202
  74.1 1.6 copy-done
  81.3 1.5 far_res.1.res_ref
  86.3 1.7 collective-permute-start.11
  90.0 1.4 far_raw.7
  91.5 1.7 collective-permute-start.9
  93.2 2.5 %far_grad.1 = bf16[512,2048]{1,0:T(8,128)(2,1)} custom-call(bf16[512,512]{1,0:T(8,128)(2,1)S(1)} %far_res.1.res_ref, bf16[256,512]{1,0:T(8,128)(2,1)S(1)} %collective-permute-done.refs_0_, bf16[256,512]{1,0:T(8,128)(2,1)S(1)} %collective-permute-done.2.refs_1_, bf16[256,512]{1,0:T(8,128)(2,1)S(1)} %collective-permute-done.4.refs_2_, ...), custom_call_target="tpu_custom_call" | custom-call | flops 1073741824 | bytes 2621440 | tf_op jit(solution)/shard_map/far_grad/pallas_call | solution.py:315
  95.7 24.3 %all-to-all-done.1 = bf16[8,64,2560]{2,1,0:T(8,128)(2,1)} async-done(((bf16[8,64,2560]{2,1,0:T(8,128)(2,1)}), bf16[8,64,2560]{2,1,0:T(8,128)(2,1)}, u32[]{:S(2)}, u32[]{:S(2)}) %all-to-all-start.1) | async-done | bytes 2621472 | tf_op jit(solution)/shard_map/all_to_all | solution.py:202
  120.0 5.3 %all-to-all-start.2 = ((bf16[8,64,2048]{2,1,0:T(8,128)(2,1)}), bf16[8,64,2048]{2,1,0:T(8,128)(2,1)}, u32[]{:S(2)}, u32[]{:S(2)}) async-start(bf16[8,64,2048]{2,1,0:T(8,128)(2,1)} %bitcast.5), calls=%async_computation.2 | async-start | bytes 4194304 | tf_op jit(solution)/shard_map/all_to_all | solution.py:202
  125.3 4.1 %near_head.1 = (bf16[512,2048]{1,0:T(8,128)(2,1)S(1)}, bf16[512,512]{1,0:T(8,128)(2,1)S(1)}) custom-call(bf16[512,2560]{1,0:T(8,128)(2,1)} %bitcast.4.x_ref, bf16[2048,512]{1,0:T(8,128)(2,1)S(1)} %copy-done.3, f32[1,512]{1,0:T(1,128)S(1)} %copy-done.25), custom_call_target="tpu_custom_call" | custom-call | flops 1099511627776 | bytes 1073741824 | tf_op jit(solution)/shard_map/near_head/pallas_call | solution.py:327
  130.7 48.0 %all-to-all-done.2 = bf16[8,64,2048]{2,1,0:T(8,128)(2,1)} async-done(((bf16[8,64,2048]{2,1,0:T(8,128)(2,1)}), bf16[8,64,2048]{2,1,0:T(8,128)(2,1)}, u32[]{:S(2)}, u32[]{:S(2)}) %all-to-all-start.2) | async-done | bytes 2097184 | tf_op jit(solution)/shard_map/all_to_all | solution.py:202
  178.7 3.5 %far_place.1.far_ref = bf16[512,2048]{1,0:T(8,128)(2,1)S(1)} custom-call(bf16[512,512]{1,0:T(8,128)(2,1)S(1)} %copy-done.19, bf16[512,2048]{1,0:T(8,128)(2,1)} %bitcast.6.got_ref), custom_call_target="tpu_custom_call" | custom-call | flops 1073741824 | bytes 4194304 | tf_op jit(solution)/shard_map/far_place/pallas_call | solution.py:346
  182.3 5.1 %all-to-all-start.3 = ((bf16[8,64,2048]{2,1,0:T(8,128)(2,1)}), bf16[8,64,2048]{2,1,0:T(8,128)(2,1)}, u32[]{:S(2)}, u32[]{:S(2)}) async-start(bf16[8,64,2048]{2,1,0:T(8,128)(2,1)} %bitcast.14), calls=%async_computation.3 | async-start | bytes 4194304 | tf_op jit(solution)/shard_map/all_to_all | solution.py:202
  188.4 2.0 raw.4
  190.4 1.9 raw.5
  193.3 1.9 raw.6
  196.3 1.9 raw.7
  199.4 1.6 collective-permute-start.14
  201.4 11.0 %collective-permute-done.14 = f32[8,128]{1,0:T(8,128)S(1)} collective-permute-done((f32[8,128]{1,0:T(8,128)S(1)}, f32[8,128]{1,0:T(8,128)S(1)}, u32[]{:S(2)}, u32[]{:S(2)}) %collective-permute-start.14) | collective-permute-done | bytes 4128 | tf_op jit(solution)/shard_map/ppermute | solution.py:199
  214.2 2.3 %collective-permute-start.18 = (f32[8,128]{1,0:T(8,128)S(1)}, f32[8,128]{1,0:T(8,128)S(1)}, u32[]{:S(2)}, u32[]{:S(2)}) collective-permute-start(f32[8,128]{1,0:T(8,128)S(1)} %add_add_fusion.1), channel_id=1, source_target_pairs={{0,12},{1,13},{2,14},{3,15},{4,8},{5,9},{6,10},{7,11},{8,4},{9,5},... | collective-permute-start | bytes 12296 | tf_op jit(solution)/shard_map/ppermute | solution.py:199
  217.6 4.6 %place_back.1 = bf16[512,2048]{1,0:T(8,128)(2,1)} custom-call(bf16[512,512]{1,0:T(8,128)(2,1)S(1)} %copy-done.21, bf16[512,2048]{1,0:T(8,128)(2,1)} %bitcast.8.got_ref, bf16[512,2048]{1,0:T(8,128)(2,1)S(1)} %far_place.1.far_ref), custom_call_target="tpu_custom_call" | custom-call | flops 1073741824 | bytes 4194304 | tf_op jit(solution)/shard_map/place_back/pallas_call | solution.py:387
  222.2 2.7 %scale.1 = f32[1,2048,512]{2,1,0:T(8,128)} custom-call(f32[512,512]{1,0:T(8,128)S(1)} %get-tuple-element.83.refs_0_, f32[512,512]{1,0:T(8,128)S(1)} %copy-done.13, f32[512,512]{1,0:T(8,128)S(1)} %copy-done.15, f32[512,512]{1,0:T(8,128)S(1)} %copy-done.17, f32[8,128]{1,0:T(8,128)S(1)} %add_add_fusion.refs_4_), custom_call_target="tpu_custom_call" | custom-call | flops 1048576 | bytes 8388608 | tf_op jit(solution)/shard_map/scale/pallas_call | solution.py:404
  (97 shorter events, 28.9 us)
Async XLA Ops:
  5.8 58.9 %all-to-all-start = ((bf16[8,64,2560]{2,1,0:T(8,128)(2,1)}), bf16[8,64,2560]{2,1,0:T(8,128)(2,1)S(1)}, u32[]{:S(2)}, u32[]{:S(2)}) async-start(bf16[8,64,2560]{2,1,0:T(8,128)(2,1)} %bitcast.19), calls=%async_computation | async-start | bytes 5242880 | tf_op jit(solution)/shard_map/all_to_all | solution.py:202
  14.6 31.1 %collective-permute-start = (bf16[256,512]{1,0:T(8,128)(2,1)}, bf16[256,512]{1,0:T(8,128)(2,1)S(1)}, u32[]{:S(2)}, u32[]{:S(2)}) collective-permute-start(bf16[256,512]{1,0:T(8,128)(2,1)} %get-tuple-element.46), channel_id=1, source_target_pairs={{0,8},{1,9},{2,10},{3,11},{4,12},{5,13},{6,14},{7,15},{8,0},{9,1},... | collective-permute-start | bytes 786440 | tf_op jit(solution)/shard_map/ppermute | solution.py:196
  16.9 34.4 %collective-permute-start.2 = (bf16[256,512]{1,0:T(8,128)(2,1)}, bf16[256,512]{1,0:T(8,128)(2,1)S(1)}, u32[]{:S(2)}, u32[]{:S(2)}) collective-permute-start(bf16[256,512]{1,0:T(8,128)(2,1)} %get-tuple-element.50), channel_id=1, source_target_pairs={{0,8},{1,9},{2,10},{3,11},{4,12},{5,13},{6,14},{7,15},{8,0},{9,1},... | collective-permute-start | bytes 786440 | tf_op jit(solution)/shard_map/ppermute | solution.py:196
  17.0 40.0 %collective-permute-start.4 = (bf16[256,512]{1,0:T(8,128)(2,1)}, bf16[256,512]{1,0:T(8,128)(2,1)S(1)}, u32[]{:S(2)}, u32[]{:S(2)}) collective-permute-start(bf16[256,512]{1,0:T(8,128)(2,1)} %get-tuple-element.51), channel_id=1, source_target_pairs={{0,8},{1,9},{2,10},{3,11},{4,12},{5,13},{6,14},{7,15},{8,0},{9,1},... | collective-permute-start | bytes 786440 | tf_op jit(solution)/shard_map/ppermute | solution.py:196
  19.3 38.9 %copy-start.25 = (f32[1,512]{1,0:T(1,128)S(1)}, f32[1,512]{1,0:T(1,128)}, u32[]{:S(2)}) copy-start(f32[1,512]{1,0:T(1,128)} %weight_ref.1) | copy-start | bytes 6148
  19.3 43.3 %collective-permute-start.6 = (bf16[256,512]{1,0:T(8,128)(2,1)}, bf16[256,512]{1,0:T(8,128)(2,1)S(1)}, u32[]{:S(2)}, u32[]{:S(2)}) collective-permute-start(bf16[256,512]{1,0:T(8,128)(2,1)} %get-tuple-element.52), channel_id=1, source_target_pairs={{0,8},{1,9},{2,10},{3,11},{4,12},{5,13},{6,14},{7,15},{8,0},{9,1},... | collective-permute-start | bytes 786440 | tf_op jit(solution)/shard_map/ppermute | solution.py:196
  45.7 16.9 %collective-permute-start.1 = (bf16[256,512]{1,0:T(8,128)(2,1)S(1)}, bf16[256,512]{1,0:T(8,128)(2,1)S(1)}, u32[]{:S(2)}, u32[]{:S(2)}) collective-permute-start(bf16[256,512]{1,0:T(8,128)(2,1)S(1)} %collective-permute-done.refs_0_), channel_id=1, source_target_pairs={{0,16},{16,0},{1,17},{17,1},{2,18},{18,2},{3,19},{19,3},{4,20},{20... | collective-permute-start | bytes 786440 | tf_op jit(solution)/shard_map/ppermute | solution.py:242
  51.3 12.0 %collective-permute-start.3 = (bf16[256,512]{1,0:T(8,128)(2,1)S(1)}, bf16[256,512]{1,0:T(8,128)(2,1)S(1)}, u32[]{:S(2)}, u32[]{:S(2)}) collective-permute-start(bf16[256,512]{1,0:T(8,128)(2,1)S(1)} %collective-permute-done.2.refs_1_), channel_id=1, source_target_pairs={{0,16},{16,0},{1,17},{17,1},{2,18},{18,2},{3,19},{19,3},{4,20},{20... | collective-permute-start | bytes 786440 | tf_op jit(solution)/shard_map/ppermute | solution.py:242
  56.9 7.1 %collective-permute-start.5 = (bf16[256,512]{1,0:T(8,128)(2,1)S(1)}, bf16[256,512]{1,0:T(8,128)(2,1)S(1)}, u32[]{:S(2)}, u32[]{:S(2)}) collective-permute-start(bf16[256,512]{1,0:T(8,128)(2,1)S(1)} %collective-permute-done.4.refs_2_), channel_id=1, source_target_pairs={{0,16},{16,0},{1,17},{17,1},{2,18},{18,2},{3,19},{19,3},{4,20},{20... | collective-permute-start | bytes 786440 | tf_op jit(solution)/shard_map/ppermute | solution.py:242
  58.2 4.4 %collective-permute-start.7 = (f32[1,512]{1,0:T(1,128)S(1)}, f32[1,512]{1,0:T(1,128)S(1)}, u32[]{:S(2)}, u32[]{:S(2)}) collective-permute-start(f32[1,512]{1,0:T(1,128)S(1)} %copy-done.25), channel_id=1, source_target_pairs={{0,8},{1,9},{2,10},{3,11},{4,12},{5,13},{6,14},{7,15},{8,0},{9,1},... | collective-permute-start | bytes 6152 | tf_op jit(solution)/shard_map/ppermute | solution.py:196
  64.8 9.3 %copy-start.22 = (s32[1,16,4]{2,1,0:T(8,128)S(1)}, s32[1,16,4]{2,1,0:T(8,128)}, u32[]{:S(2)}) copy-start(s32[1,16,4]{2,1,0:T(8,128)} %copy.9.pattern_ref) | copy-start | bytes 772
  64.8 55.2 %all-to-all-start.1 = ((bf16[8,64,2560]{2,1,0:T(8,128)(2,1)}), bf16[8,64,2560]{2,1,0:T(8,128)(2,1)}, u32[]{:S(2)}, u32[]{:S(2)}) async-start(bf16[8,64,2560]{2,1,0:T(8,128)(2,1)} %bitcast.18), calls=%async_computation.1 | async-start | bytes 5242880 | tf_op jit(solution)/shard_map/all_to_all | solution.py:202
  73.0 8.3 %collective-permute-start.8 = (bf16[256,512]{1,0:T(8,128)(2,1)}, bf16[256,512]{1,0:T(8,128)(2,1)S(1)}, u32[]{:S(2)}, u32[]{:S(2)}) collective-permute-start(bf16[256,512]{1,0:T(8,128)(2,1)} %copy-done.4), channel_id=1, source_target_pairs={{0,16},{16,0},{1,17},{17,1},{2,18},{18,2},{3,19},{19,3},{4,20},{20... | collective-permute-start | bytes 786440 | tf_op jit(solution)/shard_map/ppermute | solution.py:242
  75.7 5.6 %copy-start.5 = (bf16[256,512]{1,0:T(8,128)(2,1)S(1)}, bf16[256,512]{1,0:T(8,128)(2,1)}, u32[]{:S(2)}) copy-start(bf16[256,512]{1,0:T(8,128)(2,1)} %copy-done.4) | copy-start | bytes 786436
  75.7 5.6 %copy-start.7 = (bf16[256,512]{1,0:T(8,128)(2,1)S(1)}, bf16[256,512]{1,0:T(8,128)(2,1)}, u32[]{:S(2)}) copy-start(bf16[256,512]{1,0:T(8,128)(2,1)} %copy-done.6) | copy-start | bytes 786436
  84.2 98.1 %collective-permute-start.12 = (bf16[512,512]{1,0:T(8,128)(2,1)}, bf16[512,512]{1,0:T(8,128)(2,1)}, u32[]{:S(2)}, u32[]{:S(2)}) collective-permute-start(bf16[512,512]{1,0:T(8,128)(2,1)} %far_raw.4), channel_id=1, source_target_pairs={{0,8},{1,9},{2,10},{3,11},{4,12},{5,13},{6,14},{7,15},{8,0},{9,1},... | collective-permute-start | bytes 1572872 | tf_op jit(solution)/shard_map/ppermute | solution.py:196
  86.3 104.1 %collective-permute-start.11 = (bf16[512,512]{1,0:T(8,128)(2,1)}, bf16[512,512]{1,0:T(8,128)(2,1)}, u32[]{:S(2)}, u32[]{:S(2)}) collective-permute-start(bf16[512,512]{1,0:T(8,128)(2,1)} %far_raw.5), channel_id=1, source_target_pairs={{0,8},{1,9},{2,10},{3,11},{4,12},{5,13},{6,14},{7,15},{8,0},{9,1},... | collective-permute-start | bytes 1572872 | tf_op jit(solution)/shard_map/ppermute | solution.py:196
  89.4 103.9 %collective-permute-start.10 = (bf16[512,512]{1,0:T(8,128)(2,1)}, bf16[512,512]{1,0:T(8,128)(2,1)}, u32[]{:S(2)}, u32[]{:S(2)}) collective-permute-start(bf16[512,512]{1,0:T(8,128)(2,1)} %far_raw.6), channel_id=1, source_target_pairs={{0,8},{1,9},{2,10},{3,11},{4,12},{5,13},{6,14},{7,15},{8,0},{9,1},... | collective-permute-start | bytes 1572872 | tf_op jit(solution)/shard_map/ppermute | solution.py:196
  91.5 104.8 %collective-permute-start.9 = (bf16[512,512]{1,0:T(8,128)(2,1)}, bf16[512,512]{1,0:T(8,128)(2,1)}, u32[]{:S(2)}, u32[]{:S(2)}) collective-permute-start(bf16[512,512]{1,0:T(8,128)(2,1)} %far_raw.7), channel_id=1, source_target_pairs={{0,8},{1,9},{2,10},{3,11},{4,12},{5,13},{6,14},{7,15},{8,0},{9,1},... | collective-permute-start | bytes 1572872 | tf_op jit(solution)/shard_map/ppermute | solution.py:196
  120.0 58.7 %all-to-all-start.2 = ((bf16[8,64,2048]{2,1,0:T(8,128)(2,1)}), bf16[8,64,2048]{2,1,0:T(8,128)(2,1)}, u32[]{:S(2)}, u32[]{:S(2)}) async-start(bf16[8,64,2048]{2,1,0:T(8,128)(2,1)} %bitcast.5), calls=%async_computation.2 | async-start | bytes 4194304 | tf_op jit(solution)/shard_map/all_to_all | solution.py:202
  125.3 53.4 %copy-start.19 = (bf16[512,512]{1,0:T(8,128)(2,1)S(1)}, bf16[512,512]{1,0:T(8,128)(2,1)}, u32[]{:S(2)}) copy-start(bf16[512,512]{1,0:T(8,128)(2,1)} %copy-done.18) | copy-start | bytes 1572868
  130.7 51.6 %copy-start.26 = (bf16[512,512]{1,0:T(8,128)(2,1)}, bf16[512,512]{1,0:T(8,128)(2,1)S(1)}, u32[]{:S(2)}) copy-start(bf16[512,512]{1,0:T(8,128)(2,1)S(1)} %get-tuple-element.71.res_ref) | copy-start | bytes 1572868
  182.3 30.6 %all-to-all-start.3 = ((bf16[8,64,2048]{2,1,0:T(8,128)(2,1)}), bf16[8,64,2048]{2,1,0:T(8,128)(2,1)}, u32[]{:S(2)}, u32[]{:S(2)}) async-start(bf16[8,64,2048]{2,1,0:T(8,128)(2,1)} %bitcast.14), calls=%async_computation.3 | async-start | bytes 4194304 | tf_op jit(solution)/shard_map/all_to_all | solution.py:202
  199.2 2.1 collective-permute-start.13
  199.4 13.0 %collective-permute-start.14 = (f32[8,128]{1,0:T(8,128)S(1)}, f32[8,128]{1,0:T(8,128)S(1)}, u32[]{:S(2)}, u32[]{:S(2)}) collective-permute-start(f32[8,128]{1,0:T(8,128)S(1)} %get-tuple-element.78), channel_id=1, source_target_pairs={{0,2},{1,3},{2,0},{3,1},{4,6},{5,7},{6,4},{7,5},{8,10},{9,11},{10,... | collective-permute-start | bytes 12296 | tf_op jit(solution)/shard_map/ppermute | solution.py:199
  201.0 11.9 %collective-permute-start.15 = (f32[8,128]{1,0:T(8,128)S(1)}, f32[8,128]{1,0:T(8,128)S(1)}, u32[]{:S(2)}, u32[]{:S(2)}) collective-permute-start(f32[8,128]{1,0:T(8,128)S(1)} %get-tuple-element.78), channel_id=1, source_target_pairs={{0,3},{1,2},{2,1},{3,0},{4,7},{5,6},{6,5},{7,4},{8,11},{9,10},{10,... | collective-permute-start | bytes 12296 | tf_op jit(solution)/shard_map/ppermute | solution.py:199
  212.9 9.3 %copy-start.13 = (f32[512,512]{1,0:T(8,128)S(1)}, f32[512,512]{1,0:T(8,128)}, u32[]{:S(2)}) copy-start(f32[512,512]{1,0:T(8,128)} %copy-done.12) | copy-start | bytes 3145732
  212.9 9.3 %copy-start.15 = (f32[512,512]{1,0:T(8,128)S(1)}, f32[512,512]{1,0:T(8,128)}, u32[]{:S(2)}) copy-start(f32[512,512]{1,0:T(8,128)} %copy-done.14) | copy-start | bytes 3145732
  212.9 9.3 %copy-start.17 = (f32[512,512]{1,0:T(8,128)S(1)}, f32[512,512]{1,0:T(8,128)}, u32[]{:S(2)}) copy-start(f32[512,512]{1,0:T(8,128)} %copy-done.16) | copy-start | bytes 3145732
  212.9 9.2 %collective-permute-start.16 = (f32[8,128]{1,0:T(8,128)S(1)}, f32[8,128]{1,0:T(8,128)S(1)}, u32[]{:S(2)}, u32[]{:S(2)}) collective-permute-start(f32[8,128]{1,0:T(8,128)S(1)} %add_add_fusion.1), channel_id=1, source_target_pairs={{0,4},{1,5},{2,6},{3,7},{4,0},{5,1},{6,2},{7,3},{8,12},{9,13},{10,... | collective-permute-start | bytes 12296 | tf_op jit(solution)/shard_map/ppermute | solution.py:199
  214.2 8.0 %collective-permute-start.17 = (f32[8,128]{1,0:T(8,128)S(1)}, f32[8,128]{1,0:T(8,128)S(1)}, u32[]{:S(2)}, u32[]{:S(2)}) collective-permute-start(f32[8,128]{1,0:T(8,128)S(1)} %add_add_fusion.1), channel_id=1, source_target_pairs={{0,8},{1,9},{2,10},{3,11},{4,12},{5,13},{6,14},{7,15},{8,0},{9,1},... | collective-permute-start | bytes 12296 | tf_op jit(solution)/shard_map/ppermute | solution.py:199
  214.2 8.0 %collective-permute-start.18 = (f32[8,128]{1,0:T(8,128)S(1)}, f32[8,128]{1,0:T(8,128)S(1)}, u32[]{:S(2)}, u32[]{:S(2)}) collective-permute-start(f32[8,128]{1,0:T(8,128)S(1)} %add_add_fusion.1), channel_id=1, source_target_pairs={{0,12},{1,13},{2,14},{3,15},{4,8},{5,9},{6,10},{7,11},{8,4},{9,5},... | collective-permute-start | bytes 12296 | tf_op jit(solution)/shard_map/ppermute | solution.py:199
  (21 other events, 42.7 us)

commit v7 on v6

--- a/solution.py
+++ b/solution.py
@@ -10,7 +10,9 @@
 
 
 BLK = 128
+TERMS = 16
 CHUNKS = 4
+PARTS = 2
 F32 = jnp.float32
 BF16 = jnp.bfloat16
 VMEM = pl.BlockSpec(memory_space=pltpu.VMEM)
@@ -49,7 +51,8 @@
     slot, rank = places(inst, owner_ref, heads)
     half = heads // 2
     mine = (slot >= half) == (lax.axis_index("loc") >= half)
-    return mine, jnp.where(slot >= half, slot - half, slot), rank
+    head = jnp.where(slot >= half, slot - half, slot)
+    return mine, jnp.where(mine, head, head ^ (half // 2)), rank
 
 
 def one_hot_back(pos, size):
@@ -85,8 +88,15 @@
     return (block.astype(F32) * pattern_ref[0, row, column].astype(F32)).astype(BF16)
 
 
-def piece_kernel(w_ref, pattern_ref, *out_refs):
+def piece_kernel(w_ref, pattern_ref, weight_ref, *out_refs):
     rows, channels = out_refs[0].shape
+    high = weight_ref[...].astype(BF16)
+    rest = weight_ref[...] - high.astype(F32)
+    middle = rest.astype(BF16)
+    low = (rest - middle.astype(F32)).astype(BF16)
+    line = lax.broadcasted_iota(jnp.int32, (TERMS, channels), 0)
+    terms = jnp.where(line == 0, high.astype(F32), jnp.where(line == 1, middle.astype(F32), 0.0))
+    out_refs[-1][rows:, :] = jnp.where(line == 2, low.astype(F32), terms).astype(BF16)
     for chunk, out_ref in enumerate(out_refs):
         first = (lax.axis_index("grp") * len(out_refs) + chunk) * (rows // BLK)
         for i in range(rows // BLK):
@@ -111,21 +121,23 @@
     return pl.ds(pl.multiple_of(first * deep, deep), deep)
 
 
-def far_res_kernel(width, x_ref, weight_ref, *refs):
+def far_res_kernel(width, x_ref, *refs):
     eff_refs, res_ref = refs[:-1], refs[-1]
     deep = eff_refs[0].shape[0]
-    predicted = dot(x_ref[:, piece_columns(0, deep)], eff_refs[0][...])
+    predicted = dot(x_ref[:, piece_columns(0, deep)], eff_refs[0][:deep])
     for number in range(1, len(eff_refs)):
-        predicted += dot(x_ref[:, piece_columns(number, deep)], eff_refs[number][...])
+        predicted += dot(x_ref[:, piece_columns(number, deep)], eff_refs[number][:deep])
     misfit = predicted - x_ref[:, width:].astype(F32)
-    res_ref[...] = (weight_ref[...] * misfit).astype(BF16)
+    terms = eff_refs[CHUNKS - 1][deep:].astype(F32)
+    weight = terms[0:1] + terms[1:2] + terms[2:3]
+    res_ref[...] = (weight * misfit).astype(BF16)
 
 
 def far_grad_kernel(res_ref, *refs):
     eff_refs, grad_ref = refs[:-1], refs[-1]
     deep = eff_refs[0].shape[0]
     for number, eff_ref in enumerate(eff_refs):
-        grad = dot(res_ref[...], eff_ref[...], 1, 1)
+        grad = dot(res_ref[...], eff_ref[:deep], 1, 1)
         grad_ref[:, piece_columns(number, deep)] = grad.astype(BF16)
 
 
@@ -140,10 +152,11 @@
     out_ref[...] = dot(x_ref[...], res_ref[...], 0, 0).astype(BF16)
 
 
-def raw_kernel(first, x_ref, res_ref, far_ref, pattern_ref, before_ref, raw_ref, square_ref):
+def raw_kernel(first, x_ref, res_ref, far_ref, out_ref, pattern_ref, before_ref, raw_ref, square_ref):
     step = pl.program_id(0)
     size, channels = raw_ref.shape
     raw = dot(x_ref[...], res_ref[...], 0, 0) + far_ref[...].astype(F32)
+    raw = raw + out_ref[...].astype(F32)
 
     @pl.when(step == 0)
     def _():
@@ -158,8 +171,12 @@
             square_ref[...] += jnp.sum((part * part).reshape(BLK // 8, 8, BLK), 0)
 
 
-def scale_kernel(limit, parts, *refs):
-    raw_refs, square_ref, out_ref = refs[:parts], refs[parts], refs[parts + 1]
+def far_place_kernel(back_ref, got_ref, out_ref):
+    out_ref[...] = dot(back_ref[...], got_ref[...]).astype(BF16)
+
+
+def finish_kernel(limit, parts, back_ref, got_ref, far_ref, square_ref, *refs):
+    raw_refs, (out_ref, head_ref) = refs[:parts], refs[parts:]
     squares = jnp.sum(square_ref[...], keepdims=True)
     factor = jnp.minimum(1.0, limit / jnp.sqrt(squares + 1e-06))
     step = pl.program_id(0)
@@ -168,14 +185,8 @@
 
         @pl.when(step // per == part)
         def _():
-            out_ref[...] = (raw_refs[part][...] * factor)[None]
-
-
-def far_place_kernel(back_ref, got_ref, out_ref):
-    out_ref[...] = dot(back_ref[...], got_ref[...]).astype(BF16)
-
-
-def place_back_kernel(back_ref, got_ref, far_ref, out_ref):
+            head_ref[...] = (raw_refs[part][...] * factor)[None]
+
     out = dot(back_ref[...], got_ref[...]) + far_ref[...].astype(F32)
     out_ref[...] = out.astype(BF16)
 
@@ -188,12 +199,13 @@
     capacity = 2 * rows // heads
     half = members // 2
     placed = half * capacity
+    apart = half + half // 2
     wide = width + channels
     inst = obs_inst.reshape(1, rows)
     halves = [list(range(half)), list(range(half, members))]
 
     def partner(x):
-        return lax.ppermute(x, "loc", [(i, i ^ half) for i in range(members)])
+        return lax.ppermute(x, "loc", [(i, i ^ apart) for i in range(members)])
 
     def hop(x, distance):
         return lax.ppermute(x, "loc", [(i, i ^ distance) for i in range(members)])
@@ -225,14 +237,16 @@
     head_weights, far_send = lax.optimization_barrier((head_weights, far_send))
     pieces = pl.pallas_call(
         piece_kernel,
-        in_specs=[VMEM, SMEM],
+        in_specs=[VMEM, SMEM, VMEM],
         out_specs=[VMEM] * CHUNKS,
-        out_shape=[jax.ShapeDtypeStruct((deep, channels), BF16)] * CHUNKS,
+        out_shape=[
+            jax.ShapeDtypeStruct((deep + (TERMS if last else 0), channels), BF16)
+            for last in [False] * (CHUNKS - 1) + [True]
+        ],
         compiler_params=STREAM,
         cost_estimate=cost(CHUNKS * deep * channels, 4 * CHUNKS * deep * channels),
         name="piece",
-    )(head_weights, block_pattern)
-    far_weight = partner(error_weight)
+    )(head_weights, block_pattern, error_weight)
     crossed = [partner(piece) for piece in pieces]
     crossed[0], near_send = lax.optimization_barrier((crossed[0], near_send))
     swapped = [[piece] for piece in crossed]
@@ -244,12 +258,9 @@
     far_eff = [swapped[chunk][number] for number in range(groups) for chunk in range(CHUNKS)]
 
     far_x = in_half(far_send)
-    last = swapped[-1][groups // 2 :]
-    swapped[-1] = swapped[-1][: groups // 2]
-    near_send, far_x, swapped, far_weight = lax.optimization_barrier(
-        (near_send, far_x, swapped, far_weight)
-    )
-    swapped[-1] = swapped[-1] + last
+    early = swapped[: CHUNKS // 4]
+    near_send, far_x, early, crossed = lax.optimization_barrier((near_send, far_x, early, crossed))
+    swapped[: CHUNKS // 4] = early
     far_eff = [swapped[chunk][number] for number in range(groups) for chunk in range(CHUNKS)]
     near_x = in_half(near_send)
 
@@ -278,22 +289,22 @@
     size = placed // 2
     row_spec = pl.BlockSpec((size, wide), lambda i: (i, 0))
     res_spec = pl.BlockSpec((size, channels), lambda i: (i, 0))
-    far_specs = [whole((deep, channels))] * len(far_eff)
+    far_specs = [whole(piece.shape) for piece in far_eff]
     far_res = pl.pallas_call(
         functools.partial(far_res_kernel, width),
         grid=(2,),
-        in_specs=[row_spec, whole((1, channels))] + far_specs,
+        in_specs=[row_spec] + far_specs,
         out_specs=res_spec,
         out_shape=jax.ShapeDtypeStruct((placed, channels), BF16),
         compiler_params=SMALL,
         cost_estimate=cost(2 * placed * width * channels, 2 * placed * wide),
         name="far_res",
-    )(far_x, far_weight, *far_eff)
+    )(far_x, *far_eff)
 
     tall = 256
-    steps = width // (CHUNKS * tall)
+    steps = width // (PARTS * tall)
     far_raw = []
-    for chunk in range(CHUNKS):
+    for chunk in range(PARTS):
         part = pl.pallas_call(
             far_raw_kernel,
             grid=(steps,),
@@ -302,14 +313,19 @@
                 whole((placed, channels)),
             ],
             out_specs=pl.BlockSpec((tall, channels), lambda i: (i, 0)),
-            out_shape=jax.ShapeDtypeStruct((width // CHUNKS, channels), BF16),
+            out_shape=jax.ShapeDtypeStruct((width // PARTS, channels), BF16),
             compiler_params=SMALL,
-            cost_estimate=cost(2 * placed * width * channels // CHUNKS, 2 * width * channels),
+            cost_estimate=cost(2 * placed * width * channels // PARTS, 2 * width * channels),
             name="far_raw",
         )(far_x, far_res)
         far_raw.append(part)
     sent = far_raw
-    far_raw = [partner(part) for part in sent]
+    bit = half // 2
+    inner = [i for i in range(members) if (i // bit) % 2 != (i // half) % 2]
+    outer = [i for i in range(members) if i not in inner]
+    far_raw = [lax.ppermute(part, "loc", [(i, i ^ apart) for i in inner]) for part in sent]
+    near_x, held = lax.optimization_barrier((near_x, sent))
+    far_out = [lax.ppermute(part, "loc", [(i, i ^ apart) for i in outer]) for part in held]
 
     grad_spec = pl.BlockSpec((size, width), lambda i: (i, 0))
     far_grad = pl.pallas_call(
@@ -338,7 +354,6 @@
         name="near_head",
     )(near_x, effective, error_weight)
     near_grad, far_got = lax.optimization_barrier((near_grad, far_got))
-    near_got = in_half(near_grad)
 
     def column_spec(deep):
         return pl.BlockSpec((deep, width // cut), lambda i: (0, i))
@@ -353,9 +368,10 @@
         cost_estimate=cost(2 * rows * placed * width, 4 * placed * width),
         name="far_place",
     )(far_back, far_got)
-    far_raw[0], far_placed = lax.optimization_barrier((far_raw[0], far_placed))
+    near_grad, far_placed = lax.optimization_barrier((near_grad, far_placed))
+    near_got = in_half(near_grad)
     raw_grad, squares = [], jnp.zeros((8, 128), F32)
-    for chunk in range(CHUNKS):
+    for chunk in range(PARTS):
         part, squares = pl.pallas_call(
             functools.partial(raw_kernel, chunk * steps * (tall // BLK)),
             grid=(steps,),
@@ -363,54 +379,51 @@
                 pl.BlockSpec((placed, tall), lambda i, chunk=chunk: (0, chunk * steps + i)),
                 whole((placed, channels)),
                 pl.BlockSpec((tall, channels), lambda i: (i, 0)),
+                pl.BlockSpec((tall, channels), lambda i: (i, 0)),
                 SMEM,
                 whole((8, 128)),
             ],
             out_specs=[pl.BlockSpec((tall, channels), lambda i: (i, 0)), whole((8, 128))],
             out_shape=[
-                jax.ShapeDtypeStruct((width // CHUNKS, channels), F32),
+                jax.ShapeDtypeStruct((width // PARTS, channels), F32),
                 jax.ShapeDtypeStruct((8, 128), F32),
             ],
             compiler_params=SMALL,
             cost_estimate=cost(1 << 40, 1 << 30),
             name="raw",
-        )(near_x, near_res, far_raw[chunk], block_pattern, squares)
+        )(near_x, near_res, far_raw[chunk], far_out[chunk], block_pattern, squares)
         raw_grad.append(part)
     step = 1
     while step < members:
         ways = min(4, members // step)
         squares = squares + sum(hop(squares, step * way) for way in range(1, ways))
-        if step == 1:
-            near_got, squares = lax.optimization_barrier((near_got, squares))
         step *= ways
 
-    latent_grad = pl.pallas_call(
-        place_back_kernel,
+    near_got, squares = lax.optimization_barrier((near_got, squares))
+
+    def raw_spec(part):
+        low = part * (cut // PARTS)
+        return pl.BlockSpec(
+            (width // cut, channels), lambda i: (jnp.clip(i - low, 0, cut // PARTS - 1), 0)
+        )
+
+    latent_grad, head_grad = pl.pallas_call(
+        functools.partial(finish_kernel, math.sqrt(heads * width * channels), PARTS),
         grid=(cut,),
-        in_specs=[whole((rows, placed)), column_spec(placed), column_spec(rows)],
-        out_specs=column_spec(rows),
-        out_shape=jax.ShapeDtypeStruct((rows, width), BF16),
-        compiler_params=SMALL,
-        cost_estimate=cost(2 * rows * placed * width, 4 * placed * width),
-        name="place_back",
-    )(near_back, near_got, far_placed)
-    latent_grad, squares = lax.optimization_barrier((latent_grad, squares))
-    def raw_spec(part):
-        low = part * (cut // CHUNKS)
-        return pl.BlockSpec(
-            (width // cut, channels), lambda i: (jnp.clip(i - low, 0, cut // CHUNKS - 1), 0)
-        )
-
-    head_grad = pl.pallas_call(
-        functools.partial(scale_kernel, math.sqrt(heads * width * channels), CHUNKS),
-        grid=(cut,),
-        in_specs=[raw_spec(part) for part in range(CHUNKS)] + [whole((8, 128))],
-        out_specs=pl.BlockSpec((1, width // cut, channels), lambda i: (0, i, 0)),
-        out_shape=jax.ShapeDtypeStruct((1, width, channels), F32),
-        compiler_params=SMALL,
-        cost_estimate=cost(width * channels, 8 * width * channels),
-        name="scale",
-    )(*raw_grad, squares)
+        in_specs=[whole((rows, placed)), column_spec(placed), column_spec(rows), whole((8, 128))]
+        + [raw_spec(part) for part in range(PARTS)],
+        out_specs=[
+            column_spec(rows),
+            pl.BlockSpec((1, width // cut, channels), lambda i: (0, i, 0)),
+        ],
+        out_shape=[
+            jax.ShapeDtypeStruct((rows, width), BF16),
+            jax.ShapeDtypeStruct((1, width, channels), F32),
+        ],
+        compiler_params=STREAM,
+        cost_estimate=cost(2 * rows * placed * width, 8 * width * channels),
+        name="finish",
+    )(near_back, near_got, far_placed, squares, *raw_grad)
     return (latent_grad, head_grad)
 
 

time: 227 us -> 215 us (0.947)
  waiting for transfers between devices: 115 us -> 99.5 us
  starting transfers between devices: 47 us -> 55.5 us
  local copies, waits for them, and re-layouts: 13.9 us -> 9.94 us
    all_to_all x4, waiting for transfers between devices: 72.3 us -> 15.6 us  [in_half(): lax.all_to_all(x, 'loc', split_axis=0, concat_axis=0, tiled=True, axis_in...]
    ppermute x9 -> x8, waiting for transfers between devices: 31.4 us -> 65.5 us  [the longest x4 38.8 us: partner(): return lax.ppermute(x, 'loc', [(i, i ^ apart) for i in range(members)])]
    ppermute x4, waiting for transfers between devices: 0.29 us -> 9.94 us  [per_device(): lax.ppermute(x, 'grp', swap)]
    ppermute x9 -> x8, starting transfers between devices: 12.5 us -> 17.5 us  [the longest x2 7.44 us: per_device(): lax.ppermute(part, 'loc', [(i, i ^ apart) for i in outer])]
    ppermute x6, starting transfers between devices: 5.75 us -> 9.69 us  [hop(): return lax.ppermute(x, 'loc', [(i, i ^ distance) for i in range(members)])]
    unnamed x61 -> x37, local copies, waits for them, and re-layouts: 13.9 us -> 9.94 us
    ppermute x6, waiting for transfers between devices: 11.5 us -> 8.52 us  [hop(): return lax.ppermute(x, 'loc', [(i, i ^ distance) for i in range(members)])]
    pallas_call x4 -> x2, Pallas kernels: 5.71 us -> 5 us  [per_device(): pl.pallas_call(far_raw_kernel, grid=(steps,), in_specs=[pl.BlockSpec((pla...]
  transfers between devices with their start and end apart: 23 -> 22, of which waited for: 9 -> 13; matrix products, arithmetic and copies ran while one was open for 0% -> 1% of each run, Pallas kernels for 18% -> 16%
where the time goes in v7:
time: 215 us; the launch traced here: 214 us
  waiting for transfers between devices  99.5 us (46%)
  starting transfers between devices  55.5 us (26%)
  Pallas kernels  47.2 us (22%)
  local copies, waits for them, and re-layouts  9.94 us (5%)
    ppermute x4, waiting for transfers between devices, partner(): return lax.ppermute(x, 'loc', [(i, i ^ apart) for i in range(members)])  38.8 us
    ppermute x2, waiting for transfers between devices, per_device(): lax.ppermute(part, 'loc', [(i, i ^ apart) for i in outer])  26.6 us
    all_to_all x4, starting transfers between devices, in_half(): lax.all_to_all(x, 'loc', split_axis=0, concat_axis=0, tiled=True, axis_in...  24.4 us
    all_to_all x4, waiting for transfers between devices, in_half(): lax.all_to_all(x, 'loc', split_axis=0, concat_axis=0, tiled=True, axis_in...  15.6 us
    pallas_call x2, Pallas kernels, prep(): pl.pallas_call(functools.partial(prep_kernel, heads, capacity, near), gri...  10.4 us
    ppermute x4, waiting for transfers between devices, per_device(): lax.ppermute(x, 'grp', swap)  9.94 us
    unnamed x37, local copies, waits for them, and re-layouts  9.94 us
    ppermute x6, starting transfers between devices, hop(): return lax.ppermute(x, 'loc', [(i, i ^ distance) for i in range(members)])  9.69 us
  transfers between devices with their start and end apart: 22, of which 13 were waited for; matrix products, arithmetic and copies ran while one was open for 1% of the time, Pallas kernels for 16%

profile of v7, /device:TPU:1, one launch (start us, length us, event | category | flops | bytes accessed | tf_op | source)
XLA Modules:
  0.0 213.6 jit_solution(12994555203874036008)
XLA Ops:
  0.6 5.2 %prep_far.1 = bf16[512,2560]{1,0:T(8,128)(2,1)} custom-call(s32[1,512]{1,0:T(1,128)} %bitcast.12, s32[16]{0:T(128)} %owner_ref.5, bf16[512,2048]{1,0:T(8,128)(2,1)} %x_ref.3, bf16[512,512]{1,0:T(8,128)(2,1)} %t_ref.3), custom_call_target="tpu_custom_call" | custom-call | flops 1342177280 | bytes 5242880 | tf_op jit(solution)/shard_map/prep_far/pallas_call | solution.py:221
  5.9 5.4 %all-to-all-start = ((bf16[8,64,2560]{2,1,0:T(8,128)(2,1)}), bf16[8,64,2560]{2,1,0:T(8,128)(2,1)S(1)}, u32[]{:S(2)}, u32[]{:S(2)}) async-start(bf16[8,64,2560]{2,1,0:T(8,128)(2,1)} %bitcast.16), calls=%async_computation | async-start | bytes 5242880 | tf_op jit(solution)/shard_map/all_to_all | solution.py:214
  12.0 2.7 %piece.1 = (bf16[256,512]{1,0:T(8,128)(2,1)}, bf16[256,512]{1,0:T(8,128)(2,1)}, bf16[256,512]{1,0:T(8,128)(2,1)}, bf16[272,512]{1,0:T(8,128)(2,1)}) custom-call(bf16[1,2048,512]{2,1,0:T(8,128)(2,1)} %w_ref.1, s32[1,16,4]{2,1,0:T(8,128)} %copy.9.pattern_ref, f32[1,512]{1,0:T(1,128)} %weight_ref.3), custom_call_target="tpu_custom_call" | custom-call | flops 524288 | bytes 2097152 | tf_op jit(solution)/shard_map/piece/pallas_call | solution.py:238
  14.7 3.4 %collective-permute-start = (bf16[256,512]{1,0:T(8,128)(2,1)}, bf16[256,512]{1,0:T(8,128)(2,1)S(1)}, u32[]{:S(2)}, u32[]{:S(2)}) collective-permute-start(bf16[256,512]{1,0:T(8,128)(2,1)} %get-tuple-element.37), channel_id=1, source_target_pairs={{0,12},{1,13},{2,14},{3,15},{4,8},{5,9},{6,10},{7,11},{8,4},{9,5},... | collective-permute-start | bytes 786440 | tf_op jit(solution)/shard_map/ppermute | solution.py:208
  18.1 3.2 %collective-permute-start.3 = (bf16[256,512]{1,0:T(8,128)(2,1)}, bf16[256,512]{1,0:T(8,128)(2,1)S(1)}, u32[]{:S(2)}, u32[]{:S(2)}) collective-permute-start(bf16[256,512]{1,0:T(8,128)(2,1)} %get-tuple-element.42), channel_id=1, source_target_pairs={{0,12},{1,13},{2,14},{3,15},{4,8},{5,9},{6,10},{7,11},{8,4},{9,5},... | collective-permute-start | bytes 786440 | tf_op jit(solution)/shard_map/ppermute | solution.py:208
  21.4 5.2 %prep_near.1 = bf16[512,2560]{1,0:T(8,128)(2,1)} custom-call(s32[1,512]{1,0:T(1,128)} %bitcast.13, s32[16]{0:T(128)} %owner_ref.5, bf16[512,2048]{1,0:T(8,128)(2,1)} %x_ref.3, bf16[512,512]{1,0:T(8,128)(2,1)} %t_ref.3), custom_call_target="tpu_custom_call" | custom-call | flops 1342177280 | bytes 5242880 | tf_op jit(solution)/shard_map/prep_near/pallas_call | solution.py:221
  26.6 22.8 %collective-permute-done.refs_0_ = bf16[256,512]{1,0:T(8,128)(2,1)S(1)} collective-permute-done((bf16[256,512]{1,0:T(8,128)(2,1)}, bf16[256,512]{1,0:T(8,128)(2,1)S(1)}, u32[]{:S(2)}, u32[]{:S(2)}) %collective-permute-start) | collective-permute-done | bytes 262176 | tf_op jit(solution)/shard_map/ppermute | solution.py:208
  50.6 4.4 %collective-permute-done.2.refs_1_ = bf16[256,512]{1,0:T(8,128)(2,1)S(1)} collective-permute-done((bf16[256,512]{1,0:T(8,128)(2,1)}, bf16[256,512]{1,0:T(8,128)(2,1)S(1)}, u32[]{:S(2)}, u32[]{:S(2)}) %collective-permute-start.2) | collective-permute-done | bytes 262176 | tf_op jit(solution)/shard_map/ppermute | solution.py:208
  55.0 5.6 %collective-permute-done.3.refs_2_ = bf16[256,512]{1,0:T(8,128)(2,1)S(1)} collective-permute-done((bf16[256,512]{1,0:T(8,128)(2,1)}, bf16[256,512]{1,0:T(8,128)(2,1)S(1)}, u32[]{:S(2)}, u32[]{:S(2)}) %collective-permute-start.3) | collective-permute-done | bytes 262176 | tf_op jit(solution)/shard_map/ppermute | solution.py:208
  60.6 6.0 %collective-permute-done.4.refs_3_ = bf16[272,512]{1,0:T(8,128)(2,1)S(1)} collective-permute-done((bf16[272,512]{1,0:T(8,128)(2,1)}, bf16[272,512]{1,0:T(8,128)(2,1)S(1)}, u32[]{:S(2)}, u32[]{:S(2)}) %collective-permute-start.4) | collective-permute-done | bytes 278560 | tf_op jit(solution)/shard_map/ppermute | solution.py:208
  67.3 5.3 %all-to-all-start.1 = ((bf16[8,64,2560]{2,1,0:T(8,128)(2,1)}), bf16[8,64,2560]{2,1,0:T(8,128)(2,1)}, u32[]{:S(2)}, u32[]{:S(2)}) async-start(bf16[8,64,2560]{2,1,0:T(8,128)(2,1)} %bitcast.15), calls=%async_computation.1 | async-start | bytes 5242880 | tf_op jit(solution)/shard_map/all_to_all | solution.py:214
  82.1 4.3 %collective-permute-done.5.refs_5_ = bf16[256,512]{1,0:T(8,128)(2,1)S(1)} collective-permute-done((bf16[256,512]{1,0:T(8,128)(2,1)S(1)}, bf16[256,512]{1,0:T(8,128)(2,1)S(1)}, u32[]{:S(2)}, u32[]{:S(2)}) %collective-permute-start.5) | collective-permute-done | bytes 262176 | tf_op jit(solution)/shard_map/ppermute | solution.py:256
  86.4 5.6 %collective-permute-done.6.refs_6_ = bf16[256,512]{1,0:T(8,128)(2,1)S(1)} collective-permute-done((bf16[256,512]{1,0:T(8,128)(2,1)}, bf16[256,512]{1,0:T(8,128)(2,1)S(1)}, u32[]{:S(2)}, u32[]{:S(2)}) %collective-permute-start.6) | collective-permute-done | bytes 262176 | tf_op jit(solution)/shard_map/ppermute | solution.py:256
  93.5 2.5 %far_raw.2 = bf16[1024,512]{1,0:T(8,128)(2,1)} custom-call(bf16[512,2560]{1,0:T(8,128)(2,1)S(1)} %bitcast.10, bf16[512,512]{1,0:T(8,128)(2,1)S(1)} %far_res.1.res_ref), custom_call_target="tpu_custom_call" | custom-call | flops 536870912 | bytes 2097152 | tf_op jit(solution)/shard_map/far_raw/pallas_call | solution.py:308
  97.7 2.5 %far_raw.3 = bf16[1024,512]{1,0:T(8,128)(2,1)} custom-call(bf16[512,2560]{1,0:T(8,128)(2,1)S(1)} %bitcast.11, bf16[512,512]{1,0:T(8,128)(2,1)S(1)} %far_res.1.res_ref), custom_call_target="tpu_custom_call" | custom-call | flops 536870912 | bytes 2097152 | tf_op jit(solution)/shard_map/far_raw/pallas_call | solution.py:308
  101.8 2.5 %far_grad.1 = bf16[512,2048]{1,0:T(8,128)(2,1)} custom-call(bf16[512,512]{1,0:T(8,128)(2,1)S(1)} %far_res.1.res_ref, bf16[256,512]{1,0:T(8,128)(2,1)S(1)} %collective-permute-done.refs_0_, bf16[256,512]{1,0:T(8,128)(2,1)S(1)} %collective-permute-done.2.refs_1_, bf16[256,512]{1,0:T(8,128)(2,1)S(1)} %copy-done.7, ...), custom_call_target="tpu_custom_call" | custom-call | flops 1073741824 | bytes 2621440 | tf_op jit(solution)/shard_map/far_grad/pallas_call | solution.py:331
  104.4 7.4 %all-to-all-start.2 = ((bf16[8,64,2048]{2,1,0:T(8,128)(2,1)}), bf16[8,64,2048]{2,1,0:T(8,128)(2,1)}, u32[]{:S(2)}, u32[]{:S(2)}) async-start(bf16[8,64,2048]{2,1,0:T(8,128)(2,1)} %bitcast.5), calls=%async_computation.2 | async-start | bytes 4194304 | tf_op jit(solution)/shard_map/all_to_all | solution.py:214
  111.8 4.2 %collective-permute-start.11 = (bf16[1024,512]{1,0:T(8,128)(2,1)}, bf16[1024,512]{1,0:T(8,128)(2,1)}, u32[]{:S(2)}, u32[]{:S(2)}) collective-permute-start(bf16[1024,512]{1,0:T(8,128)(2,1)} %far_raw.2), channel_id=1, source_target_pairs={{0,12},{1,13},{2,14},{3,15},{12,0},{13,1},{14,2},{15,3},{16,28},{1... | collective-permute-start | bytes 3145736 | tf_op jit(solution)/shard_map/ppermute | solution.py:328
  116.1 5.0 %near_head.1 = (bf16[512,2048]{1,0:T(8,128)(2,1)}, bf16[512,512]{1,0:T(8,128)(2,1)S(1)}) custom-call(bf16[512,2560]{1,0:T(8,128)(2,1)} %bitcast.4.x_ref, bf16[2048,512]{1,0:T(8,128)(2,1)S(1)} %copy-done.3, f32[1,512]{1,0:T(1,128)S(1)} %copy-done.15), custom_call_target="tpu_custom_call" | custom-call | flops 1099511627776 | bytes 1073741824 | tf_op jit(solution)/shard_map/near_head/pallas_call | solution.py:343
  121.1 15.6 %all-to-all-done.2 = bf16[8,64,2048]{2,1,0:T(8,128)(2,1)} async-done(((bf16[8,64,2048]{2,1,0:T(8,128)(2,1)}), bf16[8,64,2048]{2,1,0:T(8,128)(2,1)}, u32[]{:S(2)}, u32[]{:S(2)}) %all-to-all-start.2) | async-done | bytes 2097184 | tf_op jit(solution)/shard_map/all_to_all | solution.py:214
  136.7 3.2 %collective-permute-start.9 = (bf16[1024,512]{1,0:T(8,128)(2,1)}, bf16[1024,512]{1,0:T(8,128)(2,1)}, u32[]{:S(2)}, u32[]{:S(2)}) collective-permute-start(bf16[1024,512]{1,0:T(8,128)(2,1)} %far_raw.3), channel_id=1, source_target_pairs={{0,12},{1,13},{2,14},{3,15},{12,0},{13,1},{14,2},{15,3},{16,28},{1... | collective-permute-start | bytes 3145736 | tf_op jit(solution)/shard_map/ppermute | solution.py:328
  140.0 3.5 %far_place.1.far_ref = bf16[512,2048]{1,0:T(8,128)(2,1)S(1)} custom-call(bf16[512,512]{1,0:T(8,128)(2,1)S(1)} %copy-done.12, bf16[512,2048]{1,0:T(8,128)(2,1)} %bitcast.6.got_ref), custom_call_target="tpu_custom_call" | custom-call | flops 1073741824 | bytes 4194304 | tf_op jit(solution)/shard_map/far_place/pallas_call | solution.py:361
  144.9 6.2 %all-to-all-start.3 = ((bf16[8,64,2048]{2,1,0:T(8,128)(2,1)}), bf16[8,64,2048]{2,1,0:T(8,128)(2,1)}, u32[]{:S(2)}, u32[]{:S(2)}) async-start(bf16[8,64,2048]{2,1,0:T(8,128)(2,1)} %bitcast.7), calls=%async_computation.3 | async-start | bytes 4194304 | tf_op jit(solution)/shard_map/all_to_all | solution.py:214
  151.1 9.2 %collective-permute-done.11.out_ref = bf16[1024,512]{1,0:T(8,128)(2,1)} collective-permute-done((bf16[1024,512]{1,0:T(8,128)(2,1)}, bf16[1024,512]{1,0:T(8,128)(2,1)}, u32[]{:S(2)}, u32[]{:S(2)}) %collective-permute-start.11) | collective-permute-done | bytes 1048608 | tf_op jit(solution)/shard_map/ppermute | solution.py:328
  160.2 3.6 %raw.2 = (f32[1024,512]{1,0:T(8,128)S(1)}, f32[8,128]{1,0:T(8,128)S(1)}) custom-call(bf16[512,2560]{1,0:T(8,128)(2,1)} %bitcast.4.x_ref, bf16[512,512]{1,0:T(8,128)(2,1)S(1)} %get-tuple-element.60.res_ref, bf16[1024,512]{1,0:T(8,128)(2,1)} %collective-permute-done.10.far_ref, bf16[1024,512]{1,0:T(8,128)(2,1)} %collective-permute-done.11.out_ref, ...), custom_call_target="tpu_custom_call" | custom-call | flops 1099511627776 | bytes 1073741824 | tf_op jit(solution)/shard_map/raw/pallas_call | solution.py:375
  165.2 17.5 %collective-permute-done.9.out_ref = bf16[1024,512]{1,0:T(8,128)(2,1)} collective-permute-done((bf16[1024,512]{1,0:T(8,128)(2,1)}, bf16[1024,512]{1,0:T(8,128)(2,1)}, u32[]{:S(2)}, u32[]{:S(2)}) %collective-permute-start.9) | collective-permute-done | bytes 1048608 | tf_op jit(solution)/shard_map/ppermute | solution.py:328
  182.7 3.6 %raw.3 = (f32[1024,512]{1,0:T(8,128)S(1)}, f32[8,128]{1,0:T(8,128)S(1)}) custom-call(bf16[512,2560]{1,0:T(8,128)(2,1)} %bitcast.4.x_ref, bf16[512,512]{1,0:T(8,128)(2,1)S(1)} %get-tuple-element.60.res_ref, bf16[1024,512]{1,0:T(8,128)(2,1)} %collective-permute-done.8.far_ref, bf16[1024,512]{1,0:T(8,128)(2,1)} %collective-permute-done.9.out_ref, ...), custom_call_target="tpu_custom_call" | custom-call | flops 1099511627776 | bytes 1073741824 | tf_op jit(solution)/shard_map/raw/pallas_call | solution.py:375
  187.7 2.4 %collective-permute-start.14 = (f32[8,128]{1,0:T(8,128)S(1)}, f32[8,128]{1,0:T(8,128)S(1)}, u32[]{:S(2)}, u32[]{:S(2)}) collective-permute-start(f32[8,128]{1,0:T(8,128)S(1)} %get-tuple-element.64), channel_id=1, source_target_pairs={{0,3},{1,2},{2,1},{3,0},{4,7},{5,6},{6,5},{7,4},{8,11},{9,10},{10,... | collective-permute-start | bytes 12296 | tf_op jit(solution)/shard_map/ppermute | solution.py:211
  192.5 3.2 %collective-permute-done.13 = f32[8,128]{1,0:T(8,128)S(1)} collective-permute-done((f32[8,128]{1,0:T(8,128)S(1)}, f32[8,128]{1,0:T(8,128)S(1)}, u32[]{:S(2)}, u32[]{:S(2)}) %collective-permute-start.13) | collective-permute-done | bytes 4128 | tf_op jit(solution)/shard_map/ppermute | solution.py:211
  196.9 5.6 %collective-permute-start.16 = (f32[8,128]{1,0:T(8,128)S(1)}, f32[8,128]{1,0:T(8,128)S(1)}, u32[]{:S(2)}, u32[]{:S(2)}) collective-permute-start(f32[8,128]{1,0:T(8,128)S(1)} %add_add_fusion.1), channel_id=1, source_target_pairs={{0,8},{1,9},{2,10},{3,11},{4,12},{5,13},{6,14},{7,15},{8,0},{9,1},... | collective-permute-start | bytes 12296 | tf_op jit(solution)/shard_map/ppermute | solution.py:211
  202.5 2.3 %collective-permute-done.17 = f32[8,128]{1,0:T(8,128)S(1)} collective-permute-done((f32[8,128]{1,0:T(8,128)S(1)}, f32[8,128]{1,0:T(8,128)S(1)}, u32[]{:S(2)}, u32[]{:S(2)}) %collective-permute-start.17) | collective-permute-done | bytes 4128 | tf_op jit(solution)/shard_map/ppermute | solution.py:211
  206.5 7.1 %finish.1 = (bf16[512,2048]{1,0:T(8,128)(2,1)}, f32[1,2048,512]{2,1,0:T(8,128)}) custom-call(bf16[512,512]{1,0:T(8,128)(2,1)} %copy-done.10, bf16[512,2048]{1,0:T(8,128)(2,1)} %bitcast.8.got_ref, bf16[512,2048]{1,0:T(8,128)(2,1)} %copy-done.1, f32[8,128]{1,0:T(8,128)} %add_add_fusion.square_ref, f32[1024,512]{1,0:T(8,128)} %copy-done.4, f32[1024,512]{1,0:T(8,128)} %copy-done.5), custom_call_target="tpu_custom_call" | custom-call | flops 1073741824 | bytes 8388608 | tf_op jit(solution)/shard_map/finish/pallas_call | solution.py:410
  (66 shorter events, 26.3 us)
Async XLA Ops:
  5.9 5.4 %copy-start.17 = (s32[1,16,4]{1,2,0:T(4,128)S(1)}, s32[1,16,4]{1,2,0:T(4,128)}, u32[]{:S(2)}) copy-start(s32[1,16,4]{1,2,0:T(4,128)} %param.12) | copy-start | bytes 772
  5.9 61.4 %all-to-all-start = ((bf16[8,64,2560]{2,1,0:T(8,128)(2,1)}), bf16[8,64,2560]{2,1,0:T(8,128)(2,1)S(1)}, u32[]{:S(2)}, u32[]{:S(2)}) async-start(bf16[8,64,2560]{2,1,0:T(8,128)(2,1)} %bitcast.16), calls=%async_computation | async-start | bytes 5242880 | tf_op jit(solution)/shard_map/all_to_all | solution.py:214
  14.7 34.7 %collective-permute-start = (bf16[256,512]{1,0:T(8,128)(2,1)}, bf16[256,512]{1,0:T(8,128)(2,1)S(1)}, u32[]{:S(2)}, u32[]{:S(2)}) collective-permute-start(bf16[256,512]{1,0:T(8,128)(2,1)} %get-tuple-element.37), channel_id=1, source_target_pairs={{0,12},{1,13},{2,14},{3,15},{4,8},{5,9},{6,10},{7,11},{8,4},{9,5},... | collective-permute-start | bytes 786440 | tf_op jit(solution)/shard_map/ppermute | solution.py:208
  18.1 36.9 %collective-permute-start.2 = (bf16[256,512]{1,0:T(8,128)(2,1)}, bf16[256,512]{1,0:T(8,128)(2,1)S(1)}, u32[]{:S(2)}, u32[]{:S(2)}) collective-permute-start(bf16[256,512]{1,0:T(8,128)(2,1)} %get-tuple-element.41), channel_id=1, source_target_pairs={{0,12},{1,13},{2,14},{3,15},{4,8},{5,9},{6,10},{7,11},{8,4},{9,5},... | collective-permute-start | bytes 786440 | tf_op jit(solution)/shard_map/ppermute | solution.py:208
  18.1 42.5 %collective-permute-start.3 = (bf16[256,512]{1,0:T(8,128)(2,1)}, bf16[256,512]{1,0:T(8,128)(2,1)S(1)}, u32[]{:S(2)}, u32[]{:S(2)}) collective-permute-start(bf16[256,512]{1,0:T(8,128)(2,1)} %get-tuple-element.42), channel_id=1, source_target_pairs={{0,12},{1,13},{2,14},{3,15},{4,8},{5,9},{6,10},{7,11},{8,4},{9,5},... | collective-permute-start | bytes 786440 | tf_op jit(solution)/shard_map/ppermute | solution.py:208
  21.3 45.2 %collective-permute-start.4 = (bf16[272,512]{1,0:T(8,128)(2,1)}, bf16[272,512]{1,0:T(8,128)(2,1)S(1)}, u32[]{:S(2)}, u32[]{:S(2)}) collective-permute-start(bf16[272,512]{1,0:T(8,128)(2,1)} %get-tuple-element.43), channel_id=1, source_target_pairs={{0,12},{1,13},{2,14},{3,15},{4,8},{5,9},{6,10},{7,11},{8,4},{9,5},... | collective-permute-start | bytes 835592 | tf_op jit(solution)/shard_map/ppermute | solution.py:208
  49.4 17.2 %collective-permute-start.1 = (bf16[256,512]{1,0:T(8,128)(2,1)S(1)}, bf16[256,512]{1,0:T(8,128)(2,1)S(1)}, u32[]{:S(2)}, u32[]{:S(2)}) collective-permute-start(bf16[256,512]{1,0:T(8,128)(2,1)S(1)} %collective-permute-done.refs_0_), channel_id=1, source_target_pairs={{0,16},{16,0},{1,17},{17,1},{2,18},{18,2},{3,19},{19,3},{4,20},{20... | collective-permute-start | bytes 786440 | tf_op jit(solution)/shard_map/ppermute | solution.py:256
  60.6 6.0 %copy-start.6 = (bf16[256,512]{1,0:T(8,128)(2,1)}, bf16[256,512]{1,0:T(8,128)(2,1)S(1)}, u32[]{:S(2)}) copy-start(bf16[256,512]{1,0:T(8,128)(2,1)S(1)} %collective-permute-done.3.refs_2_) | copy-start | bytes 786436
  67.3 8.0 %copy-start.13 = (s32[1,16,4]{2,1,0:T(8,128)S(1)}, s32[1,16,4]{2,1,0:T(8,128)}, u32[]{:S(2)}) copy-start(s32[1,16,4]{2,1,0:T(8,128)} %copy.9.pattern_ref) | copy-start | bytes 772
  67.3 12.0 %copy-start.14 = (s32[512,1]{0,1:T(1,128)S(1)}, s32[512,1]{0,1:T(1,128)}, u32[]{:S(2)}) copy-start(s32[512,1]{0,1:T(1,128)} %param.8) | copy-start | bytes 6148
  67.3 12.0 %copy-start.16 = (s32[16]{0:T(128)S(1)}, s32[16]{0:T(128)}, u32[]{:S(2)}) copy-start(s32[16]{0:T(128)} %owner_ref.5) | copy-start | bytes 196
  67.3 37.1 %all-to-all-start.1 = ((bf16[8,64,2560]{2,1,0:T(8,128)(2,1)}), bf16[8,64,2560]{2,1,0:T(8,128)(2,1)}, u32[]{:S(2)}, u32[]{:S(2)}) async-start(bf16[8,64,2560]{2,1,0:T(8,128)(2,1)} %bitcast.15), calls=%async_computation.1 | async-start | bytes 5242880 | tf_op jit(solution)/shard_map/all_to_all | solution.py:214
  72.6 19.4 %collective-permute-start.7 = (bf16[272,512]{1,0:T(8,128)(2,1)S(1)}, bf16[272,512]{1,0:T(8,128)(2,1)S(1)}, u32[]{:S(2)}, u32[]{:S(2)}) collective-permute-start(bf16[272,512]{1,0:T(8,128)(2,1)S(1)} %collective-permute-done.4.refs_3_), channel_id=1, source_target_pairs={{0,16},{16,0},{1,17},{17,1},{2,18},{18,2},{3,19},{19,3},{4,20},{20... | collective-permute-start | bytes 835592 | tf_op jit(solution)/shard_map/ppermute | solution.py:256
  73.8 12.6 %collective-permute-start.5 = (bf16[256,512]{1,0:T(8,128)(2,1)S(1)}, bf16[256,512]{1,0:T(8,128)(2,1)S(1)}, u32[]{:S(2)}, u32[]{:S(2)}) collective-permute-start(bf16[256,512]{1,0:T(8,128)(2,1)S(1)} %collective-permute-done.2.refs_1_), channel_id=1, source_target_pairs={{0,16},{16,0},{1,17},{17,1},{2,18},{18,2},{3,19},{19,3},{4,20},{20... | collective-permute-start | bytes 786440 | tf_op jit(solution)/shard_map/ppermute | solution.py:256
  74.1 17.9 %collective-permute-start.6 = (bf16[256,512]{1,0:T(8,128)(2,1)}, bf16[256,512]{1,0:T(8,128)(2,1)S(1)}, u32[]{:S(2)}, u32[]{:S(2)}) collective-permute-start(bf16[256,512]{1,0:T(8,128)(2,1)} %copy-done.6), channel_id=1, source_target_pairs={{0,16},{16,0},{1,17},{17,1},{2,18},{18,2},{3,19},{19,3},{4,20},{20... | collective-permute-start | bytes 786440 | tf_op jit(solution)/shard_map/ppermute | solution.py:256
  76.9 15.1 %copy-start.7 = (bf16[256,512]{1,0:T(8,128)(2,1)S(1)}, bf16[256,512]{1,0:T(8,128)(2,1)}, u32[]{:S(2)}) copy-start(bf16[256,512]{1,0:T(8,128)(2,1)} %copy-done.6) | copy-start | bytes 786436
  76.9 15.1 %copy-start.9 = (bf16[256,512]{1,0:T(8,128)(2,1)S(1)}, bf16[256,512]{1,0:T(8,128)(2,1)}, u32[]{:S(2)}) copy-start(bf16[256,512]{1,0:T(8,128)(2,1)} %copy-done.8) | copy-start | bytes 786436
  96.0 55.1 %collective-permute-start.10 = (bf16[1024,512]{1,0:T(8,128)(2,1)}, bf16[1024,512]{1,0:T(8,128)(2,1)}, u32[]{:S(2)}, u32[]{:S(2)}) collective-permute-start(bf16[1024,512]{1,0:T(8,128)(2,1)} %far_raw.2), channel_id=1, source_target_pairs={{4,8},{5,9},{6,10},{7,11},{8,4},{9,5},{10,6},{11,7},{20,24},{21,25... | collective-permute-start | bytes 3145736 | tf_op jit(solution)/shard_map/ppermute | solution.py:326
  100.2 65.0 %collective-permute-start.8 = (bf16[1024,512]{1,0:T(8,128)(2,1)}, bf16[1024,512]{1,0:T(8,128)(2,1)}, u32[]{:S(2)}, u32[]{:S(2)}) collective-permute-start(bf16[1024,512]{1,0:T(8,128)(2,1)} %far_raw.3), channel_id=1, source_target_pairs={{4,8},{5,9},{6,10},{7,11},{8,4},{9,5},{10,6},{11,7},{20,24},{21,25... | collective-permute-start | bytes 3145736 | tf_op jit(solution)/shard_map/ppermute | solution.py:326
  104.4 11.7 %copy-start.3 = (bf16[2048,512]{1,0:T(8,128)(2,1)S(1)}, bf16[2048,512]{1,0:T(8,128)(2,1)}, u32[]{:S(2)}) copy-start(bf16[2048,512]{1,0:T(8,128)(2,1)} %copy-done.2) | copy-start | bytes 6291460
  104.4 11.7 %copy-start.15 = (f32[1,512]{1,0:T(1,128)S(1)}, f32[1,512]{1,0:T(1,128)}, u32[]{:S(2)}) copy-start(f32[1,512]{1,0:T(1,128)} %weight_ref.3) | copy-start | bytes 6148
  104.4 32.4 %all-to-all-start.2 = ((bf16[8,64,2048]{2,1,0:T(8,128)(2,1)}), bf16[8,64,2048]{2,1,0:T(8,128)(2,1)}, u32[]{:S(2)}, u32[]{:S(2)}) async-start(bf16[8,64,2048]{2,1,0:T(8,128)(2,1)} %bitcast.5), calls=%async_computation.2 | async-start | bytes 4194304 | tf_op jit(solution)/shard_map/all_to_all | solution.py:214
  111.8 48.4 %collective-permute-start.11 = (bf16[1024,512]{1,0:T(8,128)(2,1)}, bf16[1024,512]{1,0:T(8,128)(2,1)}, u32[]{:S(2)}, u32[]{:S(2)}) collective-permute-start(bf16[1024,512]{1,0:T(8,128)(2,1)} %far_raw.2), channel_id=1, source_target_pairs={{0,12},{1,13},{2,14},{3,15},{12,0},{13,1},{14,2},{15,3},{16,28},{1... | collective-permute-start | bytes 3145736 | tf_op jit(solution)/shard_map/ppermute | solution.py:328
  116.1 23.9 %copy-start.12 = (bf16[512,512]{1,0:T(8,128)(2,1)S(1)}, bf16[512,512]{1,0:T(8,128)(2,1)}, u32[]{:S(2)}) copy-start(bf16[512,512]{1,0:T(8,128)(2,1)} %copy-done.11) | copy-start | bytes 1572868
  136.7 46.0 %collective-permute-start.9 = (bf16[1024,512]{1,0:T(8,128)(2,1)}, bf16[1024,512]{1,0:T(8,128)(2,1)}, u32[]{:S(2)}, u32[]{:S(2)}) collective-permute-start(bf16[1024,512]{1,0:T(8,128)(2,1)} %far_raw.3), channel_id=1, source_target_pairs={{0,12},{1,13},{2,14},{3,15},{12,0},{13,1},{14,2},{15,3},{16,28},{1... | collective-permute-start | bytes 3145736 | tf_op jit(solution)/shard_map/ppermute | solution.py:328
  144.9 61.6 %all-to-all-start.3 = ((bf16[8,64,2048]{2,1,0:T(8,128)(2,1)}), bf16[8,64,2048]{2,1,0:T(8,128)(2,1)}, u32[]{:S(2)}, u32[]{:S(2)}) async-start(bf16[8,64,2048]{2,1,0:T(8,128)(2,1)} %bitcast.7), calls=%async_computation.3 | async-start | bytes 4194304 | tf_op jit(solution)/shard_map/all_to_all | solution.py:214
  187.7 4.9 %collective-permute-start.14 = (f32[8,128]{1,0:T(8,128)S(1)}, f32[8,128]{1,0:T(8,128)S(1)}, u32[]{:S(2)}, u32[]{:S(2)}) collective-permute-start(f32[8,128]{1,0:T(8,128)S(1)} %get-tuple-element.64), channel_id=1, source_target_pairs={{0,3},{1,2},{2,1},{3,0},{4,7},{5,6},{6,5},{7,4},{8,11},{9,10},{10,... | collective-permute-start | bytes 12296 | tf_op jit(solution)/shard_map/ppermute | solution.py:211
  190.1 5.6 %collective-permute-start.13 = (f32[8,128]{1,0:T(8,128)S(1)}, f32[8,128]{1,0:T(8,128)S(1)}, u32[]{:S(2)}, u32[]{:S(2)}) collective-permute-start(f32[8,128]{1,0:T(8,128)S(1)} %get-tuple-element.64), channel_id=1, source_target_pairs={{0,2},{1,3},{2,0},{3,1},{4,6},{5,7},{6,4},{7,5},{8,10},{9,11},{10,... | collective-permute-start | bytes 12296 | tf_op jit(solution)/shard_map/ppermute | solution.py:211
  190.4 5.3 %collective-permute-start.12 = (f32[8,128]{1,0:T(8,128)S(1)}, f32[8,128]{1,0:T(8,128)S(1)}, u32[]{:S(2)}, u32[]{:S(2)}) collective-permute-start(f32[8,128]{1,0:T(8,128)S(1)} %get-tuple-element.64), channel_id=1, source_target_pairs={{0,1},{1,0},{2,3},{3,2},{4,5},{5,4},{6,7},{7,6},{8,9},{9,8},{10,11... | collective-permute-start | bytes 12296 | tf_op jit(solution)/shard_map/ppermute | solution.py:211
  195.7 9.2 %collective-permute-start.17 = (f32[8,128]{1,0:T(8,128)S(1)}, f32[8,128]{1,0:T(8,128)S(1)}, u32[]{:S(2)}, u32[]{:S(2)}) collective-permute-start(f32[8,128]{1,0:T(8,128)S(1)} %add_add_fusion.1), channel_id=1, source_target_pairs={{0,12},{1,13},{2,14},{3,15},{4,8},{5,9},{6,10},{7,11},{8,4},{9,5},... | collective-permute-start | bytes 12296 | tf_op jit(solution)/shard_map/ppermute | solution.py:211
  196.9 8.0 %collective-permute-start.16 = (f32[8,128]{1,0:T(8,128)S(1)}, f32[8,128]{1,0:T(8,128)S(1)}, u32[]{:S(2)}, u32[]{:S(2)}) collective-permute-start(f32[8,128]{1,0:T(8,128)S(1)} %add_add_fusion.1), channel_id=1, source_target_pairs={{0,8},{1,9},{2,10},{3,11},{4,12},{5,13},{6,14},{7,15},{8,0},{9,1},... | collective-permute-start | bytes 12296 | tf_op jit(solution)/shard_map/ppermute | solution.py:211
  202.5 3.4 %collective-permute-start.15 = (f32[8,128]{1,0:T(8,128)S(1)}, f32[8,128]{1,0:T(8,128)S(1)}, u32[]{:S(2)}, u32[]{:S(2)}) collective-permute-start(f32[8,128]{1,0:T(8,128)S(1)} %add_add_fusion.1), channel_id=1, source_target_pairs={{0,4},{1,5},{2,6},{3,7},{4,0},{5,1},{6,2},{7,3},{8,12},{9,13},{10,... | collective-permute-start | bytes 12296 | tf_op jit(solution)/shard_map/ppermute | solution.py:211
  (8 other events, 9.3 us)

commit v8 on v7

--- a/solution.py
+++ b/solution.py
@@ -27,6 +27,9 @@
 
 def cost(flops, nbytes):
     return pl.CostEstimate(flops=int(flops), bytes_accessed=int(nbytes), transcendentals=0)
+
+
+LATE = cost(1 << 40, 1 << 30)
 
 
 def whole(shape):
@@ -220,9 +223,9 @@
     def prep(near, name):
         return pl.pallas_call(
             functools.partial(prep_kernel, heads, capacity, near),
-            grid=(cut,),
+            grid=(2,),
             in_specs=[whole((1, rows)), SMEM, whole((rows, width)), whole((rows, channels))],
-            out_specs=pl.BlockSpec((placed // cut, wide), lambda i: (i, 0)),
+            out_specs=pl.BlockSpec((placed // 2, wide), lambda i: (i, 0)),
             out_shape=jax.ShapeDtypeStruct((placed, wide), BF16),
             scratch_shapes=[pltpu.VMEM((8, rows), jnp.int32)],
             compiler_params=STREAM,
@@ -230,7 +233,6 @@
             name=name,
         )(inst, owner_slot, latents, targets)
 
-    far_send = prep(False, "prep_far")
     far_send = prep(False, "prep_far")
     near_send = prep(True, "prep_near")
     deep = width // (groups * CHUNKS)
@@ -255,8 +257,6 @@
         swap = [(i, i ^ step) for i in range(groups)]
         swapped = [held + [lax.ppermute(x, "grp", swap) for x in held] for held in swapped]
         step *= 2
-    far_eff = [swapped[chunk][number] for number in range(groups) for chunk in range(CHUNKS)]
-
     far_x = in_half(far_send)
     early = swapped[: CHUNKS // 4]
     near_send, far_x, early, crossed = lax.optimization_barrier((near_send, far_x, early, crossed))
@@ -350,7 +350,7 @@
             jax.ShapeDtypeStruct((placed, channels), BF16),
         ],
         compiler_params=SMALL,
-        cost_estimate=cost(1 << 40, 1 << 30),
+        cost_estimate=LATE,
         name="near_head",
     )(near_x, effective, error_weight)
     near_grad, far_got = lax.optimization_barrier((near_grad, far_got))
@@ -358,13 +358,16 @@
     def column_spec(deep):
         return pl.BlockSpec((deep, width // cut), lambda i: (0, i))
 
+    def half_spec(deep):
+        return pl.BlockSpec((deep, width // 2), lambda i: (0, i))
+
     far_placed = pl.pallas_call(
         far_place_kernel,
-        grid=(cut,),
-        in_specs=[whole((rows, placed)), column_spec(placed)],
-        out_specs=column_spec(rows),
+        grid=(2,),
+        in_specs=[whole((rows, placed)), half_spec(placed)],
+        out_specs=half_spec(rows),
         out_shape=jax.ShapeDtypeStruct((rows, width), BF16),
-        compiler_params=SMALL,
+        compiler_params=STREAM,
         cost_estimate=cost(2 * rows * placed * width, 4 * placed * width),
         name="far_place",
     )(far_back, far_got)
@@ -389,7 +392,7 @@
                 jax.ShapeDtypeStruct((8, 128), F32),
             ],
             compiler_params=SMALL,
-            cost_estimate=cost(1 << 40, 1 << 30),
+            cost_estimate=LATE,
             name="raw",
         )(near_x, near_res, far_raw[chunk], far_out[chunk], block_pattern, squares)
         raw_grad.append(part)

time: 215 us -> 214 us (level)
    unnamed x37 -> x33, local copies, waits for them, and re-layouts: 9.94 us -> 8.65 us
where the time goes in v8:
time: 214 us; the launch traced here: 213 us
  waiting for transfers between devices  101 us (47%)
  starting transfers between devices  55.6 us (26%)
  Pallas kernels  46.5 us (22%)
  local copies, waits for them, and re-layouts  8.65 us (4%)
    ppermute x4, waiting for transfers between devices, partner(): return lax.ppermute(x, 'loc', [(i, i ^ apart) for i in range(members)])  39.3 us
    ppermute x2, waiting for transfers between devices, per_device(): lax.ppermute(part, 'loc', [(i, i ^ apart) for i in outer])  27.7 us
    all_to_all x4, starting transfers between devices, in_half(): lax.all_to_all(x, 'loc', split_axis=0, concat_axis=0, tiled=True, axis_in...  24.4 us
    all_to_all x4, waiting for transfers between devices, in_half(): lax.all_to_all(x, 'loc', split_axis=0, concat_axis=0, tiled=True, axis_in...  15.7 us
    ppermute x4, waiting for transfers between devices, per_device(): lax.ppermute(x, 'grp', swap)  9.92 us
    ppermute x6, starting transfers between devices, hop(): return lax.ppermute(x, 'loc', [(i, i ^ distance) for i in range(members)])  9.71 us
    pallas_call x2, Pallas kernels, prep(): pl.pallas_call(functools.partial(prep_kernel, heads, capacity, near), gri...  9.42 us
    unnamed x33, local copies, waits for them, and re-layouts  8.65 us
  transfers between devices with their start and end apart: 22, of which 13 were waited for; matrix products, arithmetic and copies ran while one was open for 1% of the time, Pallas kernels for 16%

profile of v8, /device:TPU:1, one launch (start us, length us, event | category | flops | bytes accessed | tf_op | source)
XLA Modules:
  0.0 213.1 jit_solution(14897785630009135776)
XLA Ops:
  0.6 4.7 %prep_far.1 = bf16[512,2560]{1,0:T(8,128)(2,1)} custom-call(s32[1,512]{1,0:T(1,128)} %bitcast.12, s32[16]{0:T(128)} %owner_ref.5, bf16[512,2048]{1,0:T(8,128)(2,1)} %x_ref.3, bf16[512,512]{1,0:T(8,128)(2,1)} %t_ref.3), custom_call_target="tpu_custom_call" | custom-call | flops 1342177280 | bytes 5242880 | tf_op jit(solution)/shard_map/prep_far/pallas_call | solution.py:224
  5.4 5.4 %all-to-all-start = ((bf16[8,64,2560]{2,1,0:T(8,128)(2,1)}), bf16[8,64,2560]{2,1,0:T(8,128)(2,1)S(1)}, u32[]{:S(2)}, u32[]{:S(2)}) async-start(bf16[8,64,2560]{2,1,0:T(8,128)(2,1)} %bitcast.16), calls=%async_computation | async-start | bytes 5242880 | tf_op jit(solution)/shard_map/all_to_all | solution.py:217
  11.5 2.7 %piece.1 = (bf16[256,512]{1,0:T(8,128)(2,1)}, bf16[256,512]{1,0:T(8,128)(2,1)}, bf16[256,512]{1,0:T(8,128)(2,1)}, bf16[272,512]{1,0:T(8,128)(2,1)}) custom-call(bf16[1,2048,512]{2,1,0:T(8,128)(2,1)} %w_ref.1, s32[1,16,4]{2,1,0:T(8,128)} %copy.9.pattern_ref, f32[1,512]{1,0:T(1,128)} %weight_ref.3), custom_call_target="tpu_custom_call" | custom-call | flops 524288 | bytes 2097152 | tf_op jit(solution)/shard_map/piece/pallas_call | solution.py:240
  14.2 3.4 %collective-permute-start = (bf16[256,512]{1,0:T(8,128)(2,1)}, bf16[256,512]{1,0:T(8,128)(2,1)S(1)}, u32[]{:S(2)}, u32[]{:S(2)}) collective-permute-start(bf16[256,512]{1,0:T(8,128)(2,1)} %get-tuple-element.37), channel_id=1, source_target_pairs={{0,12},{1,13},{2,14},{3,15},{4,8},{5,9},{6,10},{7,11},{8,4},{9,5},... | collective-permute-start | bytes 786440 | tf_op jit(solution)/shard_map/ppermute | solution.py:211
  17.6 3.2 %collective-permute-start.3 = (bf16[256,512]{1,0:T(8,128)(2,1)}, bf16[256,512]{1,0:T(8,128)(2,1)S(1)}, u32[]{:S(2)}, u32[]{:S(2)}) collective-permute-start(bf16[256,512]{1,0:T(8,128)(2,1)} %get-tuple-element.42), channel_id=1, source_target_pairs={{0,12},{1,13},{2,14},{3,15},{4,8},{5,9},{6,10},{7,11},{8,4},{9,5},... | collective-permute-start | bytes 786440 | tf_op jit(solution)/shard_map/ppermute | solution.py:211
  20.9 4.7 %prep_near.1 = bf16[512,2560]{1,0:T(8,128)(2,1)} custom-call(s32[1,512]{1,0:T(1,128)} %bitcast.13, s32[16]{0:T(128)} %owner_ref.5, bf16[512,2048]{1,0:T(8,128)(2,1)} %x_ref.3, bf16[512,512]{1,0:T(8,128)(2,1)} %t_ref.3), custom_call_target="tpu_custom_call" | custom-call | flops 1342177280 | bytes 5242880 | tf_op jit(solution)/shard_map/prep_near/pallas_call | solution.py:224
  25.6 23.3 %collective-permute-done.refs_0_ = bf16[256,512]{1,0:T(8,128)(2,1)S(1)} collective-permute-done((bf16[256,512]{1,0:T(8,128)(2,1)}, bf16[256,512]{1,0:T(8,128)(2,1)S(1)}, u32[]{:S(2)}, u32[]{:S(2)}) %collective-permute-start) | collective-permute-done | bytes 262176 | tf_op jit(solution)/shard_map/ppermute | solution.py:211
  50.1 4.4 %collective-permute-done.2.refs_1_ = bf16[256,512]{1,0:T(8,128)(2,1)S(1)} collective-permute-done((bf16[256,512]{1,0:T(8,128)(2,1)}, bf16[256,512]{1,0:T(8,128)(2,1)S(1)}, u32[]{:S(2)}, u32[]{:S(2)}) %collective-permute-start.2) | collective-permute-done | bytes 262176 | tf_op jit(solution)/shard_map/ppermute | solution.py:211
  54.5 5.6 %collective-permute-done.3.refs_2_ = bf16[256,512]{1,0:T(8,128)(2,1)S(1)} collective-permute-done((bf16[256,512]{1,0:T(8,128)(2,1)}, bf16[256,512]{1,0:T(8,128)(2,1)S(1)}, u32[]{:S(2)}, u32[]{:S(2)}) %collective-permute-start.3) | collective-permute-done | bytes 262176 | tf_op jit(solution)/shard_map/ppermute | solution.py:211
  60.1 6.0 %collective-permute-done.4.refs_3_ = bf16[272,512]{1,0:T(8,128)(2,1)S(1)} collective-permute-done((bf16[272,512]{1,0:T(8,128)(2,1)}, bf16[272,512]{1,0:T(8,128)(2,1)S(1)}, u32[]{:S(2)}, u32[]{:S(2)}) %collective-permute-start.4) | collective-permute-done | bytes 278560 | tf_op jit(solution)/shard_map/ppermute | solution.py:211
  66.8 5.3 %all-to-all-start.1 = ((bf16[8,64,2560]{2,1,0:T(8,128)(2,1)}), bf16[8,64,2560]{2,1,0:T(8,128)(2,1)}, u32[]{:S(2)}, u32[]{:S(2)}) async-start(bf16[8,64,2560]{2,1,0:T(8,128)(2,1)} %bitcast.15), calls=%async_computation.1 | async-start | bytes 5242880 | tf_op jit(solution)/shard_map/all_to_all | solution.py:217
  81.6 4.3 %collective-permute-done.5.refs_5_ = bf16[256,512]{1,0:T(8,128)(2,1)S(1)} collective-permute-done((bf16[256,512]{1,0:T(8,128)(2,1)S(1)}, bf16[256,512]{1,0:T(8,128)(2,1)S(1)}, u32[]{:S(2)}, u32[]{:S(2)}) %collective-permute-start.5) | collective-permute-done | bytes 262176 | tf_op jit(solution)/shard_map/ppermute | solution.py:258
  85.9 5.6 %collective-permute-done.6.refs_6_ = bf16[256,512]{1,0:T(8,128)(2,1)S(1)} collective-permute-done((bf16[256,512]{1,0:T(8,128)(2,1)}, bf16[256,512]{1,0:T(8,128)(2,1)S(1)}, u32[]{:S(2)}, u32[]{:S(2)}) %collective-permute-start.6) | collective-permute-done | bytes 262176 | tf_op jit(solution)/shard_map/ppermute | solution.py:258
  93.0 2.5 %far_raw.2 = bf16[1024,512]{1,0:T(8,128)(2,1)} custom-call(bf16[512,2560]{1,0:T(8,128)(2,1)S(1)} %bitcast.10, bf16[512,512]{1,0:T(8,128)(2,1)S(1)} %far_res.1.res_ref), custom_call_target="tpu_custom_call" | custom-call | flops 536870912 | bytes 2097152 | tf_op jit(solution)/shard_map/far_raw/pallas_call | solution.py:308
  97.2 2.5 %far_raw.3 = bf16[1024,512]{1,0:T(8,128)(2,1)} custom-call(bf16[512,2560]{1,0:T(8,128)(2,1)S(1)} %bitcast.11, bf16[512,512]{1,0:T(8,128)(2,1)S(1)} %far_res.1.res_ref), custom_call_target="tpu_custom_call" | custom-call | flops 536870912 | bytes 2097152 | tf_op jit(solution)/shard_map/far_raw/pallas_call | solution.py:308
  101.3 2.5 %far_grad.1 = bf16[512,2048]{1,0:T(8,128)(2,1)} custom-call(bf16[512,512]{1,0:T(8,128)(2,1)S(1)} %far_res.1.res_ref, bf16[256,512]{1,0:T(8,128)(2,1)S(1)} %collective-permute-done.refs_0_, bf16[256,512]{1,0:T(8,128)(2,1)S(1)} %collective-permute-done.2.refs_1_, bf16[256,512]{1,0:T(8,128)(2,1)S(1)} %copy-done.6, ...), custom_call_target="tpu_custom_call" | custom-call | flops 1073741824 | bytes 2621440 | tf_op jit(solution)/shard_map/far_grad/pallas_call | solution.py:331
  103.8 7.4 %all-to-all-start.2 = ((bf16[8,64,2048]{2,1,0:T(8,128)(2,1)}), bf16[8,64,2048]{2,1,0:T(8,128)(2,1)}, u32[]{:S(2)}, u32[]{:S(2)}) async-start(bf16[8,64,2048]{2,1,0:T(8,128)(2,1)} %bitcast.5), calls=%async_computation.2 | async-start | bytes 4194304 | tf_op jit(solution)/shard_map/all_to_all | solution.py:217
  111.3 4.2 %collective-permute-start.11 = (bf16[1024,512]{1,0:T(8,128)(2,1)}, bf16[1024,512]{1,0:T(8,128)(2,1)}, u32[]{:S(2)}, u32[]{:S(2)}) collective-permute-start(bf16[1024,512]{1,0:T(8,128)(2,1)} %far_raw.2), channel_id=1, source_target_pairs={{0,12},{1,13},{2,14},{3,15},{12,0},{13,1},{14,2},{15,3},{16,28},{1... | collective-permute-start | bytes 3145736 | tf_op jit(solution)/shard_map/ppermute | solution.py:328
  115.5 5.0 %near_head.1 = (bf16[512,2048]{1,0:T(8,128)(2,1)}, bf16[512,512]{1,0:T(8,128)(2,1)S(1)}) custom-call(bf16[512,2560]{1,0:T(8,128)(2,1)} %bitcast.4.x_ref, bf16[2048,512]{1,0:T(8,128)(2,1)S(1)} %copy-done.2, f32[1,512]{1,0:T(1,128)S(1)} %copy-done.13), custom_call_target="tpu_custom_call" | custom-call | flops 1099511627776 | bytes 1073741824 | tf_op jit(solution)/shard_map/near_head/pallas_call | solution.py:343
  120.5 15.7 %all-to-all-done.2 = bf16[8,64,2048]{2,1,0:T(8,128)(2,1)} async-done(((bf16[8,64,2048]{2,1,0:T(8,128)(2,1)}), bf16[8,64,2048]{2,1,0:T(8,128)(2,1)}, u32[]{:S(2)}, u32[]{:S(2)}) %all-to-all-start.2) | async-done | bytes 2097184 | tf_op jit(solution)/shard_map/all_to_all | solution.py:217
  136.2 3.2 %collective-permute-start.9 = (bf16[1024,512]{1,0:T(8,128)(2,1)}, bf16[1024,512]{1,0:T(8,128)(2,1)}, u32[]{:S(2)}, u32[]{:S(2)}) collective-permute-start(bf16[1024,512]{1,0:T(8,128)(2,1)} %far_raw.3), channel_id=1, source_target_pairs={{0,12},{1,13},{2,14},{3,15},{12,0},{13,1},{14,2},{15,3},{16,28},{1... | collective-permute-start | bytes 3145736 | tf_op jit(solution)/shard_map/ppermute | solution.py:328
  139.4 3.9 %far_place.1.far_ref = bf16[512,2048]{1,0:T(8,128)(2,1)} custom-call(bf16[512,512]{1,0:T(8,128)(2,1)} %copy-done.10, bf16[512,2048]{1,0:T(8,128)(2,1)} %bitcast.6.got_ref), custom_call_target="tpu_custom_call" | custom-call | flops 1073741824 | bytes 4194304 | tf_op jit(solution)/shard_map/far_place/pallas_call | solution.py:364
  143.3 6.2 %all-to-all-start.3 = ((bf16[8,64,2048]{2,1,0:T(8,128)(2,1)}), bf16[8,64,2048]{2,1,0:T(8,128)(2,1)}, u32[]{:S(2)}, u32[]{:S(2)}) async-start(bf16[8,64,2048]{2,1,0:T(8,128)(2,1)} %bitcast.7), calls=%async_computation.3 | async-start | bytes 4194304 | tf_op jit(solution)/shard_map/all_to_all | solution.py:217
  149.5 10.2 %collective-permute-done.11.out_ref = bf16[1024,512]{1,0:T(8,128)(2,1)} collective-permute-done((bf16[1024,512]{1,0:T(8,128)(2,1)}, bf16[1024,512]{1,0:T(8,128)(2,1)}, u32[]{:S(2)}, u32[]{:S(2)}) %collective-permute-start.11) | collective-permute-done | bytes 1048608 | tf_op jit(solution)/shard_map/ppermute | solution.py:328
  159.7 3.6 %raw.2 = (f32[1024,512]{1,0:T(8,128)S(1)}, f32[8,128]{1,0:T(8,128)S(1)}) custom-call(bf16[512,2560]{1,0:T(8,128)(2,1)} %bitcast.4.x_ref, bf16[512,512]{1,0:T(8,128)(2,1)S(1)} %get-tuple-element.60.res_ref, bf16[1024,512]{1,0:T(8,128)(2,1)} %collective-permute-done.10.far_ref, bf16[1024,512]{1,0:T(8,128)(2,1)} %collective-permute-done.11.out_ref, ...), custom_call_target="tpu_custom_call" | custom-call | flops 1099511627776 | bytes 1073741824 | tf_op jit(solution)/shard_map/raw/pallas_call | solution.py:378
  164.7 17.5 %collective-permute-done.9.out_ref = bf16[1024,512]{1,0:T(8,128)(2,1)} collective-permute-done((bf16[1024,512]{1,0:T(8,128)(2,1)}, bf16[1024,512]{1,0:T(8,128)(2,1)}, u32[]{:S(2)}, u32[]{:S(2)}) %collective-permute-start.9) | collective-permute-done | bytes 1048608 | tf_op jit(solution)/shard_map/ppermute | solution.py:328
  182.2 3.6 %raw.3 = (f32[1024,512]{1,0:T(8,128)S(1)}, f32[8,128]{1,0:T(8,128)S(1)}) custom-call(bf16[512,2560]{1,0:T(8,128)(2,1)} %bitcast.4.x_ref, bf16[512,512]{1,0:T(8,128)(2,1)S(1)} %get-tuple-element.60.res_ref, bf16[1024,512]{1,0:T(8,128)(2,1)} %collective-permute-done.8.far_ref, bf16[1024,512]{1,0:T(8,128)(2,1)} %collective-permute-done.9.out_ref, ...), custom_call_target="tpu_custom_call" | custom-call | flops 1099511627776 | bytes 1073741824 | tf_op jit(solution)/shard_map/raw/pallas_call | solution.py:378
  187.2 2.4 %collective-permute-start.14 = (f32[8,128]{1,0:T(8,128)S(1)}, f32[8,128]{1,0:T(8,128)S(1)}, u32[]{:S(2)}, u32[]{:S(2)}) collective-permute-start(f32[8,128]{1,0:T(8,128)S(1)} %get-tuple-element.64), channel_id=1, source_target_pairs={{0,3},{1,2},{2,1},{3,0},{4,7},{5,6},{6,5},{7,4},{8,11},{9,10},{10,... | collective-permute-start | bytes 12296 | tf_op jit(solution)/shard_map/ppermute | solution.py:214
  192.0 3.1 %collective-permute-done.13 = f32[8,128]{1,0:T(8,128)S(1)} collective-permute-done((f32[8,128]{1,0:T(8,128)S(1)}, f32[8,128]{1,0:T(8,128)S(1)}, u32[]{:S(2)}, u32[]{:S(2)}) %collective-permute-start.13) | collective-permute-done | bytes 4128 | tf_op jit(solution)/shard_map/ppermute | solution.py:214
  196.4 5.7 %collective-permute-start.16 = (f32[8,128]{1,0:T(8,128)S(1)}, f32[8,128]{1,0:T(8,128)S(1)}, u32[]{:S(2)}, u32[]{:S(2)}) collective-permute-start(f32[8,128]{1,0:T(8,128)S(1)} %add_add_fusion.1), channel_id=1, source_target_pairs={{0,8},{1,9},{2,10},{3,11},{4,12},{5,13},{6,14},{7,15},{8,0},{9,1},... | collective-permute-start | bytes 12296 | tf_op jit(solution)/shard_map/ppermute | solution.py:214
  202.1 2.3 %collective-permute-done.17 = f32[8,128]{1,0:T(8,128)S(1)} collective-permute-done((f32[8,128]{1,0:T(8,128)S(1)}, f32[8,128]{1,0:T(8,128)S(1)}, u32[]{:S(2)}, u32[]{:S(2)}) %collective-permute-start.17) | collective-permute-done | bytes 4128 | tf_op jit(solution)/shard_map/ppermute | solution.py:214
  206.0 7.1 %finish.1 = (bf16[512,2048]{1,0:T(8,128)(2,1)}, f32[1,2048,512]{2,1,0:T(8,128)}) custom-call(bf16[512,512]{1,0:T(8,128)(2,1)} %copy-done.9, bf16[512,2048]{1,0:T(8,128)(2,1)} %bitcast.8.got_ref, bf16[512,2048]{1,0:T(8,128)(2,1)} %far_place.1.far_ref, f32[8,128]{1,0:T(8,128)} %add_add_fusion.square_ref, f32[1024,512]{1,0:T(8,128)} %copy-done.3, ...), custom_call_target="tpu_custom_call" | custom-call | flops 1073741824 | bytes 8388608 | tf_op jit(solution)/shard_map/finish/pallas_call | solution.py:413
  (62 shorter events, 24.9 us)
Async XLA Ops:
  5.4 5.4 %copy-start.15 = (s32[1,16,4]{1,2,0:T(4,128)S(1)}, s32[1,16,4]{1,2,0:T(4,128)}, u32[]{:S(2)}) copy-start(s32[1,16,4]{1,2,0:T(4,128)} %param.12) | copy-start | bytes 772
  5.4 61.4 %all-to-all-start = ((bf16[8,64,2560]{2,1,0:T(8,128)(2,1)}), bf16[8,64,2560]{2,1,0:T(8,128)(2,1)S(1)}, u32[]{:S(2)}, u32[]{:S(2)}) async-start(bf16[8,64,2560]{2,1,0:T(8,128)(2,1)} %bitcast.16), calls=%async_computation | async-start | bytes 5242880 | tf_op jit(solution)/shard_map/all_to_all | solution.py:217
  14.2 34.7 %collective-permute-start = (bf16[256,512]{1,0:T(8,128)(2,1)}, bf16[256,512]{1,0:T(8,128)(2,1)S(1)}, u32[]{:S(2)}, u32[]{:S(2)}) collective-permute-start(bf16[256,512]{1,0:T(8,128)(2,1)} %get-tuple-element.37), channel_id=1, source_target_pairs={{0,12},{1,13},{2,14},{3,15},{4,8},{5,9},{6,10},{7,11},{8,4},{9,5},... | collective-permute-start | bytes 786440 | tf_op jit(solution)/shard_map/ppermute | solution.py:211
  17.6 36.9 %collective-permute-start.2 = (bf16[256,512]{1,0:T(8,128)(2,1)}, bf16[256,512]{1,0:T(8,128)(2,1)S(1)}, u32[]{:S(2)}, u32[]{:S(2)}) collective-permute-start(bf16[256,512]{1,0:T(8,128)(2,1)} %get-tuple-element.41), channel_id=1, source_target_pairs={{0,12},{1,13},{2,14},{3,15},{4,8},{5,9},{6,10},{7,11},{8,4},{9,5},... | collective-permute-start | bytes 786440 | tf_op jit(solution)/shard_map/ppermute | solution.py:211
  17.6 42.5 %collective-permute-start.3 = (bf16[256,512]{1,0:T(8,128)(2,1)}, bf16[256,512]{1,0:T(8,128)(2,1)S(1)}, u32[]{:S(2)}, u32[]{:S(2)}) collective-permute-start(bf16[256,512]{1,0:T(8,128)(2,1)} %get-tuple-element.42), channel_id=1, source_target_pairs={{0,12},{1,13},{2,14},{3,15},{4,8},{5,9},{6,10},{7,11},{8,4},{9,5},... | collective-permute-start | bytes 786440 | tf_op jit(solution)/shard_map/ppermute | solution.py:211
  20.8 45.2 %collective-permute-start.4 = (bf16[272,512]{1,0:T(8,128)(2,1)}, bf16[272,512]{1,0:T(8,128)(2,1)S(1)}, u32[]{:S(2)}, u32[]{:S(2)}) collective-permute-start(bf16[272,512]{1,0:T(8,128)(2,1)} %get-tuple-element.43), channel_id=1, source_target_pairs={{0,12},{1,13},{2,14},{3,15},{4,8},{5,9},{6,10},{7,11},{8,4},{9,5},... | collective-permute-start | bytes 835592 | tf_op jit(solution)/shard_map/ppermute | solution.py:211
  48.9 17.2 %collective-permute-start.1 = (bf16[256,512]{1,0:T(8,128)(2,1)S(1)}, bf16[256,512]{1,0:T(8,128)(2,1)S(1)}, u32[]{:S(2)}, u32[]{:S(2)}) collective-permute-start(bf16[256,512]{1,0:T(8,128)(2,1)S(1)} %collective-permute-done.refs_0_), channel_id=1, source_target_pairs={{0,16},{16,0},{1,17},{17,1},{2,18},{18,2},{3,19},{19,3},{4,20},{20... | collective-permute-start | bytes 786440 | tf_op jit(solution)/shard_map/ppermute | solution.py:258
  60.1 6.0 %copy-start.5 = (bf16[256,512]{1,0:T(8,128)(2,1)}, bf16[256,512]{1,0:T(8,128)(2,1)S(1)}, u32[]{:S(2)}) copy-start(bf16[256,512]{1,0:T(8,128)(2,1)S(1)} %collective-permute-done.3.refs_2_) | copy-start | bytes 786436
  66.8 8.0 %copy-start.11 = (s32[1,16,4]{2,1,0:T(8,128)S(1)}, s32[1,16,4]{2,1,0:T(8,128)}, u32[]{:S(2)}) copy-start(s32[1,16,4]{2,1,0:T(8,128)} %copy.9.pattern_ref) | copy-start | bytes 772
  66.8 12.0 %copy-start.12 = (s32[512,1]{0,1:T(1,128)S(1)}, s32[512,1]{0,1:T(1,128)}, u32[]{:S(2)}) copy-start(s32[512,1]{0,1:T(1,128)} %param.8) | copy-start | bytes 6148
  66.8 12.0 %copy-start.14 = (s32[16]{0:T(128)S(1)}, s32[16]{0:T(128)}, u32[]{:S(2)}) copy-start(s32[16]{0:T(128)} %owner_ref.5) | copy-start | bytes 196
  66.8 37.0 %all-to-all-start.1 = ((bf16[8,64,2560]{2,1,0:T(8,128)(2,1)}), bf16[8,64,2560]{2,1,0:T(8,128)(2,1)}, u32[]{:S(2)}, u32[]{:S(2)}) async-start(bf16[8,64,2560]{2,1,0:T(8,128)(2,1)} %bitcast.15), calls=%async_computation.1 | async-start | bytes 5242880 | tf_op jit(solution)/shard_map/all_to_all | solution.py:217
  72.1 19.4 %collective-permute-start.7 = (bf16[272,512]{1,0:T(8,128)(2,1)S(1)}, bf16[272,512]{1,0:T(8,128)(2,1)S(1)}, u32[]{:S(2)}, u32[]{:S(2)}) collective-permute-start(bf16[272,512]{1,0:T(8,128)(2,1)S(1)} %collective-permute-done.4.refs_3_), channel_id=1, source_target_pairs={{0,16},{16,0},{1,17},{17,1},{2,18},{18,2},{3,19},{19,3},{4,20},{20... | collective-permute-start | bytes 835592 | tf_op jit(solution)/shard_map/ppermute | solution.py:258
  73.3 12.6 %collective-permute-start.5 = (bf16[256,512]{1,0:T(8,128)(2,1)S(1)}, bf16[256,512]{1,0:T(8,128)(2,1)S(1)}, u32[]{:S(2)}, u32[]{:S(2)}) collective-permute-start(bf16[256,512]{1,0:T(8,128)(2,1)S(1)} %collective-permute-done.2.refs_1_), channel_id=1, source_target_pairs={{0,16},{16,0},{1,17},{17,1},{2,18},{18,2},{3,19},{19,3},{4,20},{20... | collective-permute-start | bytes 786440 | tf_op jit(solution)/shard_map/ppermute | solution.py:258
  73.6 17.9 %collective-permute-start.6 = (bf16[256,512]{1,0:T(8,128)(2,1)}, bf16[256,512]{1,0:T(8,128)(2,1)S(1)}, u32[]{:S(2)}, u32[]{:S(2)}) collective-permute-start(bf16[256,512]{1,0:T(8,128)(2,1)} %copy-done.5), channel_id=1, source_target_pairs={{0,16},{16,0},{1,17},{17,1},{2,18},{18,2},{3,19},{19,3},{4,20},{20... | collective-permute-start | bytes 786440 | tf_op jit(solution)/shard_map/ppermute | solution.py:258
  74.8 1.6 copy-start
  76.4 15.1 %copy-start.6 = (bf16[256,512]{1,0:T(8,128)(2,1)S(1)}, bf16[256,512]{1,0:T(8,128)(2,1)}, u32[]{:S(2)}) copy-start(bf16[256,512]{1,0:T(8,128)(2,1)} %copy-done.5) | copy-start | bytes 786436
  76.4 15.1 %copy-start.8 = (bf16[256,512]{1,0:T(8,128)(2,1)S(1)}, bf16[256,512]{1,0:T(8,128)(2,1)}, u32[]{:S(2)}) copy-start(bf16[256,512]{1,0:T(8,128)(2,1)} %copy-done.7) | copy-start | bytes 786436
  95.5 54.0 %collective-permute-start.10 = (bf16[1024,512]{1,0:T(8,128)(2,1)}, bf16[1024,512]{1,0:T(8,128)(2,1)}, u32[]{:S(2)}, u32[]{:S(2)}) collective-permute-start(bf16[1024,512]{1,0:T(8,128)(2,1)} %far_raw.2), channel_id=1, source_target_pairs={{4,8},{5,9},{6,10},{7,11},{8,4},{9,5},{10,6},{11,7},{20,24},{21,25... | collective-permute-start | bytes 3145736 | tf_op jit(solution)/shard_map/ppermute | solution.py:326
  99.7 65.0 %collective-permute-start.8 = (bf16[1024,512]{1,0:T(8,128)(2,1)}, bf16[1024,512]{1,0:T(8,128)(2,1)}, u32[]{:S(2)}, u32[]{:S(2)}) collective-permute-start(bf16[1024,512]{1,0:T(8,128)(2,1)} %far_raw.3), channel_id=1, source_target_pairs={{4,8},{5,9},{6,10},{7,11},{8,4},{9,5},{10,6},{11,7},{20,24},{21,25... | collective-permute-start | bytes 3145736 | tf_op jit(solution)/shard_map/ppermute | solution.py:326
  103.8 11.7 %copy-start.2 = (bf16[2048,512]{1,0:T(8,128)(2,1)S(1)}, bf16[2048,512]{1,0:T(8,128)(2,1)}, u32[]{:S(2)}) copy-start(bf16[2048,512]{1,0:T(8,128)(2,1)} %copy-done.1) | copy-start | bytes 6291460
  103.8 11.7 %copy-start.13 = (f32[1,512]{1,0:T(1,128)S(1)}, f32[1,512]{1,0:T(1,128)}, u32[]{:S(2)}) copy-start(f32[1,512]{1,0:T(1,128)} %weight_ref.3) | copy-start | bytes 6148
  103.8 32.4 %all-to-all-start.2 = ((bf16[8,64,2048]{2,1,0:T(8,128)(2,1)}), bf16[8,64,2048]{2,1,0:T(8,128)(2,1)}, u32[]{:S(2)}, u32[]{:S(2)}) async-start(bf16[8,64,2048]{2,1,0:T(8,128)(2,1)} %bitcast.5), calls=%async_computation.2 | async-start | bytes 4194304 | tf_op jit(solution)/shard_map/all_to_all | solution.py:217
  111.3 48.5 %collective-permute-start.11 = (bf16[1024,512]{1,0:T(8,128)(2,1)}, bf16[1024,512]{1,0:T(8,128)(2,1)}, u32[]{:S(2)}, u32[]{:S(2)}) collective-permute-start(bf16[1024,512]{1,0:T(8,128)(2,1)} %far_raw.2), channel_id=1, source_target_pairs={{0,12},{1,13},{2,14},{3,15},{12,0},{13,1},{14,2},{15,3},{16,28},{1... | collective-permute-start | bytes 3145736 | tf_op jit(solution)/shard_map/ppermute | solution.py:328
  136.2 46.0 %collective-permute-start.9 = (bf16[1024,512]{1,0:T(8,128)(2,1)}, bf16[1024,512]{1,0:T(8,128)(2,1)}, u32[]{:S(2)}, u32[]{:S(2)}) collective-permute-start(bf16[1024,512]{1,0:T(8,128)(2,1)} %far_raw.3), channel_id=1, source_target_pairs={{0,12},{1,13},{2,14},{3,15},{12,0},{13,1},{14,2},{15,3},{16,28},{1... | collective-permute-start | bytes 3145736 | tf_op jit(solution)/shard_map/ppermute | solution.py:328
  143.3 62.7 %all-to-all-start.3 = ((bf16[8,64,2048]{2,1,0:T(8,128)(2,1)}), bf16[8,64,2048]{2,1,0:T(8,128)(2,1)}, u32[]{:S(2)}, u32[]{:S(2)}) async-start(bf16[8,64,2048]{2,1,0:T(8,128)(2,1)} %bitcast.7), calls=%async_computation.3 | async-start | bytes 4194304 | tf_op jit(solution)/shard_map/all_to_all | solution.py:217
  187.2 4.9 %collective-permute-start.14 = (f32[8,128]{1,0:T(8,128)S(1)}, f32[8,128]{1,0:T(8,128)S(1)}, u32[]{:S(2)}, u32[]{:S(2)}) collective-permute-start(f32[8,128]{1,0:T(8,128)S(1)} %get-tuple-element.64), channel_id=1, source_target_pairs={{0,3},{1,2},{2,1},{3,0},{4,7},{5,6},{6,5},{7,4},{8,11},{9,10},{10,... | collective-permute-start | bytes 12296 | tf_op jit(solution)/shard_map/ppermute | solution.py:214
  189.6 5.6 %collective-permute-start.13 = (f32[8,128]{1,0:T(8,128)S(1)}, f32[8,128]{1,0:T(8,128)S(1)}, u32[]{:S(2)}, u32[]{:S(2)}) collective-permute-start(f32[8,128]{1,0:T(8,128)S(1)} %get-tuple-element.64), channel_id=1, source_target_pairs={{0,2},{1,3},{2,0},{3,1},{4,6},{5,7},{6,4},{7,5},{8,10},{9,11},{10,... | collective-permute-start | bytes 12296 | tf_op jit(solution)/shard_map/ppermute | solution.py:214
  189.9 5.3 %collective-permute-start.12 = (f32[8,128]{1,0:T(8,128)S(1)}, f32[8,128]{1,0:T(8,128)S(1)}, u32[]{:S(2)}, u32[]{:S(2)}) collective-permute-start(f32[8,128]{1,0:T(8,128)S(1)} %get-tuple-element.64), channel_id=1, source_target_pairs={{0,1},{1,0},{2,3},{3,2},{4,5},{5,4},{6,7},{7,6},{8,9},{9,8},{10,11... | collective-permute-start | bytes 12296 | tf_op jit(solution)/shard_map/ppermute | solution.py:214
  195.2 9.2 %collective-permute-start.17 = (f32[8,128]{1,0:T(8,128)S(1)}, f32[8,128]{1,0:T(8,128)S(1)}, u32[]{:S(2)}, u32[]{:S(2)}) collective-permute-start(f32[8,128]{1,0:T(8,128)S(1)} %add_add_fusion.1), channel_id=1, source_target_pairs={{0,12},{1,13},{2,14},{3,15},{4,8},{5,9},{6,10},{7,11},{8,4},{9,5},... | collective-permute-start | bytes 12296 | tf_op jit(solution)/shard_map/ppermute | solution.py:214
  196.4 8.0 %collective-permute-start.16 = (f32[8,128]{1,0:T(8,128)S(1)}, f32[8,128]{1,0:T(8,128)S(1)}, u32[]{:S(2)}, u32[]{:S(2)}) collective-permute-start(f32[8,128]{1,0:T(8,128)S(1)} %add_add_fusion.1), channel_id=1, source_target_pairs={{0,8},{1,9},{2,10},{3,11},{4,12},{5,13},{6,14},{7,15},{8,0},{9,1},... | collective-permute-start | bytes 12296 | tf_op jit(solution)/shard_map/ppermute | solution.py:214
  202.0 3.3 %collective-permute-start.15 = (f32[8,128]{1,0:T(8,128)S(1)}, f32[8,128]{1,0:T(8,128)S(1)}, u32[]{:S(2)}, u32[]{:S(2)}) collective-permute-start(f32[8,128]{1,0:T(8,128)S(1)} %add_add_fusion.1), channel_id=1, source_target_pairs={{0,4},{1,5},{2,6},{3,7},{4,0},{5,1},{6,2},{7,3},{8,12},{9,13},{10,... | collective-permute-start | bytes 12296 | tf_op jit(solution)/shard_map/ppermute | solution.py:214
  (6 other events, 6.4 us)

commit v9 on v8

--- a/solution.py
+++ b/solution.py
@@ -301,7 +301,7 @@
         name="far_res",
     )(far_x, *far_eff)
 
-    tall = 256
+    tall = 512
     steps = width // (PARTS * tall)
     far_raw = []
     for chunk in range(PARTS):
@@ -402,6 +402,7 @@
         squares = squares + sum(hop(squares, step * way) for way in range(1, ways))
         step *= ways
 
+    cut = 2
     near_got, squares = lax.optimization_barrier((near_got, squares))
 
     def raw_spec(part):

time: 214 us -> 212 us (level)
  Pallas kernels: 46.5 us -> 42.5 us
  transfers between devices with their start and end apart: 22 -> 22, of which waited for: 13 -> 14; matrix products, arithmetic and copies ran while one was open for 1% -> 1% of each run, Pallas kernels for 16% -> 15%
where the time goes in v9:
time: 212 us; the launch traced here: 211 us
  waiting for transfers between devices  103 us (49%)
  starting transfers between devices  55.2 us (26%)
  Pallas kernels  42.5 us (20%)
  local copies, waits for them, and re-layouts  8.65 us (4%)
    ppermute x4, waiting for transfers between devices, partner(): return lax.ppermute(x, 'loc', [(i, i ^ apart) for i in range(members)])  39.3 us
    ppermute x2, waiting for transfers between devices, per_device(): lax.ppermute(part, 'loc', [(i, i ^ apart) for i in outer])  28.6 us
    all_to_all x4, starting transfers between devices, in_half(): lax.all_to_all(x, 'loc', split_axis=0, concat_axis=0, tiled=True, axis_in...  24.3 us
    all_to_all x4, waiting for transfers between devices, in_half(): lax.all_to_all(x, 'loc', split_axis=0, concat_axis=0, tiled=True, axis_in...  15.8 us
    ppermute x4, waiting for transfers between devices, per_device(): lax.ppermute(x, 'grp', swap)  9.92 us
    ppermute x6, waiting for transfers between devices, hop(): return lax.ppermute(x, 'loc', [(i, i ^ distance) for i in range(members)])  9.66 us
    ppermute x6, starting transfers between devices, hop(): return lax.ppermute(x, 'loc', [(i, i ^ distance) for i in range(members)])  9.46 us
    pallas_call x2, Pallas kernels, prep(): pl.pallas_call(functools.partial(prep_kernel, heads, capacity, near), gri...  9.42 us
  transfers between devices with their start and end apart: 22, of which 14 were waited for; matrix products, arithmetic and copies ran while one was open for 1% of the time, Pallas kernels for 15%

profile of v9, /device:TPU:1, one launch (start us, length us, event | category | flops | bytes accessed | tf_op | source)
XLA Modules:
  0.0 210.9 jit_solution(12737918981532532096)
XLA Ops:
  0.6 4.7 %prep_far.1 = bf16[512,2560]{1,0:T(8,128)(2,1)} custom-call(s32[1,512]{1,0:T(1,128)} %bitcast.12, s32[16]{0:T(128)} %owner_ref.5, bf16[512,2048]{1,0:T(8,128)(2,1)} %x_ref.3, bf16[512,512]{1,0:T(8,128)(2,1)} %t_ref.3), custom_call_target="tpu_custom_call" | custom-call | flops 1342177280 | bytes 5242880 | tf_op jit(solution)/shard_map/prep_far/pallas_call | solution.py:224
  5.4 5.4 %all-to-all-start = ((bf16[8,64,2560]{2,1,0:T(8,128)(2,1)}), bf16[8,64,2560]{2,1,0:T(8,128)(2,1)S(1)}, u32[]{:S(2)}, u32[]{:S(2)}) async-start(bf16[8,64,2560]{2,1,0:T(8,128)(2,1)} %bitcast.16), calls=%async_computation | async-start | bytes 5242880 | tf_op jit(solution)/shard_map/all_to_all | solution.py:217
  11.5 2.7 %piece.1 = (bf16[256,512]{1,0:T(8,128)(2,1)}, bf16[256,512]{1,0:T(8,128)(2,1)}, bf16[256,512]{1,0:T(8,128)(2,1)}, bf16[272,512]{1,0:T(8,128)(2,1)}) custom-call(bf16[1,2048,512]{2,1,0:T(8,128)(2,1)} %w_ref.1, s32[1,16,4]{2,1,0:T(8,128)} %copy.9.pattern_ref, f32[1,512]{1,0:T(1,128)} %weight_ref.3), custom_call_target="tpu_custom_call" | custom-call | flops 524288 | bytes 2097152 | tf_op jit(solution)/shard_map/piece/pallas_call | solution.py:240
  14.2 3.4 %collective-permute-start = (bf16[256,512]{1,0:T(8,128)(2,1)}, bf16[256,512]{1,0:T(8,128)(2,1)S(1)}, u32[]{:S(2)}, u32[]{:S(2)}) collective-permute-start(bf16[256,512]{1,0:T(8,128)(2,1)} %get-tuple-element.37), channel_id=1, source_target_pairs={{0,12},{1,13},{2,14},{3,15},{4,8},{5,9},{6,10},{7,11},{8,4},{9,5},... | collective-permute-start | bytes 786440 | tf_op jit(solution)/shard_map/ppermute | solution.py:211
  17.6 3.2 %collective-permute-start.3 = (bf16[256,512]{1,0:T(8,128)(2,1)}, bf16[256,512]{1,0:T(8,128)(2,1)S(1)}, u32[]{:S(2)}, u32[]{:S(2)}) collective-permute-start(bf16[256,512]{1,0:T(8,128)(2,1)} %get-tuple-element.42), channel_id=1, source_target_pairs={{0,12},{1,13},{2,14},{3,15},{4,8},{5,9},{6,10},{7,11},{8,4},{9,5},... | collective-permute-start | bytes 786440 | tf_op jit(solution)/shard_map/ppermute | solution.py:211
  20.9 4.7 %prep_near.1 = bf16[512,2560]{1,0:T(8,128)(2,1)} custom-call(s32[1,512]{1,0:T(1,128)} %bitcast.13, s32[16]{0:T(128)} %owner_ref.5, bf16[512,2048]{1,0:T(8,128)(2,1)} %x_ref.3, bf16[512,512]{1,0:T(8,128)(2,1)} %t_ref.3), custom_call_target="tpu_custom_call" | custom-call | flops 1342177280 | bytes 5242880 | tf_op jit(solution)/shard_map/prep_near/pallas_call | solution.py:224
  25.6 23.3 %collective-permute-done.refs_0_ = bf16[256,512]{1,0:T(8,128)(2,1)S(1)} collective-permute-done((bf16[256,512]{1,0:T(8,128)(2,1)}, bf16[256,512]{1,0:T(8,128)(2,1)S(1)}, u32[]{:S(2)}, u32[]{:S(2)}) %collective-permute-start) | collective-permute-done | bytes 262176 | tf_op jit(solution)/shard_map/ppermute | solution.py:211
  50.1 4.4 %collective-permute-done.2.refs_1_ = bf16[256,512]{1,0:T(8,128)(2,1)S(1)} collective-permute-done((bf16[256,512]{1,0:T(8,128)(2,1)}, bf16[256,512]{1,0:T(8,128)(2,1)S(1)}, u32[]{:S(2)}, u32[]{:S(2)}) %collective-permute-start.2) | collective-permute-done | bytes 262176 | tf_op jit(solution)/shard_map/ppermute | solution.py:211
  54.5 5.6 %collective-permute-done.3.refs_2_ = bf16[256,512]{1,0:T(8,128)(2,1)S(1)} collective-permute-done((bf16[256,512]{1,0:T(8,128)(2,1)}, bf16[256,512]{1,0:T(8,128)(2,1)S(1)}, u32[]{:S(2)}, u32[]{:S(2)}) %collective-permute-start.3) | collective-permute-done | bytes 262176 | tf_op jit(solution)/shard_map/ppermute | solution.py:211
  60.1 6.0 %collective-permute-done.4.refs_3_ = bf16[272,512]{1,0:T(8,128)(2,1)S(1)} collective-permute-done((bf16[272,512]{1,0:T(8,128)(2,1)}, bf16[272,512]{1,0:T(8,128)(2,1)S(1)}, u32[]{:S(2)}, u32[]{:S(2)}) %collective-permute-start.4) | collective-permute-done | bytes 278560 | tf_op jit(solution)/shard_map/ppermute | solution.py:211
  66.8 5.3 %all-to-all-start.1 = ((bf16[8,64,2560]{2,1,0:T(8,128)(2,1)}), bf16[8,64,2560]{2,1,0:T(8,128)(2,1)}, u32[]{:S(2)}, u32[]{:S(2)}) async-start(bf16[8,64,2560]{2,1,0:T(8,128)(2,1)} %bitcast.15), calls=%async_computation.1 | async-start | bytes 5242880 | tf_op jit(solution)/shard_map/all_to_all | solution.py:217
  81.6 4.3 %collective-permute-done.5.refs_5_ = bf16[256,512]{1,0:T(8,128)(2,1)S(1)} collective-permute-done((bf16[256,512]{1,0:T(8,128)(2,1)S(1)}, bf16[256,512]{1,0:T(8,128)(2,1)S(1)}, u32[]{:S(2)}, u32[]{:S(2)}) %collective-permute-start.5) | collective-permute-done | bytes 262176 | tf_op jit(solution)/shard_map/ppermute | solution.py:258
  85.9 5.6 %collective-permute-done.6.refs_6_ = bf16[256,512]{1,0:T(8,128)(2,1)S(1)} collective-permute-done((bf16[256,512]{1,0:T(8,128)(2,1)}, bf16[256,512]{1,0:T(8,128)(2,1)S(1)}, u32[]{:S(2)}, u32[]{:S(2)}) %collective-permute-start.6) | collective-permute-done | bytes 262176 | tf_op jit(solution)/shard_map/ppermute | solution.py:258
  93.0 1.9 far_raw.2
  100.0 2.5 %far_grad.1 = bf16[512,2048]{1,0:T(8,128)(2,1)} custom-call(bf16[512,512]{1,0:T(8,128)(2,1)S(1)} %far_res.1.res_ref, bf16[256,512]{1,0:T(8,128)(2,1)S(1)} %collective-permute-done.refs_0_, bf16[256,512]{1,0:T(8,128)(2,1)S(1)} %collective-permute-done.2.refs_1_, bf16[256,512]{1,0:T(8,128)(2,1)S(1)} %copy-done.6, ...), custom_call_target="tpu_custom_call" | custom-call | flops 1073741824 | bytes 2621440 | tf_op jit(solution)/shard_map/far_grad/pallas_call | solution.py:331
  102.7 7.3 %all-to-all-start.2 = ((bf16[8,64,2048]{2,1,0:T(8,128)(2,1)}), bf16[8,64,2048]{2,1,0:T(8,128)(2,1)}, u32[]{:S(2)}, u32[]{:S(2)}) async-start(bf16[8,64,2048]{2,1,0:T(8,128)(2,1)} %bitcast.5), calls=%async_computation.2 | async-start | bytes 4194304 | tf_op jit(solution)/shard_map/all_to_all | solution.py:217
  110.0 4.2 %collective-permute-start.11 = (bf16[1024,512]{1,0:T(8,128)(2,1)}, bf16[1024,512]{1,0:T(8,128)(2,1)}, u32[]{:S(2)}, u32[]{:S(2)}) collective-permute-start(bf16[1024,512]{1,0:T(8,128)(2,1)} %far_raw.2), channel_id=1, source_target_pairs={{0,12},{1,13},{2,14},{3,15},{12,0},{13,1},{14,2},{15,3},{16,28},{1... | collective-permute-start | bytes 3145736 | tf_op jit(solution)/shard_map/ppermute | solution.py:328
  114.3 5.0 %near_head.1 = (bf16[512,2048]{1,0:T(8,128)(2,1)}, bf16[512,512]{1,0:T(8,128)(2,1)S(1)}) custom-call(bf16[512,2560]{1,0:T(8,128)(2,1)} %bitcast.4.x_ref, bf16[2048,512]{1,0:T(8,128)(2,1)S(1)} %copy-done.2, f32[1,512]{1,0:T(1,128)S(1)} %copy-done.13), custom_call_target="tpu_custom_call" | custom-call | flops 1099511627776 | bytes 1073741824 | tf_op jit(solution)/shard_map/near_head/pallas_call | solution.py:343
  119.3 15.7 %all-to-all-done.2 = bf16[8,64,2048]{2,1,0:T(8,128)(2,1)} async-done(((bf16[8,64,2048]{2,1,0:T(8,128)(2,1)}), bf16[8,64,2048]{2,1,0:T(8,128)(2,1)}, u32[]{:S(2)}, u32[]{:S(2)}) %all-to-all-start.2) | async-done | bytes 2097184 | tf_op jit(solution)/shard_map/all_to_all | solution.py:217
  134.9 3.2 %collective-permute-start.9 = (bf16[1024,512]{1,0:T(8,128)(2,1)}, bf16[1024,512]{1,0:T(8,128)(2,1)}, u32[]{:S(2)}, u32[]{:S(2)}) collective-permute-start(bf16[1024,512]{1,0:T(8,128)(2,1)} %far_raw.3), channel_id=1, source_target_pairs={{0,12},{1,13},{2,14},{3,15},{12,0},{13,1},{14,2},{15,3},{16,28},{1... | collective-permute-start | bytes 3145736 | tf_op jit(solution)/shard_map/ppermute | solution.py:328
  138.2 3.9 %far_place.1.far_ref = bf16[512,2048]{1,0:T(8,128)(2,1)} custom-call(bf16[512,512]{1,0:T(8,128)(2,1)} %copy-done.10, bf16[512,2048]{1,0:T(8,128)(2,1)} %bitcast.6.got_ref), custom_call_target="tpu_custom_call" | custom-call | flops 1073741824 | bytes 4194304 | tf_op jit(solution)/shard_map/far_place/pallas_call | solution.py:364
  142.0 6.2 %all-to-all-start.3 = ((bf16[8,64,2048]{2,1,0:T(8,128)(2,1)}), bf16[8,64,2048]{2,1,0:T(8,128)(2,1)}, u32[]{:S(2)}, u32[]{:S(2)}) async-start(bf16[8,64,2048]{2,1,0:T(8,128)(2,1)} %bitcast.7), calls=%async_computation.3 | async-start | bytes 4194304 | tf_op jit(solution)/shard_map/all_to_all | solution.py:217
  148.3 10.2 %collective-permute-done.11.out_ref = bf16[1024,512]{1,0:T(8,128)(2,1)} collective-permute-done((bf16[1024,512]{1,0:T(8,128)(2,1)}, bf16[1024,512]{1,0:T(8,128)(2,1)}, u32[]{:S(2)}, u32[]{:S(2)}) %collective-permute-start.11) | collective-permute-done | bytes 1048608 | tf_op jit(solution)/shard_map/ppermute | solution.py:328
  158.5 2.7 %raw.2 = (f32[1024,512]{1,0:T(8,128)S(1)}, f32[8,128]{1,0:T(8,128)S(1)}) custom-call(bf16[512,2560]{1,0:T(8,128)(2,1)} %bitcast.4.x_ref, bf16[512,512]{1,0:T(8,128)(2,1)S(1)} %get-tuple-element.60.res_ref, bf16[1024,512]{1,0:T(8,128)(2,1)} %collective-permute-done.10.far_ref, bf16[1024,512]{1,0:T(8,128)(2,1)} %collective-permute-done.11.out_ref, ...), custom_call_target="tpu_custom_call" | custom-call | flops 1099511627776 | bytes 1073741824 | tf_op jit(solution)/shard_map/raw/pallas_call | solution.py:378
  162.6 18.4 %collective-permute-done.9.out_ref = bf16[1024,512]{1,0:T(8,128)(2,1)} collective-permute-done((bf16[1024,512]{1,0:T(8,128)(2,1)}, bf16[1024,512]{1,0:T(8,128)(2,1)}, u32[]{:S(2)}, u32[]{:S(2)}) %collective-permute-start.9) | collective-permute-done | bytes 1048608 | tf_op jit(solution)/shard_map/ppermute | solution.py:328
  180.9 2.7 %raw.3 = (f32[1024,512]{1,0:T(8,128)S(1)}, f32[8,128]{1,0:T(8,128)S(1)}) custom-call(bf16[512,2560]{1,0:T(8,128)(2,1)} %bitcast.4.x_ref, bf16[512,512]{1,0:T(8,128)(2,1)S(1)} %get-tuple-element.60.res_ref, bf16[1024,512]{1,0:T(8,128)(2,1)} %collective-permute-done.8.far_ref, bf16[1024,512]{1,0:T(8,128)(2,1)} %collective-permute-done.9.out_ref, ...), custom_call_target="tpu_custom_call" | custom-call | flops 1099511627776 | bytes 1073741824 | tf_op jit(solution)/shard_map/raw/pallas_call | solution.py:378
  185.0 2.4 %collective-permute-start.14 = (f32[8,128]{1,0:T(8,128)S(1)}, f32[8,128]{1,0:T(8,128)S(1)}, u32[]{:S(2)}, u32[]{:S(2)}) collective-permute-start(f32[8,128]{1,0:T(8,128)S(1)} %get-tuple-element.64), channel_id=1, source_target_pairs={{0,3},{1,2},{2,1},{3,0},{4,7},{5,6},{6,5},{7,4},{8,11},{9,10},{10,... | collective-permute-start | bytes 12296 | tf_op jit(solution)/shard_map/ppermute | solution.py:214
  187.8 2.0 collective-permute-done.14
  189.9 4.1 %collective-permute-done.13 = f32[8,128]{1,0:T(8,128)S(1)} collective-permute-done((f32[8,128]{1,0:T(8,128)S(1)}, f32[8,128]{1,0:T(8,128)S(1)}, u32[]{:S(2)}, u32[]{:S(2)}) %collective-permute-start.13) | collective-permute-done | bytes 4128 | tf_op jit(solution)/shard_map/ppermute | solution.py:214
  195.1 5.4 %collective-permute-start.16 = (f32[8,128]{1,0:T(8,128)S(1)}, f32[8,128]{1,0:T(8,128)S(1)}, u32[]{:S(2)}, u32[]{:S(2)}) collective-permute-start(f32[8,128]{1,0:T(8,128)S(1)} %add_add_fusion.1), channel_id=1, source_target_pairs={{0,8},{1,9},{2,10},{3,11},{4,12},{5,13},{6,14},{7,15},{8,0},{9,1},... | collective-permute-start | bytes 12296 | tf_op jit(solution)/shard_map/ppermute | solution.py:214
  200.5 2.6 %collective-permute-done.17 = f32[8,128]{1,0:T(8,128)S(1)} collective-permute-done((f32[8,128]{1,0:T(8,128)S(1)}, f32[8,128]{1,0:T(8,128)S(1)}, u32[]{:S(2)}, u32[]{:S(2)}) %collective-permute-start.17) | collective-permute-done | bytes 4128 | tf_op jit(solution)/shard_map/ppermute | solution.py:214
  204.7 6.2 %finish.1 = (bf16[512,2048]{1,0:T(8,128)(2,1)}, f32[1,2048,512]{2,1,0:T(8,128)}) custom-call(bf16[512,512]{1,0:T(8,128)(2,1)} %copy-done.9, bf16[512,2048]{1,0:T(8,128)(2,1)} %bitcast.8.got_ref, bf16[512,2048]{1,0:T(8,128)(2,1)} %far_place.1.far_ref, f32[8,128]{1,0:T(8,128)} %add_add_fusion.square_ref, f32[1024,512]{1,0:T(8,128)} %copy-done.3, ...), custom_call_target="tpu_custom_call" | custom-call | flops 1073741824 | bytes 8388608 | tf_op jit(solution)/shard_map/finish/pallas_call | solution.py:414
  (62 shorter events, 24.9 us)
Async XLA Ops:
  5.4 5.4 %copy-start.15 = (s32[1,16,4]{1,2,0:T(4,128)S(1)}, s32[1,16,4]{1,2,0:T(4,128)}, u32[]{:S(2)}) copy-start(s32[1,16,4]{1,2,0:T(4,128)} %param.12) | copy-start | bytes 772
  5.4 61.4 %all-to-all-start = ((bf16[8,64,2560]{2,1,0:T(8,128)(2,1)}), bf16[8,64,2560]{2,1,0:T(8,128)(2,1)S(1)}, u32[]{:S(2)}, u32[]{:S(2)}) async-start(bf16[8,64,2560]{2,1,0:T(8,128)(2,1)} %bitcast.16), calls=%async_computation | async-start | bytes 5242880 | tf_op jit(solution)/shard_map/all_to_all | solution.py:217
  14.2 34.7 %collective-permute-start = (bf16[256,512]{1,0:T(8,128)(2,1)}, bf16[256,512]{1,0:T(8,128)(2,1)S(1)}, u32[]{:S(2)}, u32[]{:S(2)}) collective-permute-start(bf16[256,512]{1,0:T(8,128)(2,1)} %get-tuple-element.37), channel_id=1, source_target_pairs={{0,12},{1,13},{2,14},{3,15},{4,8},{5,9},{6,10},{7,11},{8,4},{9,5},... | collective-permute-start | bytes 786440 | tf_op jit(solution)/shard_map/ppermute | solution.py:211
  17.6 36.9 %collective-permute-start.2 = (bf16[256,512]{1,0:T(8,128)(2,1)}, bf16[256,512]{1,0:T(8,128)(2,1)S(1)}, u32[]{:S(2)}, u32[]{:S(2)}) collective-permute-start(bf16[256,512]{1,0:T(8,128)(2,1)} %get-tuple-element.41), channel_id=1, source_target_pairs={{0,12},{1,13},{2,14},{3,15},{4,8},{5,9},{6,10},{7,11},{8,4},{9,5},... | collective-permute-start | bytes 786440 | tf_op jit(solution)/shard_map/ppermute | solution.py:211
  17.6 42.5 %collective-permute-start.3 = (bf16[256,512]{1,0:T(8,128)(2,1)}, bf16[256,512]{1,0:T(8,128)(2,1)S(1)}, u32[]{:S(2)}, u32[]{:S(2)}) collective-permute-start(bf16[256,512]{1,0:T(8,128)(2,1)} %get-tuple-element.42), channel_id=1, source_target_pairs={{0,12},{1,13},{2,14},{3,15},{4,8},{5,9},{6,10},{7,11},{8,4},{9,5},... | collective-permute-start | bytes 786440 | tf_op jit(solution)/shard_map/ppermute | solution.py:211
  20.8 45.2 %collective-permute-start.4 = (bf16[272,512]{1,0:T(8,128)(2,1)}, bf16[272,512]{1,0:T(8,128)(2,1)S(1)}, u32[]{:S(2)}, u32[]{:S(2)}) collective-permute-start(bf16[272,512]{1,0:T(8,128)(2,1)} %get-tuple-element.43), channel_id=1, source_target_pairs={{0,12},{1,13},{2,14},{3,15},{4,8},{5,9},{6,10},{7,11},{8,4},{9,5},... | collective-permute-start | bytes 835592 | tf_op jit(solution)/shard_map/ppermute | solution.py:211
  48.9 17.2 %collective-permute-start.1 = (bf16[256,512]{1,0:T(8,128)(2,1)S(1)}, bf16[256,512]{1,0:T(8,128)(2,1)S(1)}, u32[]{:S(2)}, u32[]{:S(2)}) collective-permute-start(bf16[256,512]{1,0:T(8,128)(2,1)S(1)} %collective-permute-done.refs_0_), channel_id=1, source_target_pairs={{0,16},{16,0},{1,17},{17,1},{2,18},{18,2},{3,19},{19,3},{4,20},{20... | collective-permute-start | bytes 786440 | tf_op jit(solution)/shard_map/ppermute | solution.py:258
  60.1 6.0 %copy-start.5 = (bf16[256,512]{1,0:T(8,128)(2,1)}, bf16[256,512]{1,0:T(8,128)(2,1)S(1)}, u32[]{:S(2)}) copy-start(bf16[256,512]{1,0:T(8,128)(2,1)S(1)} %collective-permute-done.3.refs_2_) | copy-start | bytes 786436
  66.8 8.0 %copy-start.11 = (s32[1,16,4]{2,1,0:T(8,128)S(1)}, s32[1,16,4]{2,1,0:T(8,128)}, u32[]{:S(2)}) copy-start(s32[1,16,4]{2,1,0:T(8,128)} %copy.9.pattern_ref) | copy-start | bytes 772
  66.8 12.0 %copy-start.12 = (s32[512,1]{0,1:T(1,128)S(1)}, s32[512,1]{0,1:T(1,128)}, u32[]{:S(2)}) copy-start(s32[512,1]{0,1:T(1,128)} %param.8) | copy-start | bytes 6148
  66.8 12.0 %copy-start.14 = (s32[16]{0:T(128)S(1)}, s32[16]{0:T(128)}, u32[]{:S(2)}) copy-start(s32[16]{0:T(128)} %owner_ref.5) | copy-start | bytes 196
  66.8 35.9 %all-to-all-start.1 = ((bf16[8,64,2560]{2,1,0:T(8,128)(2,1)}), bf16[8,64,2560]{2,1,0:T(8,128)(2,1)}, u32[]{:S(2)}, u32[]{:S(2)}) async-start(bf16[8,64,2560]{2,1,0:T(8,128)(2,1)} %bitcast.15), calls=%async_computation.1 | async-start | bytes 5242880 | tf_op jit(solution)/shard_map/all_to_all | solution.py:217
  72.1 19.4 %collective-permute-start.7 = (bf16[272,512]{1,0:T(8,128)(2,1)S(1)}, bf16[272,512]{1,0:T(8,128)(2,1)S(1)}, u32[]{:S(2)}, u32[]{:S(2)}) collective-permute-start(bf16[272,512]{1,0:T(8,128)(2,1)S(1)} %collective-permute-done.4.refs_3_), channel_id=1, source_target_pairs={{0,16},{16,0},{1,17},{17,1},{2,18},{18,2},{3,19},{19,3},{4,20},{20... | collective-permute-start | bytes 835592 | tf_op jit(solution)/shard_map/ppermute | solution.py:258
  73.3 12.6 %collective-permute-start.5 = (bf16[256,512]{1,0:T(8,128)(2,1)S(1)}, bf16[256,512]{1,0:T(8,128)(2,1)S(1)}, u32[]{:S(2)}, u32[]{:S(2)}) collective-permute-start(bf16[256,512]{1,0:T(8,128)(2,1)S(1)} %collective-permute-done.2.refs_1_), channel_id=1, source_target_pairs={{0,16},{16,0},{1,17},{17,1},{2,18},{18,2},{3,19},{19,3},{4,20},{20... | collective-permute-start | bytes 786440 | tf_op jit(solution)/shard_map/ppermute | solution.py:258
  73.6 17.9 %collective-permute-start.6 = (bf16[256,512]{1,0:T(8,128)(2,1)}, bf16[256,512]{1,0:T(8,128)(2,1)S(1)}, u32[]{:S(2)}, u32[]{:S(2)}) collective-permute-start(bf16[256,512]{1,0:T(8,128)(2,1)} %copy-done.5), channel_id=1, source_target_pairs={{0,16},{16,0},{1,17},{17,1},{2,18},{18,2},{3,19},{19,3},{4,20},{20... | collective-permute-start | bytes 786440 | tf_op jit(solution)/shard_map/ppermute | solution.py:258
  74.8 1.6 copy-start
  76.4 15.1 %copy-start.6 = (bf16[256,512]{1,0:T(8,128)(2,1)S(1)}, bf16[256,512]{1,0:T(8,128)(2,1)}, u32[]{:S(2)}) copy-start(bf16[256,512]{1,0:T(8,128)(2,1)} %copy-done.5) | copy-start | bytes 786436
  76.4 15.1 %copy-start.8 = (bf16[256,512]{1,0:T(8,128)(2,1)S(1)}, bf16[256,512]{1,0:T(8,128)(2,1)}, u32[]{:S(2)}) copy-start(bf16[256,512]{1,0:T(8,128)(2,1)} %copy-done.7) | copy-start | bytes 786436
  94.9 53.4 %collective-permute-start.10 = (bf16[1024,512]{1,0:T(8,128)(2,1)}, bf16[1024,512]{1,0:T(8,128)(2,1)}, u32[]{:S(2)}, u32[]{:S(2)}) collective-permute-start(bf16[1024,512]{1,0:T(8,128)(2,1)} %far_raw.2), channel_id=1, source_target_pairs={{4,8},{5,9},{6,10},{7,11},{8,4},{9,5},{10,6},{11,7},{20,24},{21,25... | collective-permute-start | bytes 3145736 | tf_op jit(solution)/shard_map/ppermute | solution.py:326
  98.4 64.2 %collective-permute-start.8 = (bf16[1024,512]{1,0:T(8,128)(2,1)}, bf16[1024,512]{1,0:T(8,128)(2,1)}, u32[]{:S(2)}, u32[]{:S(2)}) collective-permute-start(bf16[1024,512]{1,0:T(8,128)(2,1)} %far_raw.3), channel_id=1, source_target_pairs={{4,8},{5,9},{6,10},{7,11},{8,4},{9,5},{10,6},{11,7},{20,24},{21,25... | collective-permute-start | bytes 3145736 | tf_op jit(solution)/shard_map/ppermute | solution.py:326
  102.7 11.6 %copy-start.2 = (bf16[2048,512]{1,0:T(8,128)(2,1)S(1)}, bf16[2048,512]{1,0:T(8,128)(2,1)}, u32[]{:S(2)}) copy-start(bf16[2048,512]{1,0:T(8,128)(2,1)} %copy-done.1) | copy-start | bytes 6291460
  102.7 11.6 %copy-start.13 = (f32[1,512]{1,0:T(1,128)S(1)}, f32[1,512]{1,0:T(1,128)}, u32[]{:S(2)}) copy-start(f32[1,512]{1,0:T(1,128)} %weight_ref.3) | copy-start | bytes 6148
  102.7 32.2 %all-to-all-start.2 = ((bf16[8,64,2048]{2,1,0:T(8,128)(2,1)}), bf16[8,64,2048]{2,1,0:T(8,128)(2,1)}, u32[]{:S(2)}, u32[]{:S(2)}) async-start(bf16[8,64,2048]{2,1,0:T(8,128)(2,1)} %bitcast.5), calls=%async_computation.2 | async-start | bytes 4194304 | tf_op jit(solution)/shard_map/all_to_all | solution.py:217
  110.0 48.5 %collective-permute-start.11 = (bf16[1024,512]{1,0:T(8,128)(2,1)}, bf16[1024,512]{1,0:T(8,128)(2,1)}, u32[]{:S(2)}, u32[]{:S(2)}) collective-permute-start(bf16[1024,512]{1,0:T(8,128)(2,1)} %far_raw.2), channel_id=1, source_target_pairs={{0,12},{1,13},{2,14},{3,15},{12,0},{13,1},{14,2},{15,3},{16,28},{1... | collective-permute-start | bytes 3145736 | tf_op jit(solution)/shard_map/ppermute | solution.py:328
  134.9 46.0 %collective-permute-start.9 = (bf16[1024,512]{1,0:T(8,128)(2,1)}, bf16[1024,512]{1,0:T(8,128)(2,1)}, u32[]{:S(2)}, u32[]{:S(2)}) collective-permute-start(bf16[1024,512]{1,0:T(8,128)(2,1)} %far_raw.3), channel_id=1, source_target_pairs={{0,12},{1,13},{2,14},{3,15},{12,0},{13,1},{14,2},{15,3},{16,28},{1... | collective-permute-start | bytes 3145736 | tf_op jit(solution)/shard_map/ppermute | solution.py:328
  142.0 62.7 %all-to-all-start.3 = ((bf16[8,64,2048]{2,1,0:T(8,128)(2,1)}), bf16[8,64,2048]{2,1,0:T(8,128)(2,1)}, u32[]{:S(2)}, u32[]{:S(2)}) async-start(bf16[8,64,2048]{2,1,0:T(8,128)(2,1)} %bitcast.7), calls=%async_computation.3 | async-start | bytes 4194304 | tf_op jit(solution)/shard_map/all_to_all | solution.py:217
  185.0 4.9 %collective-permute-start.14 = (f32[8,128]{1,0:T(8,128)S(1)}, f32[8,128]{1,0:T(8,128)S(1)}, u32[]{:S(2)}, u32[]{:S(2)}) collective-permute-start(f32[8,128]{1,0:T(8,128)S(1)} %get-tuple-element.64), channel_id=1, source_target_pairs={{0,3},{1,2},{2,1},{3,0},{4,7},{5,6},{6,5},{7,4},{8,11},{9,10},{10,... | collective-permute-start | bytes 12296 | tf_op jit(solution)/shard_map/ppermute | solution.py:214
  187.4 6.5 %collective-permute-start.13 = (f32[8,128]{1,0:T(8,128)S(1)}, f32[8,128]{1,0:T(8,128)S(1)}, u32[]{:S(2)}, u32[]{:S(2)}) collective-permute-start(f32[8,128]{1,0:T(8,128)S(1)} %get-tuple-element.64), channel_id=1, source_target_pairs={{0,2},{1,3},{2,0},{3,1},{4,6},{5,7},{6,4},{7,5},{8,10},{9,11},{10,... | collective-permute-start | bytes 12296 | tf_op jit(solution)/shard_map/ppermute | solution.py:214
  187.7 6.2 %collective-permute-start.12 = (f32[8,128]{1,0:T(8,128)S(1)}, f32[8,128]{1,0:T(8,128)S(1)}, u32[]{:S(2)}, u32[]{:S(2)}) collective-permute-start(f32[8,128]{1,0:T(8,128)S(1)} %get-tuple-element.64), channel_id=1, source_target_pairs={{0,1},{1,0},{2,3},{3,2},{4,5},{5,4},{6,7},{7,6},{8,9},{9,8},{10,11... | collective-permute-start | bytes 12296 | tf_op jit(solution)/shard_map/ppermute | solution.py:214
  193.9 9.2 %collective-permute-start.17 = (f32[8,128]{1,0:T(8,128)S(1)}, f32[8,128]{1,0:T(8,128)S(1)}, u32[]{:S(2)}, u32[]{:S(2)}) collective-permute-start(f32[8,128]{1,0:T(8,128)S(1)} %add_add_fusion.1), channel_id=1, source_target_pairs={{0,12},{1,13},{2,14},{3,15},{4,8},{5,9},{6,10},{7,11},{8,4},{9,5},... | collective-permute-start | bytes 12296 | tf_op jit(solution)/shard_map/ppermute | solution.py:214
  195.1 8.0 %collective-permute-start.16 = (f32[8,128]{1,0:T(8,128)S(1)}, f32[8,128]{1,0:T(8,128)S(1)}, u32[]{:S(2)}, u32[]{:S(2)}) collective-permute-start(f32[8,128]{1,0:T(8,128)S(1)} %add_add_fusion.1), channel_id=1, source_target_pairs={{0,8},{1,9},{2,10},{3,11},{4,12},{5,13},{6,14},{7,15},{8,0},{9,1},... | collective-permute-start | bytes 12296 | tf_op jit(solution)/shard_map/ppermute | solution.py:214
  200.5 3.6 %collective-permute-start.15 = (f32[8,128]{1,0:T(8,128)S(1)}, f32[8,128]{1,0:T(8,128)S(1)}, u32[]{:S(2)}, u32[]{:S(2)}) collective-permute-start(f32[8,128]{1,0:T(8,128)S(1)} %add_add_fusion.1), channel_id=1, source_target_pairs={{0,4},{1,5},{2,6},{3,7},{4,0},{5,1},{6,2},{7,3},{8,12},{9,13},{10,... | collective-permute-start | bytes 12296 | tf_op jit(solution)/shard_map/ppermute | solution.py:214
  (6 other events, 6.4 us)

commit v10 on v9

--- a/solution.py
+++ b/solution.py
@@ -270,7 +270,7 @@
         out_specs=[VMEM, VMEM],
         out_shape=[jax.ShapeDtypeStruct((rows, placed), BF16)] * 2,
         compiler_params=SMALL,
-        cost_estimate=cost(2 * rows * rows * 128, 4 * rows * placed),
+        cost_estimate=LATE,
         name="back_places",
     )(inst, owner_slot)
     effective = pl.pallas_call(
@@ -279,7 +279,7 @@
         out_specs=VMEM,
         out_shape=jax.ShapeDtypeStruct((width, channels), BF16),
         compiler_params=SMALL,
-        cost_estimate=cost(width * channels, 4 * width * channels),
+        cost_estimate=LATE,
         name="effective",
     )(head_weights, block_pattern)
     far_x, effective, near_back, far_back = lax.optimization_barrier(

time: 212 us -> 211 us (level)
  Pallas kernels: 42.5 us -> 47.8 us
  waiting for transfers between devices: 103 us -> 98.8 us
    ppermute x4, waiting for transfers between devices: 9.92 us -> 0.01 us  [per_device(): lax.ppermute(x, 'grp', swap)]
    all_to_all x4, waiting for transfers between devices: 15.8 us -> 25.3 us  [in_half(): lax.all_to_all(x, 'loc', split_axis=0, concat_axis=0, tiled=True, axis_in...]
    ppermute x4, waiting for transfers between devices: 39.3 us -> 32.3 us  [partner(): return lax.ppermute(x, 'loc', [(i, i ^ apart) for i in range(members)])]
    ppermute x6, starting transfers between devices: 9.46 us -> 6.46 us  [hop(): return lax.ppermute(x, 'loc', [(i, i ^ distance) for i in range(members)])]
    ppermute x6, waiting for transfers between devices: 9.66 us -> 12.6 us  [hop(): return lax.ppermute(x, 'loc', [(i, i ^ distance) for i in range(members)])]
    unnamed x33 -> x23, local copies, waits for them, and re-layouts: 8.65 us -> 8.58 us
  transfers between devices with their start and end apart: 22 -> 22, of which waited for: 14 -> 11; matrix products, arithmetic and copies ran while one was open for 1% -> 0% of each run, Pallas kernels for 15% -> 16%
where the time goes in v10:
time: 211 us; the launch traced here: 210 us
  waiting for transfers between devices  98.8 us (47%)
  starting transfers between devices  53.1 us (25%)
  Pallas kernels  47.8 us (23%)
  local copies, waits for them, and re-layouts  8.58 us (4%)
    ppermute x4, waiting for transfers between devices, partner(): return lax.ppermute(x, 'loc', [(i, i ^ apart) for i in range(members)])  32.3 us
    ppermute x2, waiting for transfers between devices, per_device(): lax.ppermute(part, 'loc', [(i, i ^ apart) for i in outer])  28.6 us
    all_to_all x4, waiting for transfers between devices, in_half(): lax.all_to_all(x, 'loc', split_axis=0, concat_axis=0, tiled=True, axis_in...  25.3 us
    all_to_all x4, starting transfers between devices, in_half(): lax.all_to_all(x, 'loc', split_axis=0, concat_axis=0, tiled=True, axis_in...  22.2 us
    ppermute x6, waiting for transfers between devices, hop(): return lax.ppermute(x, 'loc', [(i, i ^ distance) for i in range(members)])  12.6 us
    pallas_call x2, Pallas kernels, prep(): pl.pallas_call(functools.partial(prep_kernel, heads, capacity, near), gri...  9.39 us
    unnamed x23, local copies, waits for them, and re-layouts  8.58 us
    ppermute x2, starting transfers between devices, per_device(): lax.ppermute(part, 'loc', [(i, i ^ apart) for i in outer])  8.49 us
  transfers between devices with their start and end apart: 22, of which 11 were waited for; matrix products, arithmetic and copies ran while one was open for 0% of the time, Pallas kernels for 16%

profile of v10, /device:TPU:1, one launch (start us, length us, event | category | flops | bytes accessed | tf_op | source)
XLA Modules:
  0.0 209.7 jit_solution(7170623791752811380)
XLA Ops:
  2.0 4.7 %prep_far.1 = bf16[512,2560]{1,0:T(8,128)(2,1)} custom-call(s32[1,512]{1,0:T(1,128)} %bitcast.9, s32[16]{0:T(128)} %owner_ref.5, bf16[512,2048]{1,0:T(8,128)(2,1)} %x_ref.3, bf16[512,512]{1,0:T(8,128)(2,1)} %t_ref.3), custom_call_target="tpu_custom_call" | custom-call | flops 1342177280 | bytes 5242880 | tf_op jit(solution)/shard_map/prep_far/pallas_call | solution.py:224
  6.7 2.7 %piece.1 = (bf16[256,512]{1,0:T(8,128)(2,1)}, bf16[256,512]{1,0:T(8,128)(2,1)}, bf16[256,512]{1,0:T(8,128)(2,1)}, bf16[272,512]{1,0:T(8,128)(2,1)}) custom-call(bf16[1,2048,512]{2,1,0:T(8,128)(2,1)} %w_ref.1, s32[1,16,4]{2,1,0:T(8,128)} %copy.9.pattern_ref, f32[1,512]{1,0:T(1,128)} %weight_ref.3), custom_call_target="tpu_custom_call" | custom-call | flops 524288 | bytes 2097152 | tf_op jit(solution)/shard_map/piece/pallas_call | solution.py:240
  9.4 4.2 %collective-permute-start = (bf16[256,512]{1,0:T(8,128)(2,1)}, bf16[256,512]{1,0:T(8,128)(2,1)}, u32[]{:S(2)}, u32[]{:S(2)}) collective-permute-start(bf16[256,512]{1,0:T(8,128)(2,1)} %get-tuple-element.37), channel_id=1, source_target_pairs={{0,12},{1,13},{2,14},{3,15},{4,8},{5,9},{6,10},{7,11},{8,4},{9,5},... | collective-permute-start | bytes 786440 | tf_op jit(solution)/shard_map/ppermute | solution.py:211
  13.5 5.2 %all-to-all-start = ((bf16[8,64,2560]{2,1,0:T(8,128)(2,1)}), bf16[8,64,2560]{2,1,0:T(8,128)(2,1)}, u32[]{:S(2)}, u32[]{:S(2)}) async-start(bf16[8,64,2560]{2,1,0:T(8,128)(2,1)} %bitcast.13), calls=%async_computation | async-start | bytes 5242880 | tf_op jit(solution)/shard_map/all_to_all | solution.py:217
  19.0 3.0 %collective-permute-start.3 = (bf16[256,512]{1,0:T(8,128)(2,1)}, bf16[256,512]{1,0:T(8,128)(2,1)}, u32[]{:S(2)}, u32[]{:S(2)}) collective-permute-start(bf16[256,512]{1,0:T(8,128)(2,1)} %get-tuple-element.42), channel_id=1, source_target_pairs={{0,12},{1,13},{2,14},{3,15},{4,8},{5,9},{6,10},{7,11},{8,4},{9,5},... | collective-permute-start | bytes 786440 | tf_op jit(solution)/shard_map/ppermute | solution.py:211
  22.3 4.7 %prep_near.1 = bf16[512,2560]{1,0:T(8,128)(2,1)} custom-call(s32[1,512]{1,0:T(1,128)} %bitcast.10, s32[16]{0:T(128)} %owner_ref.5, bf16[512,2048]{1,0:T(8,128)(2,1)} %x_ref.3, bf16[512,512]{1,0:T(8,128)(2,1)} %t_ref.3), custom_call_target="tpu_custom_call" | custom-call | flops 1342177280 | bytes 5242880 | tf_op jit(solution)/shard_map/prep_near/pallas_call | solution.py:224
  31.0 23.2 %collective-permute-done.2.refs_1_ = bf16[256,512]{1,0:T(8,128)(2,1)} collective-permute-done((bf16[256,512]{1,0:T(8,128)(2,1)}, bf16[256,512]{1,0:T(8,128)(2,1)}, u32[]{:S(2)}, u32[]{:S(2)}) %collective-permute-start.2) | collective-permute-done | bytes 262176 | tf_op jit(solution)/shard_map/ppermute | solution.py:211
  55.4 4.4 %collective-permute-done.3.refs_2_ = bf16[256,512]{1,0:T(8,128)(2,1)} collective-permute-done((bf16[256,512]{1,0:T(8,128)(2,1)}, bf16[256,512]{1,0:T(8,128)(2,1)}, u32[]{:S(2)}, u32[]{:S(2)}) %collective-permute-start.3) | collective-permute-done | bytes 262176 | tf_op jit(solution)/shard_map/ppermute | solution.py:211
  61.0 4.8 %collective-permute-done.4.refs_3_ = bf16[272,512]{1,0:T(8,128)(2,1)} collective-permute-done((bf16[272,512]{1,0:T(8,128)(2,1)}, bf16[272,512]{1,0:T(8,128)(2,1)}, u32[]{:S(2)}, u32[]{:S(2)}) %collective-permute-start.4) | collective-permute-done | bytes 278560 | tf_op jit(solution)/shard_map/ppermute | solution.py:211
  67.0 5.5 %all-to-all-start.1 = ((bf16[8,64,2560]{2,1,0:T(8,128)(2,1)}), bf16[8,64,2560]{2,1,0:T(8,128)(2,1)}, u32[]{:S(2)}, u32[]{:S(2)}) async-start(bf16[8,64,2560]{2,1,0:T(8,128)(2,1)} %bitcast.12), calls=%async_computation.1 | async-start | bytes 5242880 | tf_op jit(solution)/shard_map/all_to_all | solution.py:217
  74.9 3.4 %far_res.1.res_ref = bf16[512,512]{1,0:T(8,128)(2,1)S(1)} custom-call(bf16[512,2560]{1,0:T(8,128)(2,1)} %bitcast.2.x_ref, bf16[256,512]{1,0:T(8,128)(2,1)} %collective-permute-done.refs_0_, bf16[256,512]{1,0:T(8,128)(2,1)} %collective-permute-done.2.refs_1_, bf16[256,512]{1,0:T(8,128)(2,1)} %collective-permute-done.3.refs_2_, ...), custom_call_target="tpu_custom_call" | custom-call | flops 1073741824 | bytes 2621440 | tf_op jit(solution)/shard_map/far_res/pallas_call | solution.py:293
  78.3 2.8 %far_raw.2 = bf16[1024,512]{1,0:T(8,128)(2,1)} custom-call(bf16[512,2560]{1,0:T(8,128)(2,1)} %bitcast.2.x_ref, bf16[512,512]{1,0:T(8,128)(2,1)S(1)} %far_res.1.res_ref), custom_call_target="tpu_custom_call" | custom-call | flops 536870912 | bytes 2097152 | tf_op jit(solution)/shard_map/far_raw/pallas_call | solution.py:308
  82.9 2.8 %far_raw.3 = bf16[1024,512]{1,0:T(8,128)(2,1)} custom-call(bf16[512,2560]{1,0:T(8,128)(2,1)} %bitcast.2.x_ref, bf16[512,512]{1,0:T(8,128)(2,1)S(1)} %far_res.1.res_ref), custom_call_target="tpu_custom_call" | custom-call | flops 536870912 | bytes 2097152 | tf_op jit(solution)/shard_map/far_raw/pallas_call | solution.py:308
  87.3 4.0 %far_grad.1 = bf16[512,2048]{1,0:T(8,128)(2,1)} custom-call(bf16[512,512]{1,0:T(8,128)(2,1)S(1)} %far_res.1.res_ref, bf16[256,512]{1,0:T(8,128)(2,1)} %collective-permute-done.refs_0_, bf16[256,512]{1,0:T(8,128)(2,1)} %collective-permute-done.2.refs_1_, bf16[256,512]{1,0:T(8,128)(2,1)} %collective-permute-done.3.refs_2_, ...), custom_call_target="tpu_custom_call" | custom-call | flops 1073741824 | bytes 2621440 | tf_op jit(solution)/shard_map/far_grad/pallas_call | solution.py:331
  91.3 11.7 %all-to-all-done.1 = bf16[8,64,2560]{2,1,0:T(8,128)(2,1)} async-done(((bf16[8,64,2560]{2,1,0:T(8,128)(2,1)}), bf16[8,64,2560]{2,1,0:T(8,128)(2,1)}, u32[]{:S(2)}, u32[]{:S(2)}) %all-to-all-start.1) | async-done | bytes 2621472 | tf_op jit(solution)/shard_map/all_to_all | solution.py:217
  103.1 5.2 %all-to-all-start.2 = ((bf16[8,64,2048]{2,1,0:T(8,128)(2,1)}), bf16[8,64,2048]{2,1,0:T(8,128)(2,1)}, u32[]{:S(2)}, u32[]{:S(2)}) async-start(bf16[8,64,2048]{2,1,0:T(8,128)(2,1)} %bitcast.5), calls=%async_computation.2 | async-start | bytes 4194304 | tf_op jit(solution)/shard_map/all_to_all | solution.py:217
  108.3 4.8 %collective-permute-start.11 = (bf16[1024,512]{1,0:T(8,128)(2,1)}, bf16[1024,512]{1,0:T(8,128)(2,1)}, u32[]{:S(2)}, u32[]{:S(2)}) collective-permute-start(bf16[1024,512]{1,0:T(8,128)(2,1)} %far_raw.2), channel_id=1, source_target_pairs={{0,12},{1,13},{2,14},{3,15},{12,0},{13,1},{14,2},{15,3},{16,28},{1... | collective-permute-start | bytes 3145736 | tf_op jit(solution)/shard_map/ppermute | solution.py:328
  114.7 5.0 %near_head.1 = (bf16[512,2048]{1,0:T(8,128)(2,1)}, bf16[512,512]{1,0:T(8,128)(2,1)S(1)}) custom-call(bf16[512,2560]{1,0:T(8,128)(2,1)} %bitcast.4.x_ref, bf16[2048,512]{1,0:T(8,128)(2,1)S(1)} %copy-done.10, f32[1,512]{1,0:T(1,128)S(1)} %copy-done.7), custom_call_target="tpu_custom_call" | custom-call | flops 1099511627776 | bytes 1073741824 | tf_op jit(solution)/shard_map/near_head/pallas_call | solution.py:343
  119.7 13.6 %all-to-all-done.2 = bf16[8,64,2048]{2,1,0:T(8,128)(2,1)} async-done(((bf16[8,64,2048]{2,1,0:T(8,128)(2,1)}), bf16[8,64,2048]{2,1,0:T(8,128)(2,1)}, u32[]{:S(2)}, u32[]{:S(2)}) %all-to-all-start.2) | async-done | bytes 2097184 | tf_op jit(solution)/shard_map/all_to_all | solution.py:217
  133.3 3.7 %collective-permute-start.9 = (bf16[1024,512]{1,0:T(8,128)(2,1)}, bf16[1024,512]{1,0:T(8,128)(2,1)}, u32[]{:S(2)}, u32[]{:S(2)}) collective-permute-start(bf16[1024,512]{1,0:T(8,128)(2,1)} %far_raw.3), channel_id=1, source_target_pairs={{0,12},{1,13},{2,14},{3,15},{12,0},{13,1},{14,2},{15,3},{16,28},{1... | collective-permute-start | bytes 3145736 | tf_op jit(solution)/shard_map/ppermute | solution.py:328
  137.0 3.8 %far_place.1.far_ref = bf16[512,2048]{1,0:T(8,128)(2,1)} custom-call(bf16[512,512]{1,0:T(8,128)(2,1)} %copy-done.4, bf16[512,2048]{1,0:T(8,128)(2,1)} %bitcast.6.got_ref), custom_call_target="tpu_custom_call" | custom-call | flops 1073741824 | bytes 4194304 | tf_op jit(solution)/shard_map/far_place/pallas_call | solution.py:364
  140.8 6.2 %all-to-all-start.3 = ((bf16[8,64,2048]{2,1,0:T(8,128)(2,1)}), bf16[8,64,2048]{2,1,0:T(8,128)(2,1)}, u32[]{:S(2)}, u32[]{:S(2)}) async-start(bf16[8,64,2048]{2,1,0:T(8,128)(2,1)} %bitcast.7), calls=%async_computation.3 | async-start | bytes 4194304 | tf_op jit(solution)/shard_map/all_to_all | solution.py:217
  147.1 10.1 %collective-permute-done.11.out_ref = bf16[1024,512]{1,0:T(8,128)(2,1)} collective-permute-done((bf16[1024,512]{1,0:T(8,128)(2,1)}, bf16[1024,512]{1,0:T(8,128)(2,1)}, u32[]{:S(2)}, u32[]{:S(2)}) %collective-permute-start.11) | collective-permute-done | bytes 1048608 | tf_op jit(solution)/shard_map/ppermute | solution.py:328
  157.2 2.7 %raw.2 = (f32[1024,512]{1,0:T(8,128)S(1)}, f32[8,128]{1,0:T(8,128)S(1)}) custom-call(bf16[512,2560]{1,0:T(8,128)(2,1)} %bitcast.4.x_ref, bf16[512,512]{1,0:T(8,128)(2,1)S(1)} %get-tuple-element.60.res_ref, bf16[1024,512]{1,0:T(8,128)(2,1)} %collective-permute-done.10.far_ref, bf16[1024,512]{1,0:T(8,128)(2,1)} %collective-permute-done.11.out_ref, ...), custom_call_target="tpu_custom_call" | custom-call | flops 1099511627776 | bytes 1073741824 | tf_op jit(solution)/shard_map/raw/pallas_call | solution.py:378
  161.3 18.4 %collective-permute-done.9.out_ref = bf16[1024,512]{1,0:T(8,128)(2,1)} collective-permute-done((bf16[1024,512]{1,0:T(8,128)(2,1)}, bf16[1024,512]{1,0:T(8,128)(2,1)}, u32[]{:S(2)}, u32[]{:S(2)}) %collective-permute-start.9) | collective-permute-done | bytes 1048608 | tf_op jit(solution)/shard_map/ppermute | solution.py:328
  179.7 2.7 %raw.3 = (f32[1024,512]{1,0:T(8,128)S(1)}, f32[8,128]{1,0:T(8,128)S(1)}) custom-call(bf16[512,2560]{1,0:T(8,128)(2,1)} %bitcast.4.x_ref, bf16[512,512]{1,0:T(8,128)(2,1)S(1)} %get-tuple-element.60.res_ref, bf16[1024,512]{1,0:T(8,128)(2,1)} %collective-permute-done.8.far_ref, bf16[1024,512]{1,0:T(8,128)(2,1)} %collective-permute-done.9.out_ref, ...), custom_call_target="tpu_custom_call" | custom-call | flops 1099511627776 | bytes 1073741824 | tf_op jit(solution)/shard_map/raw/pallas_call | solution.py:378
  183.8 2.4 %collective-permute-start.14 = (f32[8,128]{1,0:T(8,128)S(1)}, f32[8,128]{1,0:T(8,128)S(1)}, u32[]{:S(2)}, u32[]{:S(2)}) collective-permute-start(f32[8,128]{1,0:T(8,128)S(1)} %get-tuple-element.64), channel_id=1, source_target_pairs={{0,3},{1,2},{2,1},{3,0},{4,7},{5,6},{6,5},{7,4},{8,11},{9,10},{10,... | collective-permute-start | bytes 12296 | tf_op jit(solution)/shard_map/ppermute | solution.py:214
  186.7 2.0 collective-permute-done.14
  188.7 4.0 %collective-permute-done.13 = f32[8,128]{1,0:T(8,128)S(1)} collective-permute-done((f32[8,128]{1,0:T(8,128)S(1)}, f32[8,128]{1,0:T(8,128)S(1)}, u32[]{:S(2)}, u32[]{:S(2)}) %collective-permute-start.13) | collective-permute-done | bytes 4128 | tf_op jit(solution)/shard_map/ppermute | solution.py:214
  193.3 3.0 %collective-permute-start.15 = (f32[8,128]{1,0:T(8,128)S(1)}, f32[8,128]{1,0:T(8,128)S(1)}, u32[]{:S(2)}, u32[]{:S(2)}) collective-permute-start(f32[8,128]{1,0:T(8,128)S(1)} %add_add_fusion.1), channel_id=1, source_target_pairs={{0,4},{1,5},{2,6},{3,7},{4,0},{5,1},{6,2},{7,3},{8,12},{9,13},{10,... | collective-permute-start | bytes 12296 | tf_op jit(solution)/shard_map/ppermute | solution.py:214
  196.3 5.6 %collective-permute-done.17 = f32[8,128]{1,0:T(8,128)S(1)} collective-permute-done((f32[8,128]{1,0:T(8,128)S(1)}, f32[8,128]{1,0:T(8,128)S(1)}, u32[]{:S(2)}, u32[]{:S(2)}) %collective-permute-start.17) | collective-permute-done | bytes 4128 | tf_op jit(solution)/shard_map/ppermute | solution.py:214
  203.4 6.2 %finish.1 = (bf16[512,2048]{1,0:T(8,128)(2,1)}, f32[1,2048,512]{2,1,0:T(8,128)}) custom-call(bf16[512,512]{1,0:T(8,128)(2,1)} %copy-done.3, bf16[512,2048]{1,0:T(8,128)(2,1)} %bitcast.8.got_ref, bf16[512,2048]{1,0:T(8,128)(2,1)} %far_place.1.far_ref, f32[8,128]{1,0:T(8,128)} %add_add_fusion.square_ref, f32[1024,512]{1,0:T(8,128)} %copy-done.1, ...), custom_call_target="tpu_custom_call" | custom-call | flops 1073741824 | bytes 8388608 | tf_op jit(solution)/shard_map/finish/pallas_call | solution.py:414
  (52 shorter events, 22.2 us)
Async XLA Ops:
  9.4 17.6 %collective-permute-start = (bf16[256,512]{1,0:T(8,128)(2,1)}, bf16[256,512]{1,0:T(8,128)(2,1)}, u32[]{:S(2)}, u32[]{:S(2)}) collective-permute-start(bf16[256,512]{1,0:T(8,128)(2,1)} %get-tuple-element.37), channel_id=1, source_target_pairs={{0,12},{1,13},{2,14},{3,15},{4,8},{5,9},{6,10},{7,11},{8,4},{9,5},... | collective-permute-start | bytes 786440 | tf_op jit(solution)/shard_map/ppermute | solution.py:211
  13.5 53.4 %all-to-all-start = ((bf16[8,64,2560]{2,1,0:T(8,128)(2,1)}), bf16[8,64,2560]{2,1,0:T(8,128)(2,1)}, u32[]{:S(2)}, u32[]{:S(2)}) async-start(bf16[8,64,2560]{2,1,0:T(8,128)(2,1)} %bitcast.13), calls=%async_computation | async-start | bytes 5242880 | tf_op jit(solution)/shard_map/all_to_all | solution.py:217
  18.8 35.4 %collective-permute-start.2 = (bf16[256,512]{1,0:T(8,128)(2,1)}, bf16[256,512]{1,0:T(8,128)(2,1)}, u32[]{:S(2)}, u32[]{:S(2)}) collective-permute-start(bf16[256,512]{1,0:T(8,128)(2,1)} %get-tuple-element.41), channel_id=1, source_target_pairs={{0,12},{1,13},{2,14},{3,15},{4,8},{5,9},{6,10},{7,11},{8,4},{9,5},... | collective-permute-start | bytes 786440 | tf_op jit(solution)/shard_map/ppermute | solution.py:211
  19.0 40.7 %collective-permute-start.3 = (bf16[256,512]{1,0:T(8,128)(2,1)}, bf16[256,512]{1,0:T(8,128)(2,1)}, u32[]{:S(2)}, u32[]{:S(2)}) collective-permute-start(bf16[256,512]{1,0:T(8,128)(2,1)} %get-tuple-element.42), channel_id=1, source_target_pairs={{0,12},{1,13},{2,14},{3,15},{4,8},{5,9},{6,10},{7,11},{8,4},{9,5},... | collective-permute-start | bytes 786440 | tf_op jit(solution)/shard_map/ppermute | solution.py:211
  22.0 6.2 %copy-start.6 = (s32[512,1]{0,1:T(1,128)S(1)}, s32[512,1]{0,1:T(1,128)}, u32[]{:S(2)}) copy-start(s32[512,1]{0,1:T(1,128)} %param.8) | copy-start | bytes 6148
  22.0 6.2 %copy-start.8 = (s32[16]{0:T(128)S(1)}, s32[16]{0:T(128)}, u32[]{:S(2)}) copy-start(s32[16]{0:T(128)} %owner_ref.5) | copy-start | bytes 196
  22.0 43.7 %collective-permute-start.4 = (bf16[272,512]{1,0:T(8,128)(2,1)}, bf16[272,512]{1,0:T(8,128)(2,1)}, u32[]{:S(2)}, u32[]{:S(2)}) collective-permute-start(bf16[272,512]{1,0:T(8,128)(2,1)} %get-tuple-element.43), channel_id=1, source_target_pairs={{0,12},{1,13},{2,14},{3,15},{4,8},{5,9},{6,10},{7,11},{8,4},{9,5},... | collective-permute-start | bytes 835592 | tf_op jit(solution)/shard_map/ppermute | solution.py:211
  27.0 40.0 %collective-permute-start.1 = (bf16[256,512]{1,0:T(8,128)(2,1)}, bf16[256,512]{1,0:T(8,128)(2,1)}, u32[]{:S(2)}, u32[]{:S(2)}) collective-permute-start(bf16[256,512]{1,0:T(8,128)(2,1)} %collective-permute-done.refs_0_), channel_id=1, source_target_pairs={{0,16},{16,0},{1,17},{17,1},{2,18},{18,2},{3,19},{19,3},{4,20},{20... | collective-permute-start | bytes 786440 | tf_op jit(solution)/shard_map/ppermute | solution.py:258
  29.4 0.8 copy-start.3
  54.1 20.8 %collective-permute-start.5 = (bf16[256,512]{1,0:T(8,128)(2,1)}, bf16[256,512]{1,0:T(8,128)(2,1)}, u32[]{:S(2)}, u32[]{:S(2)}) collective-permute-start(bf16[256,512]{1,0:T(8,128)(2,1)} %collective-permute-done.2.refs_1_), channel_id=1, source_target_pairs={{0,16},{16,0},{1,17},{17,1},{2,18},{18,2},{3,19},{19,3},{4,20},{20... | collective-permute-start | bytes 786440 | tf_op jit(solution)/shard_map/ppermute | solution.py:258
  59.8 15.1 %collective-permute-start.6 = (bf16[256,512]{1,0:T(8,128)(2,1)}, bf16[256,512]{1,0:T(8,128)(2,1)}, u32[]{:S(2)}, u32[]{:S(2)}) collective-permute-start(bf16[256,512]{1,0:T(8,128)(2,1)} %collective-permute-done.3.refs_2_), channel_id=1, source_target_pairs={{0,16},{16,0},{1,17},{17,1},{2,18},{18,2},{3,19},{19,3},{4,20},{20... | collective-permute-start | bytes 786440 | tf_op jit(solution)/shard_map/ppermute | solution.py:258
  65.7 9.2 %collective-permute-start.7 = (bf16[272,512]{1,0:T(8,128)(2,1)}, bf16[272,512]{1,0:T(8,128)(2,1)}, u32[]{:S(2)}, u32[]{:S(2)}) collective-permute-start(bf16[272,512]{1,0:T(8,128)(2,1)} %collective-permute-done.4.refs_3_), channel_id=1, source_target_pairs={{0,16},{16,0},{1,17},{17,1},{2,18},{18,2},{3,19},{19,3},{4,20},{20... | collective-permute-start | bytes 835592 | tf_op jit(solution)/shard_map/ppermute | solution.py:258
  67.0 5.5 %copy-start = (bf16[1,2048,512]{2,1,0:T(8,128)(2,1)S(1)}, bf16[1,2048,512]{2,1,0:T(8,128)(2,1)}, u32[]{:S(2)}) copy-start(bf16[1,2048,512]{2,1,0:T(8,128)(2,1)} %w_ref.1) | copy-start | bytes 6291460
  67.0 5.5 %copy-start.5 = (s32[1,16,4]{2,1,0:T(8,128)S(1)}, s32[1,16,4]{2,1,0:T(8,128)}, u32[]{:S(2)}) copy-start(s32[1,16,4]{2,1,0:T(8,128)} %copy.9.pattern_ref) | copy-start | bytes 772
  67.0 36.1 %all-to-all-start.1 = ((bf16[8,64,2560]{2,1,0:T(8,128)(2,1)}), bf16[8,64,2560]{2,1,0:T(8,128)(2,1)}, u32[]{:S(2)}, u32[]{:S(2)}) async-start(bf16[8,64,2560]{2,1,0:T(8,128)(2,1)} %bitcast.12), calls=%async_computation.1 | async-start | bytes 5242880 | tf_op jit(solution)/shard_map/all_to_all | solution.py:217
  73.6 1.3 copy-start.9
  81.2 65.9 %collective-permute-start.10 = (bf16[1024,512]{1,0:T(8,128)(2,1)}, bf16[1024,512]{1,0:T(8,128)(2,1)}, u32[]{:S(2)}, u32[]{:S(2)}) collective-permute-start(bf16[1024,512]{1,0:T(8,128)(2,1)} %far_raw.2), channel_id=1, source_target_pairs={{4,8},{5,9},{6,10},{7,11},{8,4},{9,5},{10,6},{11,7},{20,24},{21,25... | collective-permute-start | bytes 3145736 | tf_op jit(solution)/shard_map/ppermute | solution.py:326
  85.7 75.6 %collective-permute-start.8 = (bf16[1024,512]{1,0:T(8,128)(2,1)}, bf16[1024,512]{1,0:T(8,128)(2,1)}, u32[]{:S(2)}, u32[]{:S(2)}) collective-permute-start(bf16[1024,512]{1,0:T(8,128)(2,1)} %far_raw.3), channel_id=1, source_target_pairs={{4,8},{5,9},{6,10},{7,11},{8,4},{9,5},{10,6},{11,7},{20,24},{21,25... | collective-permute-start | bytes 3145736 | tf_op jit(solution)/shard_map/ppermute | solution.py:326
  103.1 10.0 %copy-start.7 = (f32[1,512]{1,0:T(1,128)S(1)}, f32[1,512]{1,0:T(1,128)}, u32[]{:S(2)}) copy-start(f32[1,512]{1,0:T(1,128)} %weight_ref.3) | copy-start | bytes 6148
  103.1 30.2 %all-to-all-start.2 = ((bf16[8,64,2048]{2,1,0:T(8,128)(2,1)}), bf16[8,64,2048]{2,1,0:T(8,128)(2,1)}, u32[]{:S(2)}, u32[]{:S(2)}) async-start(bf16[8,64,2048]{2,1,0:T(8,128)(2,1)} %bitcast.5), calls=%async_computation.2 | async-start | bytes 4194304 | tf_op jit(solution)/shard_map/all_to_all | solution.py:217
  108.3 48.9 %collective-permute-start.11 = (bf16[1024,512]{1,0:T(8,128)(2,1)}, bf16[1024,512]{1,0:T(8,128)(2,1)}, u32[]{:S(2)}, u32[]{:S(2)}) collective-permute-start(bf16[1024,512]{1,0:T(8,128)(2,1)} %far_raw.2), channel_id=1, source_target_pairs={{0,12},{1,13},{2,14},{3,15},{12,0},{13,1},{14,2},{15,3},{16,28},{1... | collective-permute-start | bytes 3145736 | tf_op jit(solution)/shard_map/ppermute | solution.py:328
  113.1 1.6 copy-start.10
  133.3 46.5 %collective-permute-start.9 = (bf16[1024,512]{1,0:T(8,128)(2,1)}, bf16[1024,512]{1,0:T(8,128)(2,1)}, u32[]{:S(2)}, u32[]{:S(2)}) collective-permute-start(bf16[1024,512]{1,0:T(8,128)(2,1)} %far_raw.3), channel_id=1, source_target_pairs={{0,12},{1,13},{2,14},{3,15},{12,0},{13,1},{14,2},{15,3},{16,28},{1... | collective-permute-start | bytes 3145736 | tf_op jit(solution)/shard_map/ppermute | solution.py:328
  140.8 62.6 %all-to-all-start.3 = ((bf16[8,64,2048]{2,1,0:T(8,128)(2,1)}), bf16[8,64,2048]{2,1,0:T(8,128)(2,1)}, u32[]{:S(2)}, u32[]{:S(2)}) async-start(bf16[8,64,2048]{2,1,0:T(8,128)(2,1)} %bitcast.7), calls=%async_computation.3 | async-start | bytes 4194304 | tf_op jit(solution)/shard_map/all_to_all | solution.py:217
  159.9 1.4 copy-start.1
  182.5 1.4 copy-start.2
  183.8 4.9 %collective-permute-start.14 = (f32[8,128]{1,0:T(8,128)S(1)}, f32[8,128]{1,0:T(8,128)S(1)}, u32[]{:S(2)}, u32[]{:S(2)}) collective-permute-start(f32[8,128]{1,0:T(8,128)S(1)} %get-tuple-element.64), channel_id=1, source_target_pairs={{0,3},{1,2},{2,1},{3,0},{4,7},{5,6},{6,5},{7,4},{8,11},{9,10},{10,... | collective-permute-start | bytes 12296 | tf_op jit(solution)/shard_map/ppermute | solution.py:214
  186.2 6.4 %collective-permute-start.13 = (f32[8,128]{1,0:T(8,128)S(1)}, f32[8,128]{1,0:T(8,128)S(1)}, u32[]{:S(2)}, u32[]{:S(2)}) collective-permute-start(f32[8,128]{1,0:T(8,128)S(1)} %get-tuple-element.64), channel_id=1, source_target_pairs={{0,2},{1,3},{2,0},{3,1},{4,6},{5,7},{6,4},{7,5},{8,10},{9,11},{10,... | collective-permute-start | bytes 12296 | tf_op jit(solution)/shard_map/ppermute | solution.py:214
  186.5 6.1 %collective-permute-start.12 = (f32[8,128]{1,0:T(8,128)S(1)}, f32[8,128]{1,0:T(8,128)S(1)}, u32[]{:S(2)}, u32[]{:S(2)}) collective-permute-start(f32[8,128]{1,0:T(8,128)S(1)} %get-tuple-element.64), channel_id=1, source_target_pairs={{0,1},{1,0},{2,3},{3,2},{4,5},{5,4},{6,7},{7,6},{8,9},{9,8},{10,11... | collective-permute-start | bytes 12296 | tf_op jit(solution)/shard_map/ppermute | solution.py:214
  192.7 9.2 %collective-permute-start.17 = (f32[8,128]{1,0:T(8,128)S(1)}, f32[8,128]{1,0:T(8,128)S(1)}, u32[]{:S(2)}, u32[]{:S(2)}) collective-permute-start(f32[8,128]{1,0:T(8,128)S(1)} %add_add_fusion.1), channel_id=1, source_target_pairs={{0,12},{1,13},{2,14},{3,15},{4,8},{5,9},{6,10},{7,11},{8,4},{9,5},... | collective-permute-start | bytes 12296 | tf_op jit(solution)/shard_map/ppermute | solution.py:214
  193.3 8.6 %collective-permute-start.16 = (f32[8,128]{1,0:T(8,128)S(1)}, f32[8,128]{1,0:T(8,128)S(1)}, u32[]{:S(2)}, u32[]{:S(2)}) collective-permute-start(f32[8,128]{1,0:T(8,128)S(1)} %add_add_fusion.1), channel_id=1, source_target_pairs={{0,8},{1,9},{2,10},{3,11},{4,12},{5,13},{6,14},{7,15},{8,0},{9,1},... | collective-permute-start | bytes 12296 | tf_op jit(solution)/shard_map/ppermute | solution.py:214
  193.3 9.5 %collective-permute-start.15 = (f32[8,128]{1,0:T(8,128)S(1)}, f32[8,128]{1,0:T(8,128)S(1)}, u32[]{:S(2)}, u32[]{:S(2)}) collective-permute-start(f32[8,128]{1,0:T(8,128)S(1)} %add_add_fusion.1), channel_id=1, source_target_pairs={{0,4},{1,5},{2,6},{3,7},{4,0},{5,1},{6,2},{7,3},{8,12},{9,13},{10,... | collective-permute-start | bytes 12296 | tf_op jit(solution)/shard_map/ppermute | solution.py:214
  (1 other events, 0.8 us)
